TPU v7x, 128 devices: a whole 4x4x4 slice. The times are simulated.
128 devices in a mesh: blk: 4 (over x), tok: 32 (over y, z, core).
Axes of the slice: x: 4, y: 4, z: 4, core: 2. Of those that a mesh axis runs over, the one named last changes fastest.
Arguments:
- inputs: bfloat16 [16384, 2048], P(('blk', 'tok')), may hold values from -6 to 6
- mix_scale: bfloat16 [2048], P('tok'), may hold values from 0.5 to 1.5
- branch_mat: bfloat16 [2048, 2560], P('tok', 'blk'), may hold values from -0.125 to 0.125
- input_mat: bfloat16 [2048, 2560], P('tok', 'blk'), may hold values from -0.125 to 0.125
- conv_taps: bfloat16 [4, 2560], P(None, ('blk', 'tok')), may hold values from -3 to 3
- conv_shift: bfloat16 [2560], P(('blk', 'tok')), may hold values from -2 to 2
- rate_mat: bfloat16 [16, 160, 160], P('blk', 'tok'), may hold values from -0.5 to 0.5
- rate_shift: bfloat16 [2560], P(('blk', 'tok')), may hold values from -2 to 2
- entry_mat: bfloat16 [16, 160, 160], P('blk', 'tok'), may hold values from -0.5 to 0.5
- entry_shift: bfloat16 [2560], P(('blk', 'tok')), may hold values from -2 to 2
- decay_logit: bfloat16 [2560], P(('blk', 'tok')), may hold values from 5 to 14
- out_mat: bfloat16 [2560, 2048], P('blk', 'tok'), may hold values from -0.25 to 0.25
- feed_scale: bfloat16 [2048], P('tok'), may hold values from 0.5 to 1.5
- gate_mat: bfloat16 [2048, 6144], P('tok', 'blk'), may hold values from -0.125 to 0.125
- up_mat: bfloat16 [2048, 6144], P('tok', 'blk'), may hold values from -0.125 to 0.125
- down_mat: bfloat16 [6144, 2048], P('blk', 'tok'), may hold values from -0.15625 to 0.15625
- lengths: int32 [5], replicated, may hold values from 1024 to 8192, as said below
- cotangent: bfloat16 [16384, 2048], P(('blk', 'tok')), may hold values from -6 to 6
Outputs:
- layer_out: bfloat16 [16384, 2048], P(('blk', 'tok'))
- inputs_grad: bfloat16 [16384, 2048], P(('blk', 'tok'))
- mix_scale_grad: float32 [2048], P('tok')
- branch_mat_grad: float32 [2048, 2560], P('tok', 'blk')
- input_mat_grad: float32 [2048, 2560], P('tok', 'blk')
- conv_taps_grad: float32 [4, 2560], P(None, ('blk', 'tok'))
- conv_shift_grad: float32 [2560], P(('blk', 'tok'))
- rate_mat_grad: float32 [16, 160, 160], P('blk', 'tok')
- rate_shift_grad: float32 [2560], P(('blk', 'tok'))
- entry_mat_grad: float32 [16, 160, 160], P('blk', 'tok')
- entry_shift_grad: float32 [2560], P(('blk', 'tok'))
- decay_logit_grad: float32 [2560], P(('blk', 'tok'))
- out_mat_grad: float32 [2560, 2048], P('blk', 'tok')
- feed_scale_grad: float32 [2048], P('tok')
- gate_mat_grad: float32 [2048, 6144], P('tok', 'blk')
- up_mat_grad: float32 [2048, 6144], P('tok', 'blk')
- down_mat_grad: float32 [6144, 2048], P('blk', 'tok')
Inputs may be any that keep to these rules, and one draw needn't show every extreme that they name: `lengths`: token counts of the items laid end to end in this order; they sum to 16384, and one item has exactly 8192 tokens.
All inputs are finite; a program needn't handle non-finite values.
Results may differ from a plain program's by a relative error of at most 0.023.
Values may be sent and summed in bfloat16 or wider, within the bound.
No kernel may reach another device: no remote copies, remote signals or barrier semaphores. Data moves between devices by JAX's collectives and lax.ppermute only.
A program may use at most 192 MiB of HBM per device.

v0:
```python
import functools

import jax
import jax.numpy as jnp
from jax import lax
from jax.experimental import pallas as pl
from jax.experimental.pallas import tpu as pltpu
from jax.sharding import PartitionSpec as P

CONV = 4
MEMBERS = 4
TOKS = 32
OWN = 128
HALO = 16
SMALL = 24
FIRST = 104

eps_norm = 1e-06
decay_power = 8.0
f32 = jnp.float32
bf16 = jnp.bfloat16


def hop_blk(values, distance):
    return lax.ppermute(
        values, "blk", [(i, (i + distance) % MEMBERS) for i in range(MEMBERS)]
    )


def hop_tok(values, axis, distance):
    route = []
    for y in range(4):
        for z in range(4):
            for c in range(2):
                if axis == "y":
                    to = ((y + distance) % 4, z, c)
                elif axis == "z":
                    to = (y, (z + distance) % 4, c)
                else:
                    to = (y, z, (c + distance) % 2)
                route.append((y * 8 + z * 2 + c, to[0] * 8 + to[1] * 2 + to[2]))
    return lax.ppermute(values, "tok", route)


def hop(values, axis, distance):
    if axis == "blk":
        return hop_blk(values, distance)
    return hop_tok(values, axis, distance)


def hop_apart(values, distance, axis="blk"):
    route = []
    for b in range(MEMBERS):
        for t in range(TOKS):
            step = distance if t % 2 == 0 else -distance
            place = {"blk": b, "y": t // 8, "z": t // 2 % 4}
            place[axis] = (place[axis] + step) % 4
            to = place["blk"] * TOKS + place["y"] * 8 + place["z"] * 2 + t % 2
            route.append((b * TOKS + t, to))
    return lax.ppermute(values, ("blk", "tok"), route)


def either(core, first, second):
    return jnp.where(core == 0, first, second)


def ring_gather(values, core):
    behind = hop_apart(values, 1)
    ahead = hop_apart(values, -1)
    far = hop_apart(behind, 1)
    return [values, either(core, ahead, behind), far, either(core, behind, ahead)]


def ring_open(parts, core, axis="blk"):
    return hop_apart(parts[2].astype(bf16), 1, axis), ring_near(parts, core, axis)


def ring_near(parts, core, axis="blk"):
    return hop_apart(either(core, parts[3], parts[1]).astype(bf16), -1, axis)


def ring_pass(parts, far, core, axis="blk"):
    onward = either(core, parts[1], parts[3]).astype(f32) + far.astype(f32)
    return hop_apart(onward.astype(bf16), 1, axis)


def ring_close(parts, near, joined):
    return parts[0].astype(f32) + near.astype(f32) + joined.astype(f32)


def ring_scatter(parts, core, axis="blk"):
    far, near = ring_open(parts, core, axis)
    return ring_close(parts, near, ring_pass(parts, far, core, axis))


def direct_scatter(parts, axis):
    total = parts[0].astype(f32)
    for distance in range(1, 4):
        total = total + hop(parts[distance], axis, distance).astype(f32)
    return total


def narrow_sum(left, right):
    return (left.astype(f32) + right.astype(f32)).astype(bf16)


def after(value, *others):
    return lax.optimization_barrier((value,) + others)[0]


def hop_sum(values, axis):
    return values + hop(values, axis, 1) + hop(values, axis, -1) + hop(values, axis, 2)


def direct_gather(values, axis="blk"):
    return [values] + [hop(values, axis, -d) for d in range(1, 4)]


def turned(values, place, axis=0):
    return [
        lax.dynamic_index_in_dim(values, (place + j) % 4, axis, keepdims=False) for j in range(4)
    ]


def swap_sum(parts, core):
    mine = lax.dynamic_index_in_dim(parts, core, 1, keepdims=False)
    theirs = lax.dynamic_index_in_dim(parts, 1 - core, 1, keepdims=False)
    return narrow_sum(mine, hop(theirs, "core", 1))


def chip_sum(values, core):
    return swap_sum(values.reshape(16, 2, -1, values.shape[1]), core)


def chips_sum(values):
    cores = [[2 * i + c for i in range(16)] for c in range(2)]
    terms = lax.all_to_all(values, "tok", 0, 0, axis_index_groups=cores, tiled=True)
    return jnp.sum(terms.astype(f32), axis=0)


def together(*values):
    return lax.optimization_barrier(values)


def small_gather(values, before_last):
    values = jnp.stack([values, hop(values, "core", 1)])
    values = jnp.stack(direct_gather(values, "z"))
    return jnp.stack(direct_gather(after(values, *before_last), "y"))


def product(operand, weight, out=f32):
    return jnp.dot(operand, weight, preferred_element_type=f32).astype(out)


def product_back(operand, weight, out=f32):
    return lax.dot_general(
        operand, weight, (((1,), (1,)), ((), ())), preferred_element_type=f32
    ).astype(out)


def product_outer(operand, weight, out=bf16):
    return lax.dot_general(
        operand, weight, (((0,), (0,)), ((), ())), preferred_element_type=f32
    ).astype(out)


def norm_factor(values):
    return lax.rsqrt(jnp.mean(values * values, axis=1, keepdims=True) + eps_norm)


def normalize_back(gradient, values, factor, gains):
    weighted = gradient * gains
    return factor * weighted - values * (factor * factor * factor) * jnp.mean(
        weighted * values, axis=1, keepdims=True
    )


def sigmoid(values):
    return 1.0 / (1.0 + jnp.exp(-values))


def one_minus_exp(values):
    series = 1.0 + values * (1.0 / 6.0)
    for order in (5.0, 4.0, 3.0, 2.0):
        series = 1.0 + values * series * (1.0 / order)
    return jnp.where(values > -0.1, -values * series, 1.0 - jnp.exp(values))


def inverse_root(values):
    return lax.rsqrt(jnp.maximum(values, 1e-37))


def gelu_parts(values):
    root = 0.7978845608028654
    square = values * values
    bent = jnp.tanh(root * values * (1.0 + 0.044715 * square))
    half = 0.5 * (1.0 + bent)
    slope = half + 0.5 * values * (1.0 - bent * bent) * root * (1.0 + 3.0 * 0.044715 * square)
    return values * half, slope


def rows_at(start, size):
    return pl.ds(pl.multiple_of(start, size), size)


def conv_rows(ci_ref, slot, tile):
    base = slot * OWN + tile * HALO
    before = jnp.where(tile == 0, MEMBERS * OWN + slot * HALO, base - HALO)
    return jnp.concatenate(
        [ci_ref[rows_at(before, HALO), :].astype(f32), ci_ref[rows_at(base, HALO), :].astype(f32)],
        axis=0,
    )


def local_forward_kernel(
    ci_ref,
    place_ref,
    taps_ref,
    shift_ref,
    blocks_ref,
    bias_ref,
    soft_ref,
    conv_ref,
    rate_ref,
    entry_ref,
    local_ref,
    cum_ref,
    edge_ref,
    gates_ref,
    pre_ref,
    high_ref,
):
    channels = conv_ref.shape[1]
    block = blocks_ref.shape[0]
    width = 2 * channels
    columns = lax.broadcasted_iota(jnp.int32, (HALO, width), 1)
    columns = jnp.where(columns >= channels, columns - channels, columns)
    for group in range(channels // block):
        inside = (columns >= group * block) & (columns < (group + 1) * block)

        def spread_gates(step, carry):
            rows = blocks_ref[rows_at(step * HALO, HALO), :].astype(f32)
            gates_ref[rows_at(group * block + step * HALO, HALO), :] = jnp.where(
                inside, rows, 0.0
            ).astype(bf16)
            return carry

        lax.fori_loop(0, block // HALO, spread_gates, 0)

    for slot in range(MEMBERS):

        def convolve(tile, carry):
            base = slot * OWN + tile * HALO
            rows = conv_rows(ci_ref, slot, tile)
            places = place_ref[rows_at(base, HALO), :]
            total = shift_ref[...] + taps_ref[0:1, :] * rows[HALO:]
            for tap in range(1, CONV):
                lagged = pltpu.roll(rows, tap, 0)[HALO:]
                total = total + taps_ref[tap : tap + 1, :] * jnp.where(places >= tap, lagged, 0.0)
            conv_ref[rows_at(base, HALO), :] = total
            high_ref[rows_at(base, HALO), :] = total.astype(bf16)
            return carry

        lax.fori_loop(0, OWN // HALO, convolve, 0)

    def gate(step, carry):
        columns = pl.ds(pl.multiple_of(step * 256, 256), 256)
        weight = gates_ref[:, columns]
        pre_ref[:, columns] = (
            jnp.dot(high_ref[...], weight, preferred_element_type=f32) + bias_ref[:, columns]
        )
        return carry

    lax.fori_loop(0, 2 * channels // 256, gate, 0)

    row_ids = lax.broadcasted_iota(jnp.int32, (8, channels), 0)

    def scan(tile, carry):
        ends = []
        for slot in range(MEMBERS):
            base = slot * OWN + tile * 8
            rows = rows_at(base, 8)
            rates = sigmoid(pre_ref[rows, :channels])
            entries = 0.5 * jnp.tanh(0.5 * pre_ref[rows, channels:]) + 0.5
            log_keep = -soft_ref[...] * rates
            resets = place_ref[rows, :] == 0
            keeps = jnp.where(resets, 0.0, jnp.exp(log_keep))
            squared = one_minus_exp(2.0 * log_keep)
            scaling = jnp.where(resets, 1.0, squared * inverse_root(squared))
            value = entries * conv_ref[rows, :] * scaling
            coeff = keeps
            for distance in (1, 2, 4):
                reach = row_ids >= distance
                value = value + coeff * jnp.where(reach, pltpu.roll(value, distance, 0), 0.0)
                coeff = coeff * jnp.where(reach, pltpu.roll(coeff, distance, 0), 1.0)
            cum, state = carry[2 * slot], carry[2 * slot + 1]
            value = value + coeff * state
            coeff = coeff * cum
            rate_ref[rows, :] = rates
            entry_ref[rows, :] = entries
            local_ref[rows, :] = value
            cum_ref[rows, :] = coeff
            ends += [coeff[7:8], value[7:8]]
        return tuple(ends)

    start = (jnp.ones((1, channels), f32), jnp.zeros((1, channels), f32)) * MEMBERS
    ends = lax.fori_loop(0, OWN // 8, scan, start)
    edge_ref[...] = jnp.concatenate(ends[0::2] + ends[1::2], axis=0)


def extended(pair, block):
    return pair[0] * block[:4], block[:4] * pair[1] + block[4:]


def whole_chain(channels):
    return jnp.ones((4, channels), f32), jnp.zeros((4, channels), f32)


def fold_near_kernel(backward, spot_ref, *refs):
    pieces, (total_ref, prefix_ref, held_ref) = refs[:4], refs[4:]
    z, c = spot_ref[2], spot_ref[3]
    for distance, piece in enumerate(pieces):
        held_ref[distance] = piece[...]
    chain = whole_chain(total_ref.shape[1])
    prefix = chain
    for place in reversed(range(8)) if backward else range(8):
        here = place == 2 * z + c
        prefix = tuple(jnp.where(here, new, old) for new, old in zip(chain, prefix))
        distance = jnp.bitwise_and(place // 2 - z + 4, 3)
        chain = extended(chain, held_ref[distance, jnp.bitwise_xor(place % 2, c)])
    total_ref[...] = jnp.concatenate(chain, axis=0)
    prefix_ref[...] = jnp.concatenate(prefix, axis=0)


def slot_carries(backward, spot_ref, pieces, prefix_ref, held_ref):
    y = spot_ref[1]
    channels = prefix_ref.shape[1]
    for distance, piece in enumerate(pieces):
        held_ref[distance] = piece[...]
    total = whole_chain(channels)
    prefix = total
    for place in reversed(range(4)) if backward else range(4):
        here = place == y
        prefix = tuple(jnp.where(here, new, old) for new, old in zip(total, prefix))
        total = extended(total, held_ref[jnp.bitwise_and(place - y + 4, 3)])
    prefix = extended(prefix, prefix_ref[...])
    current = jnp.zeros((1, channels), f32)
    carries = [None] * MEMBERS
    for _ in range(2):
        for slot in reversed(range(MEMBERS)) if backward else range(MEMBERS):
            one = slice(slot, slot + 1)
            carries[slot] = prefix[0][one] * current + prefix[1][one]
            current = total[0][one] * current + total[1][one]
    return carries


def mix_kernel(
    spot_ref,
    piece0,
    piece1,
    piece2,
    piece3,
    prefix_ref,
    local_ref,
    cum_ref,
    branch_ref,
    state_ref,
    mixed_ref,
    carry_ref,
    held_ref,
):
    pieces = (piece0, piece1, piece2, piece3)
    carries = slot_carries(False, spot_ref, pieces, prefix_ref, held_ref)
    carry_ref[...] = jnp.concatenate(carries, axis=0)

    def apply(tile, token):
        for slot in range(MEMBERS):
            rows = rows_at(slot * OWN + tile * HALO, HALO)
            states = local_ref[rows, :] + cum_ref[rows, :] * carry_ref[slot : slot + 1, :]
            state_ref[rows, :] = states
            mixed_ref[rows, :] = (states * gelu_parts(branch_ref[rows, :])[0]).astype(bf16)
        return token

    lax.fori_loop(0, OWN // HALO, apply, 0)


def local_backward_kernel(
    grad_ref,
    branch_ref,
    state_ref,
    rate_ref,
    place_ref,
    soft_ref,
    bgrad_ref,
    sgrad_ref,
    local_ref,
    cum_ref,
    edge_ref,
):
    channels = grad_ref.shape[1]
    row_ids = lax.broadcasted_iota(jnp.int32, (8, channels), 0)

    def scan(step, carry):
        ends = []
        for slot in range(MEMBERS):
            pieces = {}
            base = slot * OWN + OWN - HALO - step * HALO
            cum, after = carry[2 * slot], carry[2 * slot + 1]
            slopes = []
            for part in (1, 0):
                rows = rows_at(base + 8 * part, 8)
                gated, slope = gelu_parts(branch_ref[rows, :])
                gradient = grad_ref[rows, :]
                slopes.append(slope * gradient * state_ref[rows, :])
                sgrad = gradient * gated
                keeps = jnp.where(
                    place_ref[rows, :] == 0, 0.0, jnp.exp(-soft_ref[...] * rate_ref[rows, :])
                )
                coeff = keeps
                value = keeps * sgrad
                for distance in (1, 2, 4):
                    reach = row_ids < 8 - distance
                    value = value + coeff * jnp.where(
                        reach, pltpu.roll(value, 8 - distance, 0), 0.0
                    )
                    coeff = coeff * jnp.where(reach, pltpu.roll(coeff, 8 - distance, 0), 1.0)
                value = value + coeff * after
                coeff = coeff * cum
                sgrad_ref[rows, :] = sgrad
                local_ref[rows, :] = value
                cum_ref[rows, :] = coeff
                cum, after = coeff[0:1], value[0:1]
            bgrad_ref[rows_at(base, HALO), :] = jnp.concatenate(
                [slopes[1], slopes[0]], axis=0
            ).astype(bf16)
            ends += [cum, after]
        return tuple(ends)

    start = (jnp.ones((1, channels), f32), jnp.zeros((1, channels), f32)) * MEMBERS
    ends = lax.fori_loop(0, OWN // HALO, scan, start)
    edge_ref[...] = jnp.concatenate(ends[0::2] + ends[1::2], axis=0)


def finish_backward_kernel(
    spot_ref,
    piece0,
    piece1,
    piece2,
    piece3,
    prefix_ref,
    sgrad_ref,
    local_ref,
    cum_ref,
    state_ref,
    carry_ref,
    conv_ref,
    rate_ref,
    entry_ref,
    place_ref,
    soft_ref,
    ci_ref,
    taps_ref,
    gates_ref,
    pregrad_ref,
    igrad_ref,
    owed_ref,
    sums_ref,
    cgrad_ref,
    back_ref,
    held_ref,
):
    channels = conv_ref.shape[1]
    pieces = (piece0, piece1, piece2, piece3)
    carries = slot_carries(True, spot_ref, pieces, prefix_ref, held_ref)
    back_ref[...] = jnp.concatenate(carries, axis=0)

    row_ids = lax.broadcasted_iota(jnp.int32, (8, channels), 0)
    zero = jnp.zeros((8, channels), f32)
    logit_sum, rate_sum, entry_sum = zero, zero, zero
    for slot in range(MEMBERS):

        def gate_grads(step, carry):
            later, logit_sum, rate_sum, entry_sum = carry
            base = slot * OWN + OWN - HALO - step * HALO
            low_rate, low_entry = [], []
            for part in (1, 0):
                first = base + 8 * part
                rows = rows_at(first, 8)
                held = local_ref[rows, :] + cum_ref[rows, :] * back_ref[slot : slot + 1, :]
                following = jnp.where(row_ids == 7, later, pltpu.roll(held, 7, 0))
                adjoint = sgrad_ref[rows, :] + following
                later = held[0:1]
                ahead = state_ref[rows_at(jnp.maximum(first - 8, 0), 8), :][7:8]
                at_start = first == slot * OWN
                ahead = jnp.where(at_start, carry_ref[slot : slot + 1, :], ahead)
                previous = jnp.where(row_ids == 0, ahead, pltpu.roll(state_ref[rows, :], 1, 0))
                rates, entries, conv = rate_ref[rows, :], entry_ref[rows, :], conv_ref[rows, :]
                resets = place_ref[rows, :] == 0
                log_keep = -soft_ref[...] * rates
                squared = one_minus_exp(2.0 * log_keep)
                inverse = inverse_root(squared)
                scaling = jnp.where(resets, 1.0, squared * inverse)
                turn = jnp.where(resets, 0.0, (1.0 - squared) * inverse)
                weighed = adjoint * entries
                log_grad = held * previous - weighed * conv * turn
                rate_part = log_grad * rates
                logit_sum = logit_sum + rate_part
                rate_grad = -soft_ref[...] * rate_part * (1.0 - rates)
                direct = weighed * scaling
                entry_grad = direct * conv * (1.0 - entries)
                rate_sum = rate_sum + rate_grad
                entry_sum = entry_sum + entry_grad
                cgrad_ref[rows, :] = direct
                low_rate.append(rate_grad)
                low_entry.append(entry_grad)
            rows = rows_at(base, HALO)
            pregrad_ref[rows, :channels] = jnp.concatenate(low_rate[::-1], axis=0).astype(bf16)
            pregrad_ref[rows, channels:] = jnp.concatenate(low_entry[::-1], axis=0).astype(bf16)
            return later, logit_sum, rate_sum, entry_sum

        _, logit_sum, rate_sum, entry_sum = lax.fori_loop(
            0,
            OWN // HALO,
            gate_grads,
            (back_ref[slot : slot + 1, :], logit_sum, rate_sum, entry_sum),
        )

    def gate_back(step, carry):
        columns = pl.ds(pl.multiple_of(step * 128, 128), 128)
        cgrad_ref[:, columns] += lax.dot_general(
            pregrad_ref[...],
            gates_ref[columns, :],
            (((1,), (1,)), ((), ())),
            preferred_element_type=f32,
        )
        return carry

    lax.fori_loop(0, channels // 128, gate_back, 0)

    shift_sum = jnp.zeros((HALO, channels), f32)
    tap_sums = [shift_sum] * CONV
    for slot in range(MEMBERS):

        def spread(rows, places):
            return [rows] + [jnp.where(places >= tap, rows, 0.0) for tap in range(1, CONV)]

        def shifted_sum(current, following):
            total = taps_ref[0:1, :] * current[0]
            for tap in range(1, CONV):
                both = jnp.concatenate([current[tap], following[tap]], axis=0)
                total = total + taps_ref[tap : tap + 1, :] * pltpu.roll(both, 2 * HALO - tap, 0)[:HALO]
            return total

        def conv_back(tile, carry):
            shift_sum, tap_sums = carry
            base = slot * OWN + tile * HALO
            rows = rows_at(base, HALO)
            after = jnp.minimum(base + HALO, slot * OWN + OWN - HALO)
            next_rows = rows_at(after, HALO)
            last = jnp.where(tile == OWN // HALO - 1, 0.0, 1.0)
            grads = spread(cgrad_ref[rows, :], place_ref[rows, :])
            coming = spread(cgrad_ref[next_rows, :] * last, place_ref[next_rows, :])
            igrad_ref[rows, :] = shifted_sum(grads, coming)
            inputs = conv_rows(ci_ref, slot, tile)
            shift_sum = shift_sum + grads[0]
            sums = [tap_sums[0] + grads[0] * inputs[HALO:]]
            for tap in range(1, CONV):
                sums.append(tap_sums[tap] + grads[tap] * pltpu.roll(inputs, tap, 0)[HALO:])
            return shift_sum, sums

        shift_sum, tap_sums = lax.fori_loop(0, OWN // HALO, conv_back, (shift_sum, tap_sums))
        rows = rows_at(slot * OWN, HALO)
        first = spread(cgrad_ref[rows, :], place_ref[rows, :])
        owed_ref[slot * HALO : (slot + 1) * HALO, :] = shifted_sum(
            [jnp.zeros((HALO, channels), f32)] * CONV, first
        )

    def total_rows(values):
        return jnp.sum(values, axis=0, keepdims=True)

    sums_ref[...] = jnp.concatenate(
        [total_rows(v) for v in [shift_sum, rate_sum, entry_sum, logit_sum] + list(tap_sums)],
        axis=0,
    )


def in_vmem(kernel, outs, scratch=(), scalars=0, count=1, moved=0):
    vmem = pl.BlockSpec(memory_space=pltpu.VMEM)
    smem = pl.BlockSpec(memory_space=pltpu.SMEM)
    return pl.pallas_call(
        kernel,
        out_shape=[jax.ShapeDtypeStruct(shape, dtype) for shape, dtype in outs],
        in_specs=[smem] * scalars + [vmem] * count,
        out_specs=[vmem] * len(outs),
        scratch_shapes=[pltpu.VMEM(shape, dtype) for shape, dtype in scratch],
        compiler_params=pltpu.CompilerParams(vmem_limit_bytes=40 * 1024 * 1024),
        cost_estimate=pl.CostEstimate(flops=0, bytes_accessed=moved, transcendentals=0),
    )


def exchange_edges(edges, spots, backward):
    channels = edges.shape[1]
    near = jnp.stack([edges, hop(edges, "core", 1)])
    total, prefix = in_vmem(
        functools.partial(fold_near_kernel, backward),
        [((8, channels), f32)] * 2,
        [((4, 2, 8, channels), f32)],
        scalars=1,
        count=4,
        moved=3_000_000,
    )(spots, *direct_gather(near, "z"))
    return direct_gather(total, "y") + [prefix], near


def outer_kernel(lhs_one, lhs_two, rhs_one, rhs_two, rhs_three, out_ref):
    def settle(lhs, rhs):
        out_ref[...] = lax.dot_general(
            lhs[...], rhs[...], (((0,), (0,)), ((), ())), preferred_element_type=f32
        ).astype(bf16)

    for step, (lhs, rhs) in enumerate(
        ((lhs_one, rhs_one), (lhs_one, rhs_two), (lhs_two, rhs_three))
    ):
        pl.when(pl.program_id(0) == step)(functools.partial(settle, lhs, rhs))


def feed_outer(lhs_one, lhs_two, rhs):
    rows, features = lhs_one.shape
    columns = rhs[0].shape[1]
    height = 1024
    whole = pl.BlockSpec((rows, columns), lambda j, i: (0, 0))
    return pl.pallas_call(
        outer_kernel,
        grid=(3, features // height),
        in_specs=[
            pl.BlockSpec((rows, height), lambda j, i: (0, jnp.where(j < 2, i, 0))),
            pl.BlockSpec((rows, height), lambda j, i: (0, jnp.where(j < 2, 0, i))),
            whole,
            whole,
            whole,
        ],
        out_specs=pl.BlockSpec((height, columns), lambda j, i: (i, j)),
        out_shape=jax.ShapeDtypeStruct((features, 3 * columns), bf16),
        compiler_params=pltpu.CompilerParams(vmem_limit_bytes=40 * 1024 * 1024),
        cost_estimate=pl.CostEstimate(
            flops=6 * rows * features * columns,
            bytes_accessed=6 * features * columns,
            transcendentals=0,
        ),
    )(lhs_one, lhs_two, *rhs)


def small_kernel(cut, conv_ref, pregrad_ref, sums_ref, extra_ref, out_ref):
    channels = conv_ref.shape[1]
    width = 2 * channels
    block = cut * TOKS
    dense = lax.dot_general(
        conv_ref[...].astype(bf16),
        pregrad_ref[...],
        (((0,), (0,)), ((), ())),
        preferred_element_type=f32,
    )
    columns = lax.broadcasted_iota(jnp.int32, (block, width), 1)
    columns = jnp.where(columns >= channels, columns - channels, columns)
    gates = jnp.zeros((block, width), f32)
    for group in range(channels // block):
        inside = (columns >= group * block) & (columns < (group + 1) * block)
        gates = jnp.where(inside, dense[group * block : (group + 1) * block], gates)
    spare = jnp.zeros((SMALL - 2 * cut - 9, channels), f32)
    for tok in range(TOKS):
        rows = gates[tok * cut : (tok + 1) * cut]
        pieces = [rows[:, :channels], rows[:, channels:], sums_ref[...]]
        pieces += [extra_ref[tok : tok + 1, :], spare]
        out_ref[tok] = jnp.concatenate(pieces, axis=0).astype(bf16)


def halves_kernel(count, spot_ref, small_ref, *refs):
    core = spot_ref[3]
    mine_ref, theirs_ref = refs[2 * count :]
    chips, rows, _ = mine_ref.shape
    rows = (rows - SMALL) // count
    for which in range(count):
        sums = lax.dot_general(
            refs[which][...],
            refs[count + which][...],
            (((0,), (0,)), ((), ())),
            preferred_element_type=f32,
        )
        for chip in range(chips):
            low = sums[2 * chip * rows : (2 * chip + 1) * rows]
            high = sums[(2 * chip + 1) * rows : (2 * chip + 2) * rows]
            at = slice(which * rows, (which + 1) * rows)
            mine_ref[chip, at, :] = jnp.where(core == 0, low, high).astype(bf16)
            theirs_ref[chip, at, :] = jnp.where(core == 0, high, low).astype(bf16)
    for chip in range(chips):
        low, high = small_ref[2 * chip].astype(f32), small_ref[2 * chip + 1].astype(f32)
        at = slice(count * rows, count * rows + SMALL)
        mine_ref[chip, at, :] = jnp.where(core == 0, low, high).astype(bf16)
        theirs_ref[chip, at, :] = jnp.where(core == 0, high, low).astype(bf16)


def outer_halves(spots, small, lhs, rhs):
    count = len(lhs)
    features = lhs[0].shape[1]
    rows, columns = rhs[0].shape
    height = 1024
    chips = height // 128
    total = 64 * count + SMALL
    shape = jax.ShapeDtypeStruct((features // 128, total, columns), bf16)
    out_spec = pl.BlockSpec((chips, total, columns), lambda i: (i, 0, 0))
    return pl.pallas_call(
        functools.partial(halves_kernel, count),
        grid=(features // height,),
        in_specs=[pl.BlockSpec(memory_space=pltpu.SMEM)]
        + [pl.BlockSpec((2 * chips, SMALL, columns), lambda i: (i, 0, 0))]
        + [pl.BlockSpec((rows, height), lambda i: (0, i))] * count
        + [pl.BlockSpec((rows, columns), lambda i: (0, 0))] * count,
        out_specs=[out_spec] * 2,
        out_shape=[shape] * 2,
        compiler_params=pltpu.CompilerParams(vmem_limit_bytes=40 * 1024 * 1024),
        cost_estimate=pl.CostEstimate(
            flops=2 * count * rows * features * columns,
            bytes_accessed=20_000_000,
            transcendentals=0,
        ),
    )(spots, small, *lhs, *rhs)


def per_device(
    inputs,
    mix_scale,
    branch_mat,
    input_mat,
    conv_taps,
    conv_shift,
    rate_mat,
    rate_shift,
    entry_mat,
    entry_shift,
    decay_logit,
    out_mat,
    feed_scale,
    gate_mat,
    up_mat,
    down_mat,
    lengths,
    cotangent,
):
    blk = lax.axis_index("blk")
    tok = lax.axis_index("tok")
    spot = (tok // 8, (tok // 2) % 4, tok % 2)
    spots = jnp.stack([tok] + list(spot)).astype(jnp.int32)
    channels = branch_mat.shape[1]
    hidden_units = gate_mat.shape[1]
    slice_rows = branch_mat.shape[0]
    total_rows = MEMBERS * OWN

    groups, cut, block = rate_mat.shape
    own_channels = conv_shift.shape[0]
    vectors = [conv_taps, conv_shift[None], rate_shift[None], entry_shift[None], decay_logit[None]]
    vectors = jnp.concatenate(vectors, axis=0).reshape(-1)
    extras = jnp.concatenate([vectors, mix_scale, feed_scale])
    extras = jnp.pad(extras, (0, channels - extras.shape[0]))[None]
    smalls = [jnp.moveaxis(mats, 0, 1).reshape(cut, channels) for mats in (rate_mat, entry_mat)]
    smalls = jnp.concatenate(smalls + [extras], axis=0)
    smalls = jnp.pad(smalls, ((0, HALO - smalls.shape[0]), (0, 0)))
    input_blocks = ring_gather(inputs, spot[2])
    near = after(small_gather(smalls, (input_blocks[1], input_blocks[3])), input_blocks[2])
    for axis, place in ((2, spot[2]), (1, spot[1]), (0, spot[0])):
        near = jnp.roll(near, place, axis)
    near = near.reshape(TOKS, HALO, channels)
    mixer_all = lax.all_gather(
        jnp.concatenate([input_mat, branch_mat, out_mat.T], axis=1), "tok", axis=0, tiled=True
    )
    devices = MEMBERS * TOKS
    tail = lax.ppermute(
        inputs[OWN - HALO :], ("blk", "tok"), [(i, (i + 1) % devices) for i in range(devices)]
    )
    cotangent_blocks = ring_gather(after(cotangent, input_blocks[2]), spot[2])
    rows_all = jnp.concatenate(input_blocks + direct_gather(tail), axis=0)
    cotangent_all = jnp.concatenate(cotangent_blocks, axis=0)

    extras = near[:, 2 * cut]
    vectors = extras[:, : 8 * own_channels].reshape(TOKS, 8, own_channels).astype(f32)
    vectors = jnp.moveaxis(vectors, 0, 1).reshape(8, channels)
    gains = extras[:, 8 * own_channels : 8 * own_channels + 2 * slice_rows].astype(f32)
    mix_gain = gains[:, :slice_rows].reshape(1, -1)
    feed_gain = gains[:, slice_rows:].reshape(1, -1)
    wide_values = rows_all.astype(f32)
    wide_one = (wide_values * norm_factor(wide_values) * mix_gain).astype(bf16)
    taps, shift = vectors[:CONV], vectors[4:5]
    bias = jnp.concatenate([vectors[5:6], vectors[6:7]], axis=1)
    soft = decay_power * jax.nn.softplus(-vectors[7:8])
    blocks = [near[:, i * cut : (i + 1) * cut].reshape(block, channels) for i in range(2)]
    blocks = after(jnp.concatenate(blocks, axis=1), cotangent_blocks[2])
    feed_own = jnp.concatenate([gate_mat, up_mat, down_mat.T], axis=1)
    feed_all = lax.all_gather(after(feed_own, wide_one, blocks), "tok", axis=0, tiled=True)
    gate_up_all = feed_all[:, : 2 * hidden_units]
    down_turned = feed_all[:, 2 * hidden_units :]
    own_one = wide_one[:total_rows]
    input_all = mixer_all[:, :channels]
    branch_all = mixer_all[:, channels : 2 * channels]
    project_all = mixer_all[:, : 2 * channels]
    out_turned = mixer_all[:, 2 * channels : 3 * channels]

    slots = (blk + jnp.arange(MEMBERS, dtype=jnp.int32)) % MEMBERS
    token_ids = (
        (slots * TOKS + tok)[:, None] * OWN + jnp.arange(OWN, dtype=jnp.int32)[None, :]
    ).reshape(-1)
    starts = jnp.cumsum(lengths) - lengths
    opened = jnp.max(jnp.where(starts[None, :] <= token_ids[:, None], starts[None, :], 0), axis=1)
    places = (token_ids - opened).reshape(total_rows, 1).astype(jnp.int32)

    conv_input = product(wide_one, input_all, bf16)
    branch = product(own_one, branch_all)
    state_shape = ((total_rows, channels), f32)
    conv, rates, entries, local, cum, edges, gates = in_vmem(
        local_forward_kernel,
        [state_shape] * 5 + [((8, channels), f32), ((channels, 2 * channels), bf16)],
        [
            ((total_rows, 2 * channels), f32),
            ((total_rows, channels), bf16),
        ],
        count=7,
        moved=30_000_000,
    )(conv_input, places, taps, shift, blocks, bias, soft)
    chains, _ = exchange_edges(edges, spots, False)
    states, mixture, carried = in_vmem(
        mix_kernel,
        [state_shape, ((total_rows, channels), bf16), ((MEMBERS, channels), f32)],
        [((4, 8, channels), f32)],
        scalars=1,
        count=8,
        moved=4_500_000,
    )(spots, *chains, local, cum, branch)

    def rows_of(values):
        return [values[j * OWN : (j + 1) * OWN] for j in range(MEMBERS)]

    own_values = inputs.astype(f32)
    middle = own_values + ring_scatter(rows_of(product_back(mixture, out_turned)), spot[2])

    factor_two = norm_factor(middle)
    normed_two = (middle * factor_two * feed_gain).astype(bf16)
    hidden_grad = product(after(cotangent_all, mixture), down_turned)
    blocks_two = ring_gather(normed_two, spot[2])
    blocks_two[2] = after(blocks_two[2], hidden_grad)
    wide_two = jnp.concatenate(blocks_two, axis=0)
    gate_up = product(wide_two, gate_up_all)
    gate_pre, up_pre = gate_up[:, :hidden_units], gate_up[:, hidden_units:]
    gate_act, gate_slope = gelu_parts(gate_pre)
    hidden = (gate_act * up_pre).astype(bf16)
    gate_grad = (gate_slope * hidden_grad * up_pre).astype(bf16)
    up_grad = (gate_act * hidden_grad).astype(bf16)
    both_grads = jnp.concatenate([gate_grad, up_grad], axis=1)
    two_shares = product_back(both_grads, gate_up_all)
    two_parts = rows_of(two_shares)
    two_far, two_near = ring_open(two_parts, spot[2])
    two_grad = ring_close(two_parts, two_near, ring_pass(two_parts, two_far, spot[2]))
    middle_grad = cotangent.astype(f32) + normalize_back(two_grad, middle, factor_two, feed_gain)
    grad_feed_scale = jnp.sum(two_grad * middle * factor_two, axis=0)
    feed_shares = feed_outer(
        wide_two, cotangent_all, after((gate_grad, up_grad, hidden), two_shares)
    )
    feed_grads = lax.psum_scatter(
        after(feed_shares, two_grad), "tok", scatter_dimension=0, tiled=True
    )

    layer_shares = product_back(after(hidden, two_far), down_turned, bf16)
    middle_blocks = ring_gather(middle_grad.astype(bf16), spot[2])
    middle_blocks[2] = after(middle_blocks[2], layer_shares)
    middle_wide = jnp.concatenate(middle_blocks, axis=0)
    mixture_grad = product(middle_wide, out_turned)
    branch_grad, sgrad, local_back, cum_back, back_edges = in_vmem(
        local_backward_kernel,
        [((total_rows, channels), bf16)] + [state_shape] * 3 + [((8, channels), f32)],
        count=6,
        moved=9_500_000,
    )(mixture_grad, branch, states, rates, places, soft)
    chains_back, near_back = exchange_edges(back_edges, spots, True)
    pregrads, igrad, owed, sums = in_vmem(
        finish_backward_kernel,
        [
            ((total_rows, 2 * channels), bf16),
            state_shape,
            ((MEMBERS * HALO, channels), f32),
            ((8, channels), f32),
        ],
        [
            ((total_rows, channels), f32),
            ((MEMBERS, channels), f32),
            ((4, 8, channels), f32),
        ],
        scalars=1,
        count=18,
        moved=40_000_000,
    )(
        spots,
        *chains_back,
        sgrad,
        local_back,
        cum_back,
        states,
        carried,
        conv,
        rates,
        entries,
        places,
        soft,
        conv_input,
        taps,
        gates,
    )
    returned = lax.ppermute(
        owed.reshape(MEMBERS, HALO, channels)[:, HALO - 3 :],
        "tok",
        [(i, (i - 1) % TOKS) for i in range(TOKS)],
    )
    turned_on = jnp.concatenate([returned[1:], returned[:1]], axis=0)
    landing = jnp.where(tok == TOKS - 1, turned_on, returned)
    input_grad = igrad.reshape(MEMBERS, OWN, channels) + jnp.pad(
        landing, ((0, 0), (OWN - 3, 0), (0, 0))
    )
    input_low = input_grad.reshape(total_rows, channels).astype(bf16)
    feed_rows = jnp.pad(
        grad_feed_scale.reshape(TOKS, slice_rows), ((0, 0), (0, channels - slice_rows))
    )
    (small_rows,) = in_vmem(
        functools.partial(small_kernel, cut),
        [((TOKS, SMALL, channels), bf16)],
        count=4,
        moved=11_000_000,
    )(conv, pregrads, sums, feed_rows)

    core = spot[2]
    weight_mine, weight_theirs = outer_halves(
        spots, small_rows, (middle_wide, wide_one, wide_one), (mixture, branch_grad, input_low)
    )
    weight_other = hop(weight_theirs, "core", 1)
    late = after(input_low, weight_theirs)
    one_shares = product_back(jnp.concatenate([late, branch_grad], axis=1), project_all, bf16)
    one_parts = rows_of(one_shares)
    one_grad = ring_scatter(one_parts, core)
    factor_one = norm_factor(own_values)
    first_grad = normalize_back(one_grad, own_values, factor_one, mix_gain)
    inputs_grad = (middle_grad + first_grad).astype(bf16)
    settled = chips_sum(narrow_sum(weight_mine, weight_other))
    layer_out = middle + ring_scatter(rows_of(after(layer_shares, one_grad)), core)
    grad_out, grad_branch, grad_input = [
        settled[i * slice_rows : (i + 1) * slice_rows] for i in range(3)
    ]
    settled = settled[3 * slice_rows :]
    grad_mix_scale = jnp.sum(
        grad_branch * branch_mat.astype(f32) + grad_input * input_mat.astype(f32), axis=1
    ) / mix_scale.astype(f32)
    gains_own = jnp.concatenate([grad_mix_scale, settled[2 * cut + 8, :slice_rows]])
    gains_own = hop_sum(gains_own.reshape(1, -1), "blk")[0]
    gate_own = [
        jnp.moveaxis(settled[i * cut : (i + 1) * cut].reshape(cut, groups, block), 1, 0)
        for i in range(2)
    ]
    sums_own = lax.dynamic_slice(
        settled[2 * cut : 2 * cut + 8], (0, tok * own_channels), (8, own_channels)
    )
    own_logits = decay_logit.astype(f32)
    return (
        layer_out.astype(bf16),
        inputs_grad,
        gains_own[:slice_rows],
        grad_branch,
        grad_input,
        sums_own[4:],
        sums_own[0],
        gate_own[0],
        sums_own[1],
        gate_own[1],
        sums_own[2],
        sums_own[3] * decay_power * jax.nn.sigmoid(-own_logits),
        grad_out.T,
        gains_own[slice_rows : 2 * slice_rows],
        feed_grads[:, :hidden_units].astype(f32),
        feed_grads[:, hidden_units : 2 * hidden_units].astype(f32),
        feed_grads[:, 2 * hidden_units :].T.astype(f32),
    )


def solution(mesh):
    in_specs = (
        P(("blk", "tok"), None),
        P("tok"),
        P("tok", "blk"),
        P("tok", "blk"),
        P(None, ("blk", "tok")),
        P(("blk", "tok")),
        P("blk", "tok", None),
        P(("blk", "tok")),
        P("blk", "tok", None),
        P(("blk", "tok")),
        P(("blk", "tok")),
        P("blk", "tok"),
        P("tok"),
        P("tok", "blk"),
        P("tok", "blk"),
        P("blk", "tok"),
        P(),
        P(("blk", "tok"), None),
    )
    out_specs = (
        P(("blk", "tok"), None),
        P(("blk", "tok"), None),
        P("tok"),
        P("tok", "blk"),
        P("tok", "blk"),
        P(None, ("blk", "tok")),
        P(("blk", "tok")),
        P("blk", "tok", None),
        P(("blk", "tok")),
        P("blk", "tok", None),
        P(("blk", "tok")),
        P(("blk", "tok")),
        P("blk", "tok"),
        P("tok"),
        P("tok", "blk"),
        P("tok", "blk"),
        P("blk", "tok"),
    )
    return jax.shard_map(
        per_device, mesh=mesh, in_specs=in_specs, out_specs=out_specs, check_vma=False
    )
```

profile of v0, /device:TPU:68, one launch (start us, length us, event | category | flops | bytes accessed | tf_op | source)
XLA Modules:
  0.0 409.6 jit_solution(12925769290027878124)
XLA Ops:
  7.2 1.7 pad_maximum_fusion.6
  14.4 2.0 pad_maximum_fusion.4
  26.9 3.6 collective-permute-start.5
  30.6 2.8 collective-permute-done.2
  35.2 3.0 collective-permute-start.12
  41.9 4.1 %collective-permute-done.12 = bf16[4,2,16,640]{3,2,1,0:T(8,128)(2,1)S(1)} collective-permute-done((bf16[4,2,16,640]{3,2,1,0:T(8,128)(2,1)S(1)}, bf16[4,2,16,640]{3,2,1,0:T(8,128)(2,1)S(1)}, u32[]{:S(2)}, u32[]{:S(2)}) %collective-permute-start.12) | collective-permute-done | bytes 163872 | tf_op jit(solution)/shard_map/ppermute | solution.py:42
  49.2 2.0 collective-permute-start.15
  51.2 2.4 fusion.12.refs_1_.refs_2_
  53.7 5.0 %collective-permute-done.15 = bf16[128,2048]{1,0:T(8,128)(2,1)} collective-permute-done((bf16[128,2048]{1,0:T(8,128)(2,1)}, bf16[128,2048]{1,0:T(8,128)(2,1)}, u32[]{:S(2)}, u32[]{:S(2)}) %collective-permute-start.15) | collective-permute-done | bytes 524320 | tf_op jit(solution)/shard_map/ppermute | solution.py:60
  61.4 2.8 all-gather.3.cloned.1.call-done
  64.2 3.9 fusion.32.ci_ref
  68.1 8.5 %shard_map.305 = (f32[512,640]{1,0:T(8,128)S(1)}, f32[512,640]{1,0:T(8,128)S(1)}, f32[512,640]{1,0:T(8,128)S(1)}, f32[512,640]{1,0:T(8,128)S(1)}, f32[512,640]{1...) custom-call(bf16[576,640]{1,0:T(8,128)(2,1)S(1)} %fusion.32.ci_ref, s32[512,1]{1,0:T(8,128)S(1)} %sub.47.place_ref, ...), custom_call_target="tpu_custom_call" | custom-call | bytes 30000000 | tf_op jit(solution)/shard_map/pallas_call | solution.py:817
  81.1 3.9 collective-permute-start.18
  85.0 2.6 collective-permute-start.19
  87.9 2.1 collective-permute-done.19.refs_3_
  93.8 3.4 fusion.23.branch_ref
  99.1 1.8 fusion.29
  102.1 2.4 collective-permute-start.24
  104.5 11.5 %collective-permute-done.24 = bf16[128,2048]{1,0:T(8,128)(2,1)S(1)} collective-permute-done((bf16[128,2048]{1,0:T(8,128)(2,1)S(1)}, bf16[128,2048]{1,0:T(8,128)(2,1)S(1)}, u32[]{:S(2)}, u32[]{:S(2)}) %collective-permute-start.24) | collective-permute-done | bytes 524320 | tf_op jit(solution)/shard_map/ppermute | solution.py:60
  119.1 8.3 %collective-permute-done.25 = bf16[128,2048]{1,0:T(8,128)(2,1)} collective-permute-done((bf16[128,2048]{1,0:T(8,128)(2,1)}, bf16[128,2048]{1,0:T(8,128)(2,1)}, u32[]{:S(2)}, u32[]{:S(2)}) %collective-permute-start.25) | collective-permute-done | bytes 524320 | tf_op jit(solution)/shard_map/ppermute | solution.py:60
  127.3 3.1 multiply_reduce_fusion.2
  131.9 1.8 collective-permute-start.26
  135.3 2.8 pad_maximum_fusion.lhs_two
  138.1 5.9 %collective-permute-done.27 = bf16[128,2048]{1,0:T(8,128)(2,1)} collective-permute-done((bf16[128,2048]{1,0:T(8,128)(2,1)S(1)}, bf16[128,2048]{1,0:T(8,128)(2,1)}, u32[]{:S(2)}, u32[]{:S(2)}) %collective-permute-start.27) | collective-permute-done | bytes 524320 | tf_op jit(solution)/shard_map/ppermute | solution.py:60
  144.4 2.1 broadcast_select_fusion.7
  146.5 6.3 %fusion.6 = f32[512,1536]{1,0:T(8,128)S(1)} fusion(bf16[512,2048]{1,0:T(8,128)(2,1)} %pad_maximum_fusion.lhs_two, bf16[2048,4608]{1,0:T(8,128)(2,1)} %all-gather.5.cloned.1.call-done), kind=kOutput, calls=%fused_computation.10 | convolution fusion | flops 3221225472 | bytes 11534336 | tf_op jit(solution)/shard_map/dot_general | solution.py:152
  153.8 9.7 %fusion.2 = f32[512,3072]{1,0:T(8,128)S(1)} fusion(bf16[2048,4608]{1,0:T(8,128)(2,1)} %all-gather.5.cloned.1.call-done, bf16[128,2048]{1,0:T(8,128)(2,1)S(1)} %copy-done.38, bf16[128,2048]{1,0:T(8,128)(2,1)} %collective-permute-done.28, bf16[128,2048]{1,0:T(8,128)(2,1)S(1)} %copy-done.37, bf16[128,2048]{1,0:T(8,128)(2,1)S(1)} %copy-done.40), kind=kOutput, calls=%fused_computation.2 | convolution fusion | flops 6450839552 | bytes 20971520 | tf_op jit(solution)/shard_map/dot_general | solution.py:152
  163.6 2.6 multiply_convert_fusion.1
  166.2 10.3 %fusion = f32[512,2048]{1,0:T(8,128)S(1)} fusion(bf16[2048,4608]{1,0:T(8,128)(2,1)} %all-gather.5.cloned.1.call-done, bf16[512,1536]{1,0:T(8,128)(2,1)S(1)} %get-tuple-element.94.rhs_two, bf16[512,1536]{1,0:T(8,128)(2,1)S(1)} %get-tuple-element.93.rhs_one), kind=kOutput, calls=%fused_computation | convolution fusion | flops 6448742400 | bytes 19922944 | tf_op jit(solution)/shard_map/dot_general | solution.py:156
  177.6 2.9 collective-permute-start.30
  182.4 8.6 %collective-permute-done.30 = bf16[128,2048]{1,0:T(8,128)(2,1)S(1)} collective-permute-done((bf16[128,2048]{1,0:T(8,128)(2,1)S(1)}, bf16[128,2048]{1,0:T(8,128)(2,1)S(1)}, u32[]{:S(2)}, u32[]{:S(2)}) %collective-permute-start.30) | collective-permute-done | bytes 524320 | tf_op jit(solution)/shard_map/ppermute | solution.py:60
  193.6 13.5 %shard_map.313 = bf16[2048,4608]{1,0:T(8,128)(2,1)} custom-call(bf16[512,2048]{1,0:T(8,128)(2,1)S(1)} %pad_maximum_fusion.1.lhs_one, bf16[512,2048]{1,0:T(8,128)(2,1)S(1)} %copy-done.9, bf16[512,1536]{1,0:T(8,128)(2,1)S(1)} %get-tuple-element.93.rhs_one, bf16[512,1536]{1,0:T(8,128)(2,1)S(1)} %get-tuple-element.94.rhs_two, ...), custom_call_target="tpu_custom_call" | custom-call | flops 9663676416 | bytes 18874368 | tf_op jit(solution)/shard_map/pallas_call | solution.py:632
  207.1 3.2 multiply_reduce_fusion
  210.3 3.1 fusion.69
  213.5 3.6 collective-permute-start.34
  217.1 6.7 %collective-permute-done.34 = bf16[128,2048]{1,0:T(8,128)(2,1)S(1)} collective-permute-done((bf16[128,2048]{1,0:T(8,128)(2,1)S(1)}, bf16[128,2048]{1,0:T(8,128)(2,1)S(1)}, u32[]{:S(2)}, u32[]{:S(2)}) %collective-permute-start.34) | collective-permute-done | bytes 524320 | tf_op jit(solution)/shard_map/ppermute | solution.py:60
  223.8 2.5 collective-permute-start.35
  226.2 8.3 %fusion.20 = bf16[512,2048]{1,0:T(8,128)(2,1)} fusion(bf16[512,1536]{1,0:T(8,128)(2,1)S(1)} %copy-done.12, bf16[2048,4608]{1,0:T(8,128)(2,1)} %all-gather.5.cloned.1.call-done), kind=kOutput, calls=%fused_computation.27 | convolution fusion | flops 3222274048 | bytes 9961472 | tf_op jit(solution)/shard_map/dot_general | solution.py:156
  234.7 4.4 %fusion.27.grad_ref = f32[512,640]{1,0:T(8,128)S(1)} fusion(bf16[2048,1920]{1,0:T(8,128)(2,1)} %all-gather.3.cloned.1.call-done, bf16[128,2048]{1,0:T(8,128)(2,1)S(1)} %get-tuple-element.130, bf16[128,2048]{1,0:T(8,128)(2,1)S(1)} %collective-permute-done.35, bf16[128,2048]{1,0:T(8,128)(2,1)S(1)} %get-tuple-element.129, ...), kind=kOutput, calls=%fused_computation.32 | convolution fusion | flops 1350565888 | bytes 6029312 | tf_op jit(solution)/shard_map/dot_general | solution.py:152
  239.1 2.6 shard_map.308
  247.4 2.8 collective-permute-start.38
  251.1 2.0 collective-permute-done.38.refs_2_
  254.9 1.7 collective-permute-start.40
  258.8 3.1 collective-permute-done.41.piece2
  267.3 1.7 copy-done.18
  270.4 11.3 %shard_map.310 = (bf16[512,1280]{1,0:T(8,128)(2,1)S(1)}, f32[512,640]{1,0:T(8,128)S(1)}, f32[64,640]{1,0:T(8,128)S(1)}, f32[8,640]{1,0:T(8,128)S(1)}) custom-call(s32[4]{0:T(128)S(1)} %pad_add_fusion.spot_ref, f32[8,640]{1,0:T(8,128)S(1)} %get-tuple-element.75.piece0, f32[8,640]{1,0:T(8,128)S(1)} %collective-permute-done.40.piece1, ...), custom_call_target="tpu_custom_call" | custom-call | bytes 40000000 | tf_op jit(solution)/shard_map/pallas_call | solution.py:881
  284.4 7.6 %shard_map.312 = (bf16[16,216,640]{2,1,0:T(8,128)(2,1)S(1)}, bf16[16,216,640]{2,1,0:T(8,128)(2,1)}) custom-call(s32[4]{0:T(128)S(1)} %pad_add_fusion.spot_ref, bf16[32,24,640]{2,1,0:T(8,128)(2,1)S(1)} %shard_map.311.small_ref, bf16[512,2048]{1,0:T(8,128)(2,1)S(1)} %pad_maximum_fusion.2.refs_0_, bf16[576,2048]{1,0:T(8,128)(2,1)S(1)} %copy-done.8, ...), custom_call_target="tpu_custom_call" | custom-call | flops 4026531840 | bytes 20000000 | tf_op jit(solution)/shard_map/pallas_call | solution.py:711
  292.1 2.5 collective-permute-start.50
  294.6 5.8 %fusion.17 = bf16[512,2048]{1,0:T(8,128)(2,1)S(1)} fusion(bf16[2048,1920]{1,0:T(8,128)(2,1)} %all-gather.3.cloned.1.call-done, bf16[512,640]{1,0:T(8,128)(2,1)S(1)} %copy-done.24, bf16[512,640]{1,0:T(8,128)(2,1)S(1)} %bitcast.71), kind=kOutput, calls=%fused_computation.26 | convolution fusion | flops 2688024576 | bytes 8650752 | tf_op jit(solution)/shard_map/dot_general | solution.py:156
  302.9 3.3 add_convert_fusion
  306.2 6.5 %all-to-all-start = ((bf16[16,216,640]{2,1,0:T(8,128)(2,1)}), bf16[16,216,640]{2,1,0:T(8,128)(2,1)}, u32[]{:S(2)}, u32[]{:S(2)}) async-start(bf16[16,216,640]{2,1,0:T(8,128)(2,1)} %add_convert_fusion), calls=%async_computation | async-start | bytes 8847360 | tf_op jit(solution)/shard_map/all_to_all | solution.py:137
  316.4 10.7 %collective-permute-done.44 = bf16[128,2048]{1,0:T(8,128)(2,1)S(1)} collective-permute-done((bf16[128,2048]{1,0:T(8,128)(2,1)}, bf16[128,2048]{1,0:T(8,128)(2,1)S(1)}, u32[]{:S(2)}, u32[]{:S(2)}) %collective-permute-start.44) | collective-permute-done | bytes 524320 | tf_op jit(solution)/shard_map/ppermute | solution.py:60
  327.0 2.4 fusion.38
  330.5 3.3 collective-permute-start.48
  333.9 12.4 %collective-permute-done.48 = bf16[128,2048]{1,0:T(8,128)(2,1)S(1)} collective-permute-done((bf16[128,2048]{1,0:T(8,128)(2,1)}, bf16[128,2048]{1,0:T(8,128)(2,1)S(1)}, u32[]{:S(2)}, u32[]{:S(2)}) %collective-permute-start.48) | collective-permute-done | bytes 524320 | tf_op jit(solution)/shard_map/ppermute | solution.py:60
  346.5 2.7 collective-permute-start.49
  349.2 2.9 fusion.42
  352.0 3.9 collective-permute-done.49
  356.0 2.3 add_convert_fusion.2
  358.3 20.8 %all-to-all-done = bf16[16,216,640]{2,1,0:T(8,128)(2,1)} async-done(((bf16[16,216,640]{2,1,0:T(8,128)(2,1)}), bf16[16,216,640]{2,1,0:T(8,128)(2,1)}, u32[]{:S(2)}, u32[]{:S(2)}) %all-to-all-start) | async-done | bytes 4423712 | tf_op jit(solution)/shard_map/all_to_all | solution.py:137
  379.1 3.0 convert_reduce_fusion
  383.1 11.7 %collective-permute-start.53 = (f32[1,128]{1,0:T(1,128)S(1)}, f32[1,128]{1,0:T(1,128)S(1)}, u32[]{:S(2)}, u32[]{:S(2)}) collective-permute-start(f32[1,128]{1,0:T(1,128)S(1)} %maximum_bitcast_fusion), channel_id=1, source_target_pairs={{0,64},{32,96},{64,0},{96,32},{1,65},{33,97},{65,1},{97,33},{2,66}... | collective-permute-start | bytes 1544 | tf_op jit(solution)/shard_map/ppermute | solution.py:25
  394.8 2.0 collective-permute-start.51
  400.5 2.1 convert_bitcast_fusion
  (290 shorter events, 84.3 us)
Async XLA Ops:
  7.2 57.0 %all-gather.3.cloned.1.call-start = ((), (), s32[]{:S(2)}) async-start(), calls=%async_computation.2 | async-start | bytes 8110080 | tf_op jit(solution)/shard_map/all_gather | solution.py:772
  8.9 137.6 %all-gather.5.cloned.1.call-start = ((), (), s32[]{:S(2)}) async-start(), calls=%async_computation.3 | async-start | bytes 19464192 | tf_op jit(solution)/shard_map/all_gather | solution.py:797
  9.0 21.5 %collective-permute-start = (bf16[128,2048]{1,0:T(8,128)(2,1)}, bf16[128,2048]{1,0:T(8,128)(2,1)S(1)}, u32[]{:S(2)}, u32[]{:S(2)}) collective-permute-start(bf16[128,2048]{1,0:T(8,128)(2,1)} %param.18), channel_id=1, source_target_pairs={{0,96},{1,33},{2,98},{3,35},{4,100},{5,37},{6,102},{7,39},{8,104},... | collective-permute-start | bytes 1572872 | tf_op jit(solution)/shard_map/ppermute | solution.py:60
  9.6 13.3 %collective-permute-start.1 = (bf16[128,2048]{1,0:T(8,128)(2,1)}, bf16[128,2048]{1,0:T(8,128)(2,1)S(1)}, u32[]{:S(2)}, u32[]{:S(2)}) collective-permute-start(bf16[128,2048]{1,0:T(8,128)(2,1)} %param.18), channel_id=1, source_target_pairs={{0,32},{1,97},{2,34},{3,99},{4,36},{5,101},{6,38},{7,103},{8,40},{... | collective-permute-start | bytes 1572872 | tf_op jit(solution)/shard_map/ppermute | solution.py:60
  14.3 2.1 collective-permute-start.7
  17.0 5.1 %collective-permute-start.10 = (bf16[2,16,640]{2,1,0:T(8,128)(2,1)}, bf16[2,16,640]{2,1,0:T(8,128)(2,1)S(1)}, u32[]{:S(2)}, u32[]{:S(2)}) collective-permute-start(bf16[2,16,640]{2,1,0:T(8,128)(2,1)} %get-tuple-element.144), channel_id=1, source_target_pairs={{0,2},{1,3},{2,4},{3,5},{4,6},{5,7},{6,0},{7,1},{8,10},{9,11},{10,... | collective-permute-start | bytes 122888 | tf_op jit(solution)/shard_map/ppermute | solution.py:42
  18.6 6.2 %collective-permute-start.9 = (bf16[2,16,640]{2,1,0:T(8,128)(2,1)}, bf16[2,16,640]{2,1,0:T(8,128)(2,1)}, u32[]{:S(2)}, u32[]{:S(2)}) collective-permute-start(bf16[2,16,640]{2,1,0:T(8,128)(2,1)} %get-tuple-element.144), channel_id=1, source_target_pairs={{0,4},{1,5},{2,6},{3,7},{4,0},{5,1},{6,2},{7,3},{8,12},{9,13},{10,... | collective-permute-start | bytes 122888 | tf_op jit(solution)/shard_map/ppermute | solution.py:42
  18.6 6.2 %collective-permute-start.8 = (bf16[2,16,640]{2,1,0:T(8,128)(2,1)}, bf16[2,16,640]{2,1,0:T(8,128)(2,1)}, u32[]{:S(2)}, u32[]{:S(2)}) collective-permute-start(bf16[2,16,640]{2,1,0:T(8,128)(2,1)} %get-tuple-element.144), channel_id=1, source_target_pairs={{0,6},{1,7},{2,0},{3,1},{4,2},{5,3},{6,4},{7,5},{8,14},{9,15},{10,... | collective-permute-start | bytes 122888 | tf_op jit(solution)/shard_map/ppermute | solution.py:42
  22.1 4.3 %collective-permute-start.3 = (bf16[16,2048]{1,0:T(8,128)(2,1)S(1)}, bf16[16,2048]{1,0:T(8,128)(2,1)S(1)}, u32[]{:S(2)}, u32[]{:S(2)}) collective-permute-start(bf16[16,2048]{1,0:T(8,128)(2,1)S(1)} %slice.200), channel_id=1, source_target_pairs={{0,1},{1,2},{2,3},{3,4},{4,5},{5,6},{6,7},{7,8},{8,9},{9,10},{10,1... | collective-permute-start | bytes 196616 | tf_op jit(solution)/shard_map/ppermute | solution.py:776
  22.9 10.5 %collective-permute-start.2 = (bf16[128,2048]{1,0:T(8,128)(2,1)S(1)}, bf16[128,2048]{1,0:T(8,128)(2,1)S(1)}, u32[]{:S(2)}, u32[]{:S(2)}) collective-permute-start(bf16[128,2048]{1,0:T(8,128)(2,1)S(1)} %collective-permute-done.1), channel_id=1, source_target_pairs={{0,32},{1,97},{2,34},{3,99},{4,36},{5,101},{6,38},{7,103},{8,40},{... | collective-permute-start | bytes 1572872 | tf_op jit(solution)/shard_map/ppermute | solution.py:60
  26.4 11.9 %collective-permute-start.4 = (bf16[16,2048]{1,0:T(8,128)(2,1)S(1)}, bf16[16,2048]{1,0:T(8,128)(2,1)S(1)}, u32[]{:S(2)}, u32[]{:S(2)}) collective-permute-start(bf16[16,2048]{1,0:T(8,128)(2,1)S(1)} %collective-permute-done.3), channel_id=1, source_target_pairs={{0,96},{32,0},{64,32},{96,64},{1,97},{33,1},{65,33},{97,65},{2,98}... | collective-permute-start | bytes 196616 | tf_op jit(solution)/shard_map/ppermute | solution.py:25
  26.9 12.7 %collective-permute-start.5 = (bf16[16,2048]{1,0:T(8,128)(2,1)S(1)}, bf16[16,2048]{1,0:T(8,128)(2,1)S(1)}, u32[]{:S(2)}, u32[]{:S(2)}) collective-permute-start(bf16[16,2048]{1,0:T(8,128)(2,1)S(1)} %collective-permute-done.3), channel_id=1, source_target_pairs={{0,64},{32,96},{64,0},{96,32},{1,65},{33,97},{65,1},{97,33},{2,66}... | collective-permute-start | bytes 196616 | tf_op jit(solution)/shard_map/ppermute | solution.py:25
  30.5 10.8 %collective-permute-start.6 = (bf16[16,2048]{1,0:T(8,128)(2,1)S(1)}, bf16[16,2048]{1,0:T(8,128)(2,1)S(1)}, u32[]{:S(2)}, u32[]{:S(2)}) collective-permute-start(bf16[16,2048]{1,0:T(8,128)(2,1)S(1)} %collective-permute-done.3), channel_id=1, source_target_pairs={{0,32},{32,64},{64,96},{96,0},{1,33},{33,65},{65,97},{97,1},{2,34}... | collective-permute-start | bytes 196616 | tf_op jit(solution)/shard_map/ppermute | solution.py:25
  33.6 8.3 %collective-permute-start.13 = (bf16[4,2,16,640]{3,2,1,0:T(8,128)(2,1)S(1)}, bf16[4,2,16,640]{3,2,1,0:T(8,128)(2,1)S(1)}, u32[]{:S(2)}, u32[]{:S(2)}) collective-permute-start(bf16[4,2,16,640]{3,2,1,0:T(8,128)(2,1)S(1)} %pad_maximum_fusion.7), channel_id=1, source_target_pairs={{0,8},{1,9},{2,10},{3,11},{4,12},{5,13},{6,14},{7,15},{8,16},{9,17... | collective-permute-start | bytes 491528 | tf_op jit(solution)/shard_map/ppermute | solution.py:42
  35.2 10.8 %collective-permute-start.12 = (bf16[4,2,16,640]{3,2,1,0:T(8,128)(2,1)S(1)}, bf16[4,2,16,640]{3,2,1,0:T(8,128)(2,1)S(1)}, u32[]{:S(2)}, u32[]{:S(2)}) collective-permute-start(bf16[4,2,16,640]{3,2,1,0:T(8,128)(2,1)S(1)} %pad_maximum_fusion.7), channel_id=1, source_target_pairs={{0,16},{1,17},{2,18},{3,19},{4,20},{5,21},{6,22},{7,23},{8,24},{9,... | collective-permute-start | bytes 491528 | tf_op jit(solution)/shard_map/ppermute | solution.py:42
  38.3 7.8 %collective-permute-start.11 = (bf16[4,2,16,640]{3,2,1,0:T(8,128)(2,1)S(1)}, bf16[4,2,16,640]{3,2,1,0:T(8,128)(2,1)S(1)}, u32[]{:S(2)}, u32[]{:S(2)}) collective-permute-start(bf16[4,2,16,640]{3,2,1,0:T(8,128)(2,1)S(1)} %pad_maximum_fusion.7), channel_id=1, source_target_pairs={{0,24},{1,25},{2,26},{3,27},{4,28},{5,29},{6,30},{7,31},{8,0},{9,1... | collective-permute-start | bytes 491528 | tf_op jit(solution)/shard_map/ppermute | solution.py:42
  39.6 9.6 %collective-permute-start.14 = (bf16[128,2048]{1,0:T(8,128)(2,1)}, bf16[128,2048]{1,0:T(8,128)(2,1)}, u32[]{:S(2)}, u32[]{:S(2)}) collective-permute-start(bf16[128,2048]{1,0:T(8,128)(2,1)} %param.35), channel_id=1, source_target_pairs={{0,32},{1,97},{2,34},{3,99},{4,36},{5,101},{6,38},{7,103},{8,40},{... | collective-permute-start | bytes 1572872 | tf_op jit(solution)/shard_map/ppermute | solution.py:60
  49.2 9.5 %collective-permute-start.15 = (bf16[128,2048]{1,0:T(8,128)(2,1)}, bf16[128,2048]{1,0:T(8,128)(2,1)}, u32[]{:S(2)}, u32[]{:S(2)}) collective-permute-start(bf16[128,2048]{1,0:T(8,128)(2,1)} %collective-permute-done.14), channel_id=1, source_target_pairs={{0,32},{1,97},{2,34},{3,99},{4,36},{5,101},{6,38},{7,103},{8,40},{... | collective-permute-start | bytes 1572872 | tf_op jit(solution)/shard_map/ppermute | solution.py:60
  58.7 341.8 %reduce-scatter.2.cloned.1.call-start = ((), (), s32[]{:S(2)}) async-start(), calls=%async_computation.4 | async-start | bytes 19464192 | tf_op jit(solution)/shard_map/reduce_scatter | solution.py:865
  64.2 29.7 %copy-start.51 = (bf16[2048,1920]{1,0:T(8,128)(2,1)S(1)}, bf16[2048,1920]{1,0:T(8,128)(2,1)}, u32[]{:S(2)}) copy-start(bf16[2048,1920]{1,0:T(8,128)(2,1)} %all-gather.3.cloned.1.call-done) | copy-start | bytes 23592964
  78.6 1.2 collective-permute-start.16
  79.8 7.9 %collective-permute-start.17 = (f32[2,8,640]{2,1,0:T(8,128)S(1)}, f32[2,8,640]{2,1,0:T(8,128)S(1)}, u32[]{:S(2)}, u32[]{:S(2)}) collective-permute-start(f32[2,8,640]{2,1,0:T(8,128)S(1)} %pad_maximum_fusion.9.refs_0_), channel_id=1, source_target_pairs={{0,6},{1,7},{2,0},{3,1},{4,2},{5,3},{6,4},{7,5},{8,14},{9,15},{10,... | collective-permute-start | bytes 122888 | tf_op jit(solution)/shard_map/ppermute | solution.py:42
  81.1 6.7 %collective-permute-start.18 = (f32[2,8,640]{2,1,0:T(8,128)S(1)}, f32[2,8,640]{2,1,0:T(8,128)S(1)}, u32[]{:S(2)}, u32[]{:S(2)}) collective-permute-start(f32[2,8,640]{2,1,0:T(8,128)S(1)} %pad_maximum_fusion.9.refs_0_), channel_id=1, source_target_pairs={{0,4},{1,5},{2,6},{3,7},{4,0},{5,1},{6,2},{7,3},{8,12},{9,13},{10,... | collective-permute-start | bytes 122888 | tf_op jit(solution)/shard_map/ppermute | solution.py:42
  85.0 4.9 %collective-permute-start.19 = (f32[2,8,640]{2,1,0:T(8,128)S(1)}, f32[2,8,640]{2,1,0:T(8,128)S(1)}, u32[]{:S(2)}, u32[]{:S(2)}) collective-permute-start(f32[2,8,640]{2,1,0:T(8,128)S(1)} %pad_maximum_fusion.9.refs_0_), channel_id=1, source_target_pairs={{0,2},{1,3},{2,4},{3,5},{4,6},{5,7},{6,0},{7,1},{8,10},{9,11},{10,... | collective-permute-start | bytes 122888 | tf_op jit(solution)/shard_map/ppermute | solution.py:42
  90.6 6.7 %collective-permute-start.20 = (f32[8,640]{1,0:T(8,128)S(1)}, f32[8,640]{1,0:T(8,128)S(1)}, u32[]{:S(2)}, u32[]{:S(2)}) collective-permute-start(f32[8,640]{1,0:T(8,128)S(1)} %get-tuple-element.62.piece0), channel_id=1, source_target_pairs={{0,24},{1,25},{2,26},{3,27},{4,28},{5,29},{6,30},{7,31},{8,0},{9,1... | collective-permute-start | bytes 61448 | tf_op jit(solution)/shard_map/ppermute | solution.py:42
  91.6 5.7 %collective-permute-start.21 = (f32[8,640]{1,0:T(8,128)S(1)}, f32[8,640]{1,0:T(8,128)S(1)}, u32[]{:S(2)}, u32[]{:S(2)}) collective-permute-start(f32[8,640]{1,0:T(8,128)S(1)} %get-tuple-element.62.piece0), channel_id=1, source_target_pairs={{0,16},{1,17},{2,18},{3,19},{4,20},{5,21},{6,22},{7,23},{8,24},{9,... | collective-permute-start | bytes 61448 | tf_op jit(solution)/shard_map/ppermute | solution.py:42
  92.9 5.0 %collective-permute-start.22 = (f32[8,640]{1,0:T(8,128)S(1)}, f32[8,640]{1,0:T(8,128)S(1)}, u32[]{:S(2)}, u32[]{:S(2)}) collective-permute-start(f32[8,640]{1,0:T(8,128)S(1)} %get-tuple-element.62.piece0), channel_id=1, source_target_pairs={{0,8},{1,9},{2,10},{3,11},{4,12},{5,13},{6,14},{7,15},{8,16},{9,17... | collective-permute-start | bytes 61448 | tf_op jit(solution)/shard_map/ppermute | solution.py:42
  102.1 13.9 %collective-permute-start.24 = (bf16[128,2048]{1,0:T(8,128)(2,1)S(1)}, bf16[128,2048]{1,0:T(8,128)(2,1)S(1)}, u32[]{:S(2)}, u32[]{:S(2)}) collective-permute-start(bf16[128,2048]{1,0:T(8,128)(2,1)S(1)} %get-tuple-element.124), channel_id=1, source_target_pairs={{0,32},{1,97},{2,34},{3,99},{4,36},{5,101},{6,38},{7,103},{8,40},{... | collective-permute-start | bytes 1572872 | tf_op jit(solution)/shard_map/ppermute | solution.py:60
  104.5 14.5 %collective-permute-start.23 = (bf16[128,2048]{1,0:T(8,128)(2,1)}, bf16[128,2048]{1,0:T(8,128)(2,1)}, u32[]{:S(2)}, u32[]{:S(2)}) collective-permute-start(bf16[128,2048]{1,0:T(8,128)(2,1)} %get-tuple-element.123), channel_id=1, source_target_pairs={{0,96},{1,33},{2,98},{3,35},{4,100},{5,37},{6,102},{7,39},{8,104},... | collective-permute-start | bytes 1572872 | tf_op jit(solution)/shard_map/ppermute | solution.py:60
  116.9 10.4 %collective-permute-start.25 = (bf16[128,2048]{1,0:T(8,128)(2,1)}, bf16[128,2048]{1,0:T(8,128)(2,1)}, u32[]{:S(2)}, u32[]{:S(2)}) collective-permute-start(bf16[128,2048]{1,0:T(8,128)(2,1)} %add_convert_fusion.6), channel_id=1, source_target_pairs={{0,32},{1,97},{2,34},{3,99},{4,36},{5,101},{6,38},{7,103},{8,40},{... | collective-permute-start | bytes 1572872 | tf_op jit(solution)/shard_map/ppermute | solution.py:60
  118.3 15.6 %collective-permute-start.29 = (bf16[128,2048]{1,0:T(8,128)(2,1)}, bf16[128,2048]{1,0:T(8,128)(2,1)}, u32[]{:S(2)}, u32[]{:S(2)}) collective-permute-start(bf16[128,2048]{1,0:T(8,128)(2,1)} %param.35), channel_id=1, source_target_pairs={{0,96},{1,33},{2,98},{3,35},{4,100},{5,37},{6,102},{7,39},{8,104},... | collective-permute-start | bytes 1572872 | tf_op jit(solution)/shard_map/ppermute | solution.py:60
  131.9 12.6 %collective-permute-start.26 = (bf16[128,2048]{1,0:T(8,128)(2,1)S(1)}, bf16[128,2048]{1,0:T(8,128)(2,1)S(1)}, u32[]{:S(2)}, u32[]{:S(2)}) collective-permute-start(bf16[128,2048]{1,0:T(8,128)(2,1)S(1)} %multiply_convert_fusion.3), channel_id=1, source_target_pairs={{0,96},{1,33},{2,98},{3,35},{4,100},{5,37},{6,102},{7,39},{8,104},... | collective-permute-start | bytes 1572872 | tf_op jit(solution)/shard_map/ppermute | solution.py:60
  133.6 10.3 %collective-permute-start.27 = (bf16[128,2048]{1,0:T(8,128)(2,1)S(1)}, bf16[128,2048]{1,0:T(8,128)(2,1)}, u32[]{:S(2)}, u32[]{:S(2)}) collective-permute-start(bf16[128,2048]{1,0:T(8,128)(2,1)S(1)} %multiply_convert_fusion.3), channel_id=1, source_target_pairs={{0,32},{1,97},{2,34},{3,99},{4,36},{5,101},{6,38},{7,103},{8,40},{... | collective-permute-start | bytes 1572872 | tf_op jit(solution)/shard_map/ppermute | solution.py:60
  143.9 9.9 %collective-permute-start.28 = (bf16[128,2048]{1,0:T(8,128)(2,1)}, bf16[128,2048]{1,0:T(8,128)(2,1)}, u32[]{:S(2)}, u32[]{:S(2)}) collective-permute-start(bf16[128,2048]{1,0:T(8,128)(2,1)} %collective-permute-done.27), channel_id=1, source_target_pairs={{0,32},{1,97},{2,34},{3,99},{4,36},{5,101},{6,38},{7,103},{8,40},{... | collective-permute-start | bytes 1572872 | tf_op jit(solution)/shard_map/ppermute | solution.py:60
  166.2 27.4 %copy-start.11 = (bf16[512,1536]{1,0:T(8,128)(2,1)}, bf16[512,1536]{1,0:T(8,128)(2,1)S(1)}, u32[]{:S(2)}) copy-start(bf16[512,1536]{1,0:T(8,128)(2,1)S(1)} %get-tuple-element.95.rhs_three) | copy-start | bytes 4718596
  177.6 13.4 %collective-permute-start.30 = (bf16[128,2048]{1,0:T(8,128)(2,1)S(1)}, bf16[128,2048]{1,0:T(8,128)(2,1)S(1)}, u32[]{:S(2)}, u32[]{:S(2)}) collective-permute-start(bf16[128,2048]{1,0:T(8,128)(2,1)S(1)} %get-tuple-element.122), channel_id=1, source_target_pairs={{0,32},{1,97},{2,34},{3,99},{4,36},{5,101},{6,38},{7,103},{8,40},{... | collective-permute-start | bytes 1572872 | tf_op jit(solution)/shard_map/ppermute | solution.py:60
  180.5 26.6 %collective-permute-start.31 = (bf16[128,2048]{1,0:T(8,128)(2,1)}, bf16[128,2048]{1,0:T(8,128)(2,1)}, u32[]{:S(2)}, u32[]{:S(2)}) collective-permute-start(bf16[128,2048]{1,0:T(8,128)(2,1)} %get-tuple-element.121), channel_id=1, source_target_pairs={{0,96},{1,33},{2,98},{3,35},{4,100},{5,37},{6,102},{7,39},{8,104},... | collective-permute-start | bytes 1572872 | tf_op jit(solution)/shard_map/ppermute | solution.py:60
  192.0 15.1 %collective-permute-start.32 = (bf16[128,2048]{1,0:T(8,128)(2,1)}, bf16[128,2048]{1,0:T(8,128)(2,1)}, u32[]{:S(2)}, u32[]{:S(2)}) collective-permute-start(bf16[128,2048]{1,0:T(8,128)(2,1)} %add_convert_fusion.5), channel_id=1, source_target_pairs={{0,32},{1,97},{2,34},{3,99},{4,36},{5,101},{6,38},{7,103},{8,40},{... | collective-permute-start | bytes 1572872 | tf_op jit(solution)/shard_map/ppermute | solution.py:60
  213.5 10.3 %collective-permute-start.34 = (bf16[128,2048]{1,0:T(8,128)(2,1)S(1)}, bf16[128,2048]{1,0:T(8,128)(2,1)S(1)}, u32[]{:S(2)}, u32[]{:S(2)}) collective-permute-start(bf16[128,2048]{1,0:T(8,128)(2,1)S(1)} %get-tuple-element.109), channel_id=1, source_target_pairs={{0,32},{1,97},{2,34},{3,99},{4,36},{5,101},{6,38},{7,103},{8,40},{... | collective-permute-start | bytes 1572872 | tf_op jit(solution)/shard_map/ppermute | solution.py:60
  217.1 17.4 %collective-permute-start.33 = (bf16[128,2048]{1,0:T(8,128)(2,1)S(1)}, bf16[128,2048]{1,0:T(8,128)(2,1)S(1)}, u32[]{:S(2)}, u32[]{:S(2)}) collective-permute-start(bf16[128,2048]{1,0:T(8,128)(2,1)S(1)} %get-tuple-element.109), channel_id=1, source_target_pairs={{0,96},{1,33},{2,98},{3,35},{4,100},{5,37},{6,102},{7,39},{8,104},... | collective-permute-start | bytes 1572872 | tf_op jit(solution)/shard_map/ppermute | solution.py:60
  223.8 10.9 %collective-permute-start.35 = (bf16[128,2048]{1,0:T(8,128)(2,1)S(1)}, bf16[128,2048]{1,0:T(8,128)(2,1)S(1)}, u32[]{:S(2)}, u32[]{:S(2)}) collective-permute-start(bf16[128,2048]{1,0:T(8,128)(2,1)S(1)} %collective-permute-done.34), channel_id=1, source_target_pairs={{0,32},{1,97},{2,34},{3,99},{4,36},{5,101},{6,38},{7,103},{8,40},{... | collective-permute-start | bytes 1572872 | tf_op jit(solution)/shard_map/ppermute | solution.py:60
  245.8 1.2 collective-permute-start.36
  247.0 4.1 collective-permute-start.37
  247.4 5.6 %collective-permute-start.38 = (f32[2,8,640]{2,1,0:T(8,128)S(1)}, f32[2,8,640]{2,1,0:T(8,128)S(1)}, u32[]{:S(2)}, u32[]{:S(2)}) collective-permute-start(f32[2,8,640]{2,1,0:T(8,128)S(1)} %pad_maximum_fusion.10.refs_0_), channel_id=1, source_target_pairs={{0,4},{1,5},{2,6},{3,7},{4,0},{5,1},{6,2},{7,3},{8,12},{9,13},{10,... | collective-permute-start | bytes 122888 | tf_op jit(solution)/shard_map/ppermute | solution.py:42
  250.3 4.0 collective-permute-start.39
  254.9 3.9 collective-permute-start.40
  256.6 5.3 %collective-permute-start.41 = (f32[8,640]{1,0:T(8,128)S(1)}, f32[8,640]{1,0:T(8,128)S(1)}, u32[]{:S(2)}, u32[]{:S(2)}) collective-permute-start(f32[8,640]{1,0:T(8,128)S(1)} %get-tuple-element.75.piece0), channel_id=1, source_target_pairs={{0,16},{1,17},{2,18},{3,19},{4,20},{5,21},{6,22},{7,23},{8,24},{9,... | collective-permute-start | bytes 61448 | tf_op jit(solution)/shard_map/ppermute | solution.py:42
  257.1 5.2 %collective-permute-start.42 = (f32[8,640]{1,0:T(8,128)S(1)}, f32[8,640]{1,0:T(8,128)S(1)}, u32[]{:S(2)}, u32[]{:S(2)}) collective-permute-start(f32[8,640]{1,0:T(8,128)S(1)} %get-tuple-element.75.piece0), channel_id=1, source_target_pairs={{0,8},{1,9},{2,10},{3,11},{4,12},{5,13},{6,14},{7,15},{8,16},{9,17... | collective-permute-start | bytes 61448 | tf_op jit(solution)/shard_map/ppermute | solution.py:42
  281.6 2.6 collective-permute-start.43
  292.1 10.8 %collective-permute-start.50 = (bf16[16,216,640]{2,1,0:T(8,128)(2,1)}, bf16[16,216,640]{2,1,0:T(8,128)(2,1)S(1)}, u32[]{:S(2)}, u32[]{:S(2)}) collective-permute-start(bf16[16,216,640]{2,1,0:T(8,128)(2,1)} %get-tuple-element.89), channel_id=1, source_target_pairs={{0,1},{1,0},{2,3},{3,2},{4,5},{5,4},{6,7},{7,6},{8,9},{9,8},{10,11... | collective-permute-start | bytes 13271048 | tf_op jit(solution)/shard_map/ppermute | solution.py:42
  301.5 11.9 %collective-permute-start.45 = (bf16[128,2048]{1,0:T(8,128)(2,1)}, bf16[128,2048]{1,0:T(8,128)(2,1)S(1)}, u32[]{:S(2)}, u32[]{:S(2)}) collective-permute-start(bf16[128,2048]{1,0:T(8,128)(2,1)} %get-tuple-element.128), channel_id=1, source_target_pairs={{0,32},{1,97},{2,34},{3,99},{4,36},{5,101},{6,38},{7,103},{8,40},{... | collective-permute-start | bytes 1572872 | tf_op jit(solution)/shard_map/ppermute | solution.py:60
  306.2 72.9 %all-to-all-start = ((bf16[16,216,640]{2,1,0:T(8,128)(2,1)}), bf16[16,216,640]{2,1,0:T(8,128)(2,1)}, u32[]{:S(2)}, u32[]{:S(2)}) async-start(bf16[16,216,640]{2,1,0:T(8,128)(2,1)} %add_convert_fusion), calls=%async_computation | async-start | bytes 8847360 | tf_op jit(solution)/shard_map/all_to_all | solution.py:137
  312.6 14.4 %collective-permute-start.44 = (bf16[128,2048]{1,0:T(8,128)(2,1)}, bf16[128,2048]{1,0:T(8,128)(2,1)S(1)}, u32[]{:S(2)}, u32[]{:S(2)}) collective-permute-start(bf16[128,2048]{1,0:T(8,128)(2,1)} %get-tuple-element.127), channel_id=1, source_target_pairs={{0,96},{1,33},{2,98},{3,35},{4,100},{5,37},{6,102},{7,39},{8,104},... | collective-permute-start | bytes 1572872 | tf_op jit(solution)/shard_map/ppermute | solution.py:60
  314.9 12.1 %collective-permute-start.46 = (bf16[128,2048]{1,0:T(8,128)(2,1)S(1)}, bf16[128,2048]{1,0:T(8,128)(2,1)S(1)}, u32[]{:S(2)}, u32[]{:S(2)}) collective-permute-start(bf16[128,2048]{1,0:T(8,128)(2,1)S(1)} %add_convert_fusion.4), channel_id=1, source_target_pairs={{0,32},{1,97},{2,34},{3,99},{4,36},{5,101},{6,38},{7,103},{8,40},{... | collective-permute-start | bytes 1572872 | tf_op jit(solution)/shard_map/ppermute | solution.py:60
  330.5 15.7 %collective-permute-start.48 = (bf16[128,2048]{1,0:T(8,128)(2,1)}, bf16[128,2048]{1,0:T(8,128)(2,1)S(1)}, u32[]{:S(2)}, u32[]{:S(2)}) collective-permute-start(bf16[128,2048]{1,0:T(8,128)(2,1)} %get-tuple-element.126), channel_id=1, source_target_pairs={{0,32},{1,97},{2,34},{3,99},{4,36},{5,101},{6,38},{7,103},{8,40},{... | collective-permute-start | bytes 1572872 | tf_op jit(solution)/shard_map/ppermute | solution.py:60
  333.9 18.2 %collective-permute-start.47 = (bf16[128,2048]{1,0:T(8,128)(2,1)}, bf16[128,2048]{1,0:T(8,128)(2,1)S(1)}, u32[]{:S(2)}, u32[]{:S(2)}) collective-permute-start(bf16[128,2048]{1,0:T(8,128)(2,1)} %get-tuple-element.125), channel_id=1, source_target_pairs={{0,96},{1,33},{2,98},{3,35},{4,100},{5,37},{6,102},{7,39},{8,104},... | collective-permute-start | bytes 1572872 | tf_op jit(solution)/shard_map/ppermute | solution.py:60
  346.5 9.5 %collective-permute-start.49 = (bf16[128,2048]{1,0:T(8,128)(2,1)S(1)}, bf16[128,2048]{1,0:T(8,128)(2,1)S(1)}, u32[]{:S(2)}, u32[]{:S(2)}) collective-permute-start(bf16[128,2048]{1,0:T(8,128)(2,1)S(1)} %add_convert_fusion.3), channel_id=1, source_target_pairs={{0,32},{1,97},{2,34},{3,99},{4,36},{5,101},{6,38},{7,103},{8,40},{... | collective-permute-start | bytes 1572872 | tf_op jit(solution)/shard_map/ppermute | solution.py:60
  358.3 23.8 %copy-start.43 = (bf16[64,640]{1,0:T(8,128)(2,1)S(1)}, bf16[64,640]{1,0:T(8,128)(2,1)}, u32[]{:S(2)}) copy-start(bf16[64,640]{1,0:T(8,128)(2,1)} %param.20) | copy-start | bytes 245764
  358.3 23.8 %copy-start.44 = (bf16[64,640]{1,0:T(8,128)(2,1)S(1)}, bf16[64,640]{1,0:T(8,128)(2,1)}, u32[]{:S(2)}) copy-start(bf16[64,640]{1,0:T(8,128)(2,1)} %param.21) | copy-start | bytes 245764
  358.3 24.7 %copy-start.49 = (bf16[64]{0:T(256)(128)(2,1)S(1)}, bf16[64]{0:T(256)(128)(2,1)}, u32[]{:S(2)}) copy-start(bf16[64]{0:T(256)(128)(2,1)} %param.19) | copy-start | bytes 388
  358.3 39.1 %copy-start.50 = (bf16[20]{0:T(256)(128)(2,1)S(1)}, bf16[20]{0:T(256)(128)(2,1)}, u32[]{:S(2)}) copy-start(bf16[20]{0:T(256)(128)(2,1)} %param.28) | copy-start | bytes 124
  383.1 16.8 %collective-permute-start.53 = (f32[1,128]{1,0:T(1,128)S(1)}, f32[1,128]{1,0:T(1,128)S(1)}, u32[]{:S(2)}, u32[]{:S(2)}) collective-permute-start(f32[1,128]{1,0:T(1,128)S(1)} %maximum_bitcast_fusion), channel_id=1, source_target_pairs={{0,64},{32,96},{64,0},{96,32},{1,65},{33,97},{65,1},{97,33},{2,66}... | collective-permute-start | bytes 1544 | tf_op jit(solution)/shard_map/ppermute | solution.py:25
  394.8 5.1 %collective-permute-start.52 = (f32[1,128]{1,0:T(1,128)S(1)}, f32[1,128]{1,0:T(1,128)S(1)}, u32[]{:S(2)}, u32[]{:S(2)}) collective-permute-start(f32[1,128]{1,0:T(1,128)S(1)} %maximum_bitcast_fusion), channel_id=1, source_target_pairs={{0,96},{32,0},{64,32},{96,64},{1,97},{33,1},{65,33},{97,65},{2,98}... | collective-permute-start | bytes 1544 | tf_op jit(solution)/shard_map/ppermute | solution.py:25
  394.8 5.1 %collective-permute-start.51 = (f32[1,128]{1,0:T(1,128)S(1)}, f32[1,128]{1,0:T(1,128)S(1)}, u32[]{:S(2)}, u32[]{:S(2)}) collective-permute-start(f32[1,128]{1,0:T(1,128)S(1)} %maximum_bitcast_fusion), channel_id=1, source_target_pairs={{0,32},{32,64},{64,96},{96,0},{1,33},{33,65},{65,97},{97,1},{2,34}... | collective-permute-start | bytes 1544 | tf_op jit(solution)/shard_map/ppermute | solution.py:25
  (47 other events, 335.3 us)
Sparse Core Ops, SparseCore 0:
  10.8 53.2 all-gather.2
  66.4 79.8 all-gather.4
  210.4 169.4 reduce-scatter.1
where the time goes:
time: 418 us; the launch traced here: 410 us
  waiting for transfers between devices  121 us (29%)
  starting transfers between devices  90.3 us (22%)
  other arithmetic  58.7 us (14%)
  matrix products  53.8 us (13%)
  Pallas kernels  46.9 us (11%)
  local copies, waits for them, and re-layouts  24.2 us (6%)
  between operations  15.2 us (4%)
    ppermute x24, waiting for transfers between devices, hop_apart(): return lax.ppermute(values, ('blk', 'tok'), route)  78.4 us
    ppermute x24, starting transfers between devices, hop_apart(): return lax.ppermute(values, ('blk', 'tok'), route)  35.1 us
    ppermute x22, starting transfers between devices, hop_tok(): return lax.ppermute(values, 'tok', route)  30.5 us
    dot_general x5, matrix products, product(): return jnp.dot(operand, weight, preferred_element_type=f32).astype(out)  27.7 us
    dot_general x4, matrix products, product_back(): lax.dot_general(operand, weight, (((1,), (1,)), ((), ())), preferred_elem...  26.2 us
    all_to_all x1, waiting for transfers between devices, chips_sum(): lax.all_to_all(values, 'tok', 0, 0, axis_index_groups=cores, tiled=True)  20.8 us
    ppermute x6, starting transfers between devices, hop_blk(): lax.ppermute(values, 'blk', [(i, (i + distance) % MEMBERS) for i in range...  17.8 us
    ppermute x22, waiting for transfers between devices, hop_tok(): return lax.ppermute(values, 'tok', route)  16.5 us
  transfers between devices with their start and end apart: 58, of which 29 were waited for; matrix products, arithmetic and copies ran while one was open for 22% of the time, Pallas kernels for 11%

commit v1 on v0

--- a/solution.py
+++ b/solution.py
@@ -64,10 +64,10 @@
     return jnp.where(core == 0, first, second)
 
 
-def ring_gather(values, core):
+def ring_gather(values, core, before_last=()):
     behind = hop_apart(values, 1)
     ahead = hop_apart(values, -1)
-    far = hop_apart(behind, 1)
+    far = hop_apart(after(behind, *before_last), 1)
     return [values, either(core, ahead, behind), far, either(core, behind, ahead)]
 
 
@@ -203,23 +203,21 @@
     return pl.ds(pl.multiple_of(start, size), size)
 
 
-def conv_rows(ci_ref, slot, tile):
-    base = slot * OWN + tile * HALO
-    before = jnp.where(tile == 0, MEMBERS * OWN + slot * HALO, base - HALO)
-    return jnp.concatenate(
-        [ci_ref[rows_at(before, HALO), :].astype(f32), ci_ref[rows_at(base, HALO), :].astype(f32)],
-        axis=0,
-    )
+def conv_rows(ci_ref, halo_ref, tile):
+    before = halo_ref[...] if tile == 0 else ci_ref[(tile - 1) * HALO : tile * HALO, :]
+    here = ci_ref[tile * HALO : (tile + 1) * HALO, :]
+    return jnp.concatenate([before.astype(f32), here.astype(f32)], axis=0)
 
 
 def local_forward_kernel(
-    ci_ref,
-    place_ref,
     taps_ref,
     shift_ref,
     blocks_ref,
     bias_ref,
     soft_ref,
+    ci_ref,
+    halo_ref,
+    place_ref,
     conv_ref,
     rate_ref,
     entry_ref,
@@ -230,82 +228,67 @@
     pre_ref,
     high_ref,
 ):
+    slot = pl.program_id(0)
     channels = conv_ref.shape[1]
     block = blocks_ref.shape[0]
     width = 2 * channels
-    columns = lax.broadcasted_iota(jnp.int32, (HALO, width), 1)
-    columns = jnp.where(columns >= channels, columns - channels, columns)
-    for group in range(channels // block):
-        inside = (columns >= group * block) & (columns < (group + 1) * block)
-
-        def spread_gates(step, carry):
-            rows = blocks_ref[rows_at(step * HALO, HALO), :].astype(f32)
-            gates_ref[rows_at(group * block + step * HALO, HALO), :] = jnp.where(
-                inside, rows, 0.0
-            ).astype(bf16)
-            return carry
-
-        lax.fori_loop(0, block // HALO, spread_gates, 0)
-
-    for slot in range(MEMBERS):
-
-        def convolve(tile, carry):
-            base = slot * OWN + tile * HALO
-            rows = conv_rows(ci_ref, slot, tile)
-            places = place_ref[rows_at(base, HALO), :]
-            total = shift_ref[...] + taps_ref[0:1, :] * rows[HALO:]
-            for tap in range(1, CONV):
-                lagged = pltpu.roll(rows, tap, 0)[HALO:]
-                total = total + taps_ref[tap : tap + 1, :] * jnp.where(places >= tap, lagged, 0.0)
-            conv_ref[rows_at(base, HALO), :] = total
-            high_ref[rows_at(base, HALO), :] = total.astype(bf16)
-            return carry
-
-        lax.fori_loop(0, OWN // HALO, convolve, 0)
-
-    def gate(step, carry):
-        columns = pl.ds(pl.multiple_of(step * 256, 256), 256)
-        weight = gates_ref[:, columns]
+
+    @pl.when(slot == 0)
+    def spread_gates():
+        columns = lax.broadcasted_iota(jnp.int32, (HALO, width), 1)
+        columns = jnp.where(columns >= channels, columns - channels, columns)
+        for group in range(channels // block):
+            inside = (columns >= group * block) & (columns < (group + 1) * block)
+            for step in range(0, block, HALO):
+                rows = blocks_ref[step : step + HALO, :].astype(f32)
+                at = group * block + step
+                gates_ref[at : at + HALO, :] = jnp.where(inside, rows, 0.0).astype(bf16)
+
+    for tile in range(OWN // HALO):
+        at = slice(tile * HALO, (tile + 1) * HALO)
+        rows = conv_rows(ci_ref, halo_ref, tile)
+        places = place_ref[at, :]
+        total = shift_ref[...] + taps_ref[0:1, :] * rows[HALO:]
+        for tap in range(1, CONV):
+            lagged = pltpu.roll(rows, tap, 0)[HALO:]
+            total = total + taps_ref[tap : tap + 1, :] * jnp.where(places >= tap, lagged, 0.0)
+        conv_ref[at, :] = total
+        high_ref[at, :] = total.astype(bf16)
+    for step in range(0, width, 256):
+        columns = slice(step, step + 256)
         pre_ref[:, columns] = (
-            jnp.dot(high_ref[...], weight, preferred_element_type=f32) + bias_ref[:, columns]
+            jnp.dot(high_ref[...], gates_ref[:, columns], preferred_element_type=f32)
+            + bias_ref[:, columns]
         )
-        return carry
-
-    lax.fori_loop(0, 2 * channels // 256, gate, 0)
 
     row_ids = lax.broadcasted_iota(jnp.int32, (8, channels), 0)
 
     def scan(tile, carry):
-        ends = []
-        for slot in range(MEMBERS):
-            base = slot * OWN + tile * 8
-            rows = rows_at(base, 8)
-            rates = sigmoid(pre_ref[rows, :channels])
-            entries = 0.5 * jnp.tanh(0.5 * pre_ref[rows, channels:]) + 0.5
-            log_keep = -soft_ref[...] * rates
-            resets = place_ref[rows, :] == 0
-            keeps = jnp.where(resets, 0.0, jnp.exp(log_keep))
-            squared = one_minus_exp(2.0 * log_keep)
-            scaling = jnp.where(resets, 1.0, squared * inverse_root(squared))
-            value = entries * conv_ref[rows, :] * scaling
-            coeff = keeps
-            for distance in (1, 2, 4):
-                reach = row_ids >= distance
-                value = value + coeff * jnp.where(reach, pltpu.roll(value, distance, 0), 0.0)
-                coeff = coeff * jnp.where(reach, pltpu.roll(coeff, distance, 0), 1.0)
-            cum, state = carry[2 * slot], carry[2 * slot + 1]
-            value = value + coeff * state
-            coeff = coeff * cum
-            rate_ref[rows, :] = rates
-            entry_ref[rows, :] = entries
-            local_ref[rows, :] = value
-            cum_ref[rows, :] = coeff
-            ends += [coeff[7:8], value[7:8]]
-        return tuple(ends)
-
-    start = (jnp.ones((1, channels), f32), jnp.zeros((1, channels), f32)) * MEMBERS
-    ends = lax.fori_loop(0, OWN // 8, scan, start)
-    edge_ref[...] = jnp.concatenate(ends[0::2] + ends[1::2], axis=0)
+        rows = rows_at(tile * 8, 8)
+        rates = sigmoid(pre_ref[rows, :channels])
+        entries = 0.5 * jnp.tanh(0.5 * pre_ref[rows, channels:]) + 0.5
+        log_keep = -soft_ref[...] * rates
+        resets = place_ref[rows, :] == 0
+        coeff = jnp.where(resets, 0.0, jnp.exp(log_keep))
+        squared = one_minus_exp(2.0 * log_keep)
+        scaling = jnp.where(resets, 1.0, squared * inverse_root(squared))
+        value = entries * conv_ref[rows, :] * scaling
+        for distance in (1, 2, 4):
+            reach = row_ids >= distance
+            value = value + coeff * jnp.where(reach, pltpu.roll(value, distance, 0), 0.0)
+            coeff = coeff * jnp.where(reach, pltpu.roll(coeff, distance, 0), 1.0)
+        value = value + coeff * carry[1]
+        coeff = coeff * carry[0]
+        rate_ref[rows, :] = rates
+        entry_ref[rows, :] = entries
+        local_ref[rows, :] = value
+        cum_ref[rows, :] = coeff
+        return coeff[7:8], value[7:8]
+
+    start = (jnp.ones((1, channels), f32), jnp.zeros((1, channels), f32))
+    coeff, value = lax.fori_loop(0, OWN // 8, scan, start, unroll=4)
+    edge_ref[pl.ds(slot, 1), :] = coeff
+    edge_ref[pl.ds(slot + MEMBERS, 1), :] = value
 
 
 def extended(pair, block):
@@ -369,76 +352,71 @@
     carry_ref,
     held_ref,
 ):
-    pieces = (piece0, piece1, piece2, piece3)
-    carries = slot_carries(False, spot_ref, pieces, prefix_ref, held_ref)
-    carry_ref[...] = jnp.concatenate(carries, axis=0)
+    slot = pl.program_id(0)
+
+    @pl.when(slot == 0)
+    def begin():
+        pieces = (piece0, piece1, piece2, piece3)
+        carries = slot_carries(False, spot_ref, pieces, prefix_ref, held_ref)
+        carry_ref[...] = jnp.concatenate(carries, axis=0)
+
+    carry = carry_ref[pl.ds(slot, 1), :]
 
     def apply(tile, token):
-        for slot in range(MEMBERS):
-            rows = rows_at(slot * OWN + tile * HALO, HALO)
-            states = local_ref[rows, :] + cum_ref[rows, :] * carry_ref[slot : slot + 1, :]
-            state_ref[rows, :] = states
-            mixed_ref[rows, :] = (states * gelu_parts(branch_ref[rows, :])[0]).astype(bf16)
+        rows = rows_at(tile * HALO, HALO)
+        states = local_ref[rows, :] + cum_ref[rows, :] * carry
+        state_ref[rows, :] = states
+        mixed_ref[rows, :] = (states * gelu_parts(branch_ref[rows, :])[0]).astype(bf16)
         return token
 
-    lax.fori_loop(0, OWN // HALO, apply, 0)
+    lax.fori_loop(0, OWN // HALO, apply, 0, unroll=2)
+
+
+def reverse_scan(rows, later, gated, grad_ref, rate_ref, place_ref, soft_ref, row_ids):
+    sgrad = grad_ref[rows, :] * gated
+    keeps = jnp.exp(-soft_ref[...] * rate_ref[rows, :])
+    coeff = jnp.where(place_ref[rows, :] == 0, 0.0, keeps)
+    value = coeff * sgrad
+    for distance in (1, 2, 4):
+        reach = row_ids < 8 - distance
+        value = value + coeff * jnp.where(reach, pltpu.roll(value, 8 - distance, 0), 0.0)
+        coeff = coeff * jnp.where(reach, pltpu.roll(coeff, 8 - distance, 0), 1.0)
+    return value + coeff * later, sgrad, coeff
 
 
 def local_backward_kernel(
+    soft_ref,
     grad_ref,
     branch_ref,
     state_ref,
     rate_ref,
     place_ref,
-    soft_ref,
     bgrad_ref,
-    sgrad_ref,
-    local_ref,
-    cum_ref,
     edge_ref,
 ):
+    slot = pl.program_id(0)
     channels = grad_ref.shape[1]
     row_ids = lax.broadcasted_iota(jnp.int32, (8, channels), 0)
 
     def scan(step, carry):
-        ends = []
-        for slot in range(MEMBERS):
-            pieces = {}
-            base = slot * OWN + OWN - HALO - step * HALO
-            cum, after = carry[2 * slot], carry[2 * slot + 1]
-            slopes = []
-            for part in (1, 0):
-                rows = rows_at(base + 8 * part, 8)
-                gated, slope = gelu_parts(branch_ref[rows, :])
-                gradient = grad_ref[rows, :]
-                slopes.append(slope * gradient * state_ref[rows, :])
-                sgrad = gradient * gated
-                keeps = jnp.where(
-                    place_ref[rows, :] == 0, 0.0, jnp.exp(-soft_ref[...] * rate_ref[rows, :])
-                )
-                coeff = keeps
-                value = keeps * sgrad
-                for distance in (1, 2, 4):
-                    reach = row_ids < 8 - distance
-                    value = value + coeff * jnp.where(
-                        reach, pltpu.roll(value, 8 - distance, 0), 0.0
-                    )
-                    coeff = coeff * jnp.where(reach, pltpu.roll(coeff, 8 - distance, 0), 1.0)
-                value = value + coeff * after
-                coeff = coeff * cum
-                sgrad_ref[rows, :] = sgrad
-                local_ref[rows, :] = value
-                cum_ref[rows, :] = coeff
-                cum, after = coeff[0:1], value[0:1]
-            bgrad_ref[rows_at(base, HALO), :] = jnp.concatenate(
-                [slopes[1], slopes[0]], axis=0
-            ).astype(bf16)
-            ends += [cum, after]
-        return tuple(ends)
-
-    start = (jnp.ones((1, channels), f32), jnp.zeros((1, channels), f32)) * MEMBERS
-    ends = lax.fori_loop(0, OWN // HALO, scan, start)
-    edge_ref[...] = jnp.concatenate(ends[0::2] + ends[1::2], axis=0)
+        base = OWN - HALO - step * HALO
+        cum, later = carry
+        slopes = []
+        for part in (1, 0):
+            rows = rows_at(base + 8 * part, 8)
+            gated, slope = gelu_parts(branch_ref[rows, :])
+            slopes.append(slope * grad_ref[rows, :] * state_ref[rows, :])
+            held, _, coeff = reverse_scan(
+                rows, later, gated, grad_ref, rate_ref, place_ref, soft_ref, row_ids
+            )
+            cum, later = coeff[0:1] * cum, held[0:1]
+        bgrad_ref[rows_at(base, HALO), :] = jnp.concatenate(slopes[::-1], axis=0).astype(bf16)
+        return cum, later
+
+    start = (jnp.ones((1, channels), f32), jnp.zeros((1, channels), f32))
+    coeff, value = lax.fori_loop(0, OWN // HALO, scan, start, unroll=2)
+    edge_ref[pl.ds(slot, 1), :] = coeff
+    edge_ref[pl.ds(slot + MEMBERS, 1), :] = value
 
 
 def finish_backward_kernel(
@@ -448,19 +426,19 @@
     piece2,
     piece3,
     prefix_ref,
-    sgrad_ref,
-    local_ref,
-    cum_ref,
+    carry_ref,
+    soft_ref,
+    taps_ref,
+    gates_ref,
+    grad_ref,
+    branch_ref,
     state_ref,
-    carry_ref,
     conv_ref,
     rate_ref,
     entry_ref,
     place_ref,
-    soft_ref,
     ci_ref,
-    taps_ref,
-    gates_ref,
+    halo_ref,
     pregrad_ref,
     igrad_ref,
     owed_ref,
@@ -469,119 +447,136 @@
     back_ref,
     held_ref,
 ):
+    slot = pl.program_id(0)
     channels = conv_ref.shape[1]
-    pieces = (piece0, piece1, piece2, piece3)
-    carries = slot_carries(True, spot_ref, pieces, prefix_ref, held_ref)
-    back_ref[...] = jnp.concatenate(carries, axis=0)
+
+    @pl.when(slot == 0)
+    def begin():
+        pieces = (piece0, piece1, piece2, piece3)
+        carries = slot_carries(True, spot_ref, pieces, prefix_ref, held_ref)
+        back_ref[...] = jnp.concatenate(carries, axis=0)
+        sums_ref[...] = jnp.zeros_like(sums_ref)
 
     row_ids = lax.broadcasted_iota(jnp.int32, (8, channels), 0)
+    back = back_ref[pl.ds(slot, 1), :]
+    ahead_first = carry_ref[pl.ds(slot, 1), :]
+
+    def gate_grads(step, carry):
+        later, logit_sum, rate_sum, entry_sum = carry
+        base = OWN - HALO - step * HALO
+        low_rate, low_entry = [], []
+        for part in (1, 0):
+            first = base + 8 * part
+            rows = rows_at(first, 8)
+            gated, _ = gelu_parts(branch_ref[rows, :])
+            held, sgrad, _ = reverse_scan(
+                rows, later, gated, grad_ref, rate_ref, place_ref, soft_ref, row_ids
+            )
+            adjoint = sgrad + jnp.where(row_ids == 7, later, pltpu.roll(held, 7, 0))
+            later = held[0:1]
+            ahead = state_ref[rows_at(jnp.maximum(first - 8, 0), 8), :][7:8]
+            ahead = jnp.where(first == 0, ahead_first, ahead)
+            previous = jnp.where(row_ids == 0, ahead, pltpu.roll(state_ref[rows, :], 1, 0))
+            rates, entries, conv = rate_ref[rows, :], entry_ref[rows, :], conv_ref[rows, :]
+            resets = place_ref[rows, :] == 0
+            log_keep = -soft_ref[...] * rates
+            squared = one_minus_exp(2.0 * log_keep)
+            inverse = inverse_root(squared)
+            scaling = jnp.where(resets, 1.0, squared * inverse)
+            turn = jnp.where(resets, 0.0, (1.0 - squared) * inverse)
+            weighed = adjoint * entries
+            log_grad = held * previous - weighed * conv * turn
+            rate_part = log_grad * rates
+            logit_sum = logit_sum + rate_part
+            rate_grad = -soft_ref[...] * rate_part * (1.0 - rates)
+            direct = weighed * scaling
+            entry_grad = direct * conv * (1.0 - entries)
+            rate_sum = rate_sum + rate_grad
+            entry_sum = entry_sum + entry_grad
+            cgrad_ref[rows, :] = direct
+            low_rate.append(rate_grad)
+            low_entry.append(entry_grad)
+        rows = rows_at(base, HALO)
+        pregrad_ref[rows, :channels] = jnp.concatenate(low_rate[::-1], axis=0).astype(bf16)
+        pregrad_ref[rows, channels:] = jnp.concatenate(low_entry[::-1], axis=0).astype(bf16)
+        return later, logit_sum, rate_sum, entry_sum
+
     zero = jnp.zeros((8, channels), f32)
-    logit_sum, rate_sum, entry_sum = zero, zero, zero
-    for slot in range(MEMBERS):
-
-        def gate_grads(step, carry):
-            later, logit_sum, rate_sum, entry_sum = carry
-            base = slot * OWN + OWN - HALO - step * HALO
-            low_rate, low_entry = [], []
-            for part in (1, 0):
-                first = base + 8 * part
-                rows = rows_at(first, 8)
-                held = local_ref[rows, :] + cum_ref[rows, :] * back_ref[slot : slot + 1, :]
-                following = jnp.where(row_ids == 7, later, pltpu.roll(held, 7, 0))
-                adjoint = sgrad_ref[rows, :] + following
-                later = held[0:1]
-                ahead = state_ref[rows_at(jnp.maximum(first - 8, 0), 8), :][7:8]
-                at_start = first == slot * OWN
-                ahead = jnp.where(at_start, carry_ref[slot : slot + 1, :], ahead)
-                previous = jnp.where(row_ids == 0, ahead, pltpu.roll(state_ref[rows, :], 1, 0))
-                rates, entries, conv = rate_ref[rows, :], entry_ref[rows, :], conv_ref[rows, :]
-                resets = place_ref[rows, :] == 0
-                log_keep = -soft_ref[...] * rates
-                squared = one_minus_exp(2.0 * log_keep)
-                inverse = inverse_root(squared)
-                scaling = jnp.where(resets, 1.0, squared * inverse)
-                turn = jnp.where(resets, 0.0, (1.0 - squared) * inverse)
-                weighed = adjoint * entries
-                log_grad = held * previous - weighed * conv * turn
-                rate_part = log_grad * rates
-                logit_sum = logit_sum + rate_part
-                rate_grad = -soft_ref[...] * rate_part * (1.0 - rates)
-                direct = weighed * scaling
-                entry_grad = direct * conv * (1.0 - entries)
-                rate_sum = rate_sum + rate_grad
-                entry_sum = entry_sum + entry_grad
-                cgrad_ref[rows, :] = direct
-                low_rate.append(rate_grad)
-                low_entry.append(entry_grad)
-            rows = rows_at(base, HALO)
-            pregrad_ref[rows, :channels] = jnp.concatenate(low_rate[::-1], axis=0).astype(bf16)
-            pregrad_ref[rows, channels:] = jnp.concatenate(low_entry[::-1], axis=0).astype(bf16)
-            return later, logit_sum, rate_sum, entry_sum
-
-        _, logit_sum, rate_sum, entry_sum = lax.fori_loop(
-            0,
-            OWN // HALO,
-            gate_grads,
-            (back_ref[slot : slot + 1, :], logit_sum, rate_sum, entry_sum),
-        )
-
-    def gate_back(step, carry):
-        columns = pl.ds(pl.multiple_of(step * 128, 128), 128)
+    _, logit_sum, rate_sum, entry_sum = lax.fori_loop(
+        0, OWN // HALO, gate_grads, (back, zero, zero, zero), unroll=2
+    )
+    for step in range(0, channels, 128):
+        columns = slice(step, step + 128)
         cgrad_ref[:, columns] += lax.dot_general(
             pregrad_ref[...],
             gates_ref[columns, :],
             (((1,), (1,)), ((), ())),
             preferred_element_type=f32,
         )
-        return carry
-
-    lax.fori_loop(0, channels // 128, gate_back, 0)
-
-    shift_sum = jnp.zeros((HALO, channels), f32)
-    tap_sums = [shift_sum] * CONV
-    for slot in range(MEMBERS):
-
-        def spread(rows, places):
-            return [rows] + [jnp.where(places >= tap, rows, 0.0) for tap in range(1, CONV)]
-
-        def shifted_sum(current, following):
-            total = taps_ref[0:1, :] * current[0]
-            for tap in range(1, CONV):
-                both = jnp.concatenate([current[tap], following[tap]], axis=0)
-                total = total + taps_ref[tap : tap + 1, :] * pltpu.roll(both, 2 * HALO - tap, 0)[:HALO]
-            return total
-
-        def conv_back(tile, carry):
-            shift_sum, tap_sums = carry
-            base = slot * OWN + tile * HALO
-            rows = rows_at(base, HALO)
-            after = jnp.minimum(base + HALO, slot * OWN + OWN - HALO)
-            next_rows = rows_at(after, HALO)
-            last = jnp.where(tile == OWN // HALO - 1, 0.0, 1.0)
-            grads = spread(cgrad_ref[rows, :], place_ref[rows, :])
-            coming = spread(cgrad_ref[next_rows, :] * last, place_ref[next_rows, :])
-            igrad_ref[rows, :] = shifted_sum(grads, coming)
-            inputs = conv_rows(ci_ref, slot, tile)
-            shift_sum = shift_sum + grads[0]
-            sums = [tap_sums[0] + grads[0] * inputs[HALO:]]
-            for tap in range(1, CONV):
-                sums.append(tap_sums[tap] + grads[tap] * pltpu.roll(inputs, tap, 0)[HALO:])
-            return shift_sum, sums
-
-        shift_sum, tap_sums = lax.fori_loop(0, OWN // HALO, conv_back, (shift_sum, tap_sums))
-        rows = rows_at(slot * OWN, HALO)
-        first = spread(cgrad_ref[rows, :], place_ref[rows, :])
-        owed_ref[slot * HALO : (slot + 1) * HALO, :] = shifted_sum(
-            [jnp.zeros((HALO, channels), f32)] * CONV, first
-        )
+
+    def spread(tile):
+        at = slice(tile * HALO, (tile + 1) * HALO)
+        rows, places = cgrad_ref[at, :], place_ref[at, :]
+        return [rows] + [jnp.where(places >= tap, rows, 0.0) for tap in range(1, CONV)]
+
+    def shifted_sum(current, following):
+        total = taps_ref[0:1, :] * current[0]
+        for tap in range(1, CONV):
+            both = jnp.concatenate([current[tap], following[tap]], axis=0)
+            total = total + taps_ref[tap : tap + 1, :] * pltpu.roll(both, 2 * HALO - tap, 0)[:HALO]
+        return total
+
+    nothing = [jnp.zeros((HALO, channels), f32)] * CONV
+    shift_sum, tap_sums = nothing[0], list(nothing)
+    tiles = OWN // HALO
+    coming = spread(0)
+    owed_ref[...] = shifted_sum(nothing, coming)
+    for tile in range(tiles):
+        grads, coming = coming, spread(tile + 1) if tile + 1 < tiles else nothing
+        igrad_ref[tile * HALO : (tile + 1) * HALO, :] = shifted_sum(grads, coming)
+        inputs = conv_rows(ci_ref, halo_ref, tile)
+        shift_sum = shift_sum + grads[0]
+        tap_sums[0] = tap_sums[0] + grads[0] * inputs[HALO:]
+        for tap in range(1, CONV):
+            tap_sums[tap] = tap_sums[tap] + grads[tap] * pltpu.roll(inputs, tap, 0)[HALO:]
 
     def total_rows(values):
         return jnp.sum(values, axis=0, keepdims=True)
 
-    sums_ref[...] = jnp.concatenate(
-        [total_rows(v) for v in [shift_sum, rate_sum, entry_sum, logit_sum] + list(tap_sums)],
-        axis=0,
-    )
+    sums_ref[...] += jnp.concatenate(
+        [total_rows(v) for v in [shift_sum, rate_sum, entry_sum, logit_sum] + tap_sums], axis=0
+    )
+
+
+def in_hbm(values):
+    return pltpu.with_memory_space_constraint(values, pltpu.HBM)
+
+
+def by_slot(kernel, outs, ins, scratch, scalars, moved, far_outs=None):
+    whole = [pl.BlockSpec(a.shape, lambda i, n=a.ndim: (0,) * n) for a in ins if not isinstance(a, tuple)]
+    parts = [
+        pl.BlockSpec((rows, a.shape[1]), lambda i, first=first: (first + i, 0))
+        for a, rows, first in (a for a in ins if isinstance(a, tuple))
+    ]
+    out_specs = [
+        pl.BlockSpec(shape, lambda i: (0, 0))
+        if rows is None
+        else pl.BlockSpec((rows, shape[1]), lambda i: (i, 0))
+        for rows, shape, _ in outs
+    ]
+    return pl.pallas_call(
+        kernel,
+        grid=(MEMBERS,),
+        in_specs=[pl.BlockSpec(memory_space=pltpu.SMEM)] * len(scalars) + whole + parts,
+        out_specs=out_specs,
+        out_shape=[
+            pltpu.HBM(shape, dtype) if far else jax.ShapeDtypeStruct(shape, dtype)
+            for (_, shape, dtype), far in zip(outs, far_outs or [False] * len(outs))
+        ],
+        scratch_shapes=[pltpu.VMEM(shape, dtype) for shape, dtype in scratch],
+        compiler_params=pltpu.CompilerParams(vmem_limit_bytes=16 * 1024 * 1024),
+        cost_estimate=pl.CostEstimate(flops=0, bytes_accessed=moved, transcendentals=0),
+    )(*scalars, *[a[0] if isinstance(a, tuple) else a for a in ins])
 
 
 def in_vmem(kernel, outs, scratch=(), scalars=0, count=1, moved=0):
@@ -593,7 +588,7 @@
         in_specs=[smem] * scalars + [vmem] * count,
         out_specs=[vmem] * len(outs),
         scratch_shapes=[pltpu.VMEM(shape, dtype) for shape, dtype in scratch],
-        compiler_params=pltpu.CompilerParams(vmem_limit_bytes=40 * 1024 * 1024),
+        compiler_params=pltpu.CompilerParams(vmem_limit_bytes=16 * 1024 * 1024),
         cost_estimate=pl.CostEstimate(flops=0, bytes_accessed=moved, transcendentals=0),
     )
 
@@ -641,7 +636,7 @@
         ],
         out_specs=pl.BlockSpec((height, columns), lambda j, i: (i, j)),
         out_shape=jax.ShapeDtypeStruct((features, 3 * columns), bf16),
-        compiler_params=pltpu.CompilerParams(vmem_limit_bytes=40 * 1024 * 1024),
+        compiler_params=pltpu.CompilerParams(vmem_limit_bytes=32 * 1024 * 1024),
         cost_estimate=pl.CostEstimate(
             flops=6 * rows * features * columns,
             bytes_accessed=6 * features * columns,
@@ -674,11 +669,12 @@
         out_ref[tok] = jnp.concatenate(pieces, axis=0).astype(bf16)
 
 
-def halves_kernel(count, spot_ref, small_ref, *refs):
+def halves_kernel(count, small, spot_ref, *refs):
     core = spot_ref[3]
+    small_ref, refs = (refs[0], refs[1:]) if small else (None, refs)
     mine_ref, theirs_ref = refs[2 * count :]
     chips, rows, _ = mine_ref.shape
-    rows = (rows - SMALL) // count
+    rows = (rows - small) // count
     for which in range(count):
         sums = lax.dot_general(
             refs[which][...],
@@ -692,9 +688,9 @@
             at = slice(which * rows, (which + 1) * rows)
             mine_ref[chip, at, :] = jnp.where(core == 0, low, high).astype(bf16)
             theirs_ref[chip, at, :] = jnp.where(core == 0, high, low).astype(bf16)
-    for chip in range(chips):
+    for chip in range(chips if small else 0):
         low, high = small_ref[2 * chip].astype(f32), small_ref[2 * chip + 1].astype(f32)
-        at = slice(count * rows, count * rows + SMALL)
+        at = slice(count * rows, count * rows + small)
         mine_ref[chip, at, :] = jnp.where(core == 0, low, high).astype(bf16)
         theirs_ref[chip, at, :] = jnp.where(core == 0, high, low).astype(bf16)
 
@@ -705,25 +701,26 @@
     rows, columns = rhs[0].shape
     height = 1024
     chips = height // 128
-    total = 64 * count + SMALL
+    extra = SMALL if small is not None else 0
+    total = 64 * count + extra
     shape = jax.ShapeDtypeStruct((features // 128, total, columns), bf16)
     out_spec = pl.BlockSpec((chips, total, columns), lambda i: (i, 0, 0))
     return pl.pallas_call(
-        functools.partial(halves_kernel, count),
+        functools.partial(halves_kernel, count, extra),
         grid=(features // height,),
         in_specs=[pl.BlockSpec(memory_space=pltpu.SMEM)]
-        + [pl.BlockSpec((2 * chips, SMALL, columns), lambda i: (i, 0, 0))]
+        + [pl.BlockSpec((2 * chips, SMALL, columns), lambda i: (i, 0, 0))] * (extra > 0)
         + [pl.BlockSpec((rows, height), lambda i: (0, i))] * count
         + [pl.BlockSpec((rows, columns), lambda i: (0, 0))] * count,
         out_specs=[out_spec] * 2,
         out_shape=[shape] * 2,
-        compiler_params=pltpu.CompilerParams(vmem_limit_bytes=40 * 1024 * 1024),
+        compiler_params=pltpu.CompilerParams(vmem_limit_bytes=28 * 1024 * 1024),
         cost_estimate=pl.CostEstimate(
             flops=2 * count * rows * features * columns,
-            bytes_accessed=20_000_000,
+            bytes_accessed=0,
             transcendentals=0,
         ),
-    )(spots, small, *lhs, *rhs)
+    )(spots, *([small] if extra else []), *lhs, *rhs)
 
 
 def per_device(
@@ -813,26 +810,40 @@
 
     conv_input = product(wide_one, input_all, bf16)
     branch = product(own_one, branch_all)
-    state_shape = ((total_rows, channels), f32)
-    conv, rates, entries, local, cum, edges, gates = in_vmem(
+    halo_first = total_rows // HALO
+    conv, rates, entries, local, cum, edges, gates = by_slot(
         local_forward_kernel,
-        [state_shape] * 5 + [((8, channels), f32), ((channels, 2 * channels), bf16)],
+        [(OWN, (total_rows, channels), f32)] * 5
+        + [(None, (8, channels), f32), (None, (channels, 2 * channels), bf16)],
         [
-            ((total_rows, 2 * channels), f32),
-            ((total_rows, channels), bf16),
+            taps,
+            shift,
+            blocks,
+            bias,
+            soft,
+            (conv_input, OWN, 0),
+            (conv_input, HALO, halo_first),
+            (places, OWN, 0),
         ],
-        count=7,
-        moved=30_000_000,
-    )(conv_input, places, taps, shift, blocks, bias, soft)
+        [((OWN, 2 * channels), f32), ((OWN, channels), bf16)],
+        (),
+        30_000_000,
+        [True, True, True, False, False, False, True],
+    )
+    conv, rates, entries, gates = [in_hbm(a) for a in (conv, rates, entries, gates)]
     chains, _ = exchange_edges(edges, spots, False)
-    states, mixture, carried = in_vmem(
+    states, mixture, carried = by_slot(
         mix_kernel,
-        [state_shape, ((total_rows, channels), bf16), ((MEMBERS, channels), f32)],
+        [
+            (OWN, (total_rows, channels), f32),
+            (OWN, (total_rows, channels), bf16),
+            (None, (MEMBERS, channels), f32),
+        ],
+        [*chains] + [(a, OWN, 0) for a in (local, cum, branch)],
         [((4, 8, channels), f32)],
-        scalars=1,
-        count=8,
-        moved=4_500_000,
-    )(spots, *chains, local, cum, branch)
+        (spots,),
+        4_500_000,
+    )
 
     def rows_of(values):
         return [values[j * OWN : (j + 1) * OWN] for j in range(MEMBERS)]
@@ -843,7 +854,7 @@
     factor_two = norm_factor(middle)
     normed_two = (middle * factor_two * feed_gain).astype(bf16)
     hidden_grad = product(after(cotangent_all, mixture), down_turned)
-    blocks_two = ring_gather(normed_two, spot[2])
+    blocks_two = ring_gather(normed_two, spot[2], (feed_all,))
     blocks_two[2] = after(blocks_two[2], hidden_grad)
     wide_two = jnp.concatenate(blocks_two, axis=0)
     gate_up = product(wide_two, gate_up_all)
@@ -852,64 +863,48 @@
     hidden = (gate_act * up_pre).astype(bf16)
     gate_grad = (gate_slope * hidden_grad * up_pre).astype(bf16)
     up_grad = (gate_act * hidden_grad).astype(bf16)
-    both_grads = jnp.concatenate([gate_grad, up_grad], axis=1)
-    two_shares = product_back(both_grads, gate_up_all)
+    feed_shares = feed_outer(wide_two, cotangent_all, (gate_grad, up_grad, hidden))
+    feed_grads = lax.psum_scatter(feed_shares, "tok", scatter_dimension=0, tiled=True)
+    gate_late, up_late = after((gate_grad, up_grad), feed_shares)
+    two_shares = product_back(jnp.concatenate([gate_late, up_late], axis=1), gate_up_all)
     two_parts = rows_of(two_shares)
     two_far, two_near = ring_open(two_parts, spot[2])
     two_grad = ring_close(two_parts, two_near, ring_pass(two_parts, two_far, spot[2]))
     middle_grad = cotangent.astype(f32) + normalize_back(two_grad, middle, factor_two, feed_gain)
     grad_feed_scale = jnp.sum(two_grad * middle * factor_two, axis=0)
-    feed_shares = feed_outer(
-        wide_two, cotangent_all, after((gate_grad, up_grad, hidden), two_shares)
-    )
-    feed_grads = lax.psum_scatter(
-        after(feed_shares, two_grad), "tok", scatter_dimension=0, tiled=True
-    )
-
     layer_shares = product_back(after(hidden, two_far), down_turned, bf16)
     middle_blocks = ring_gather(middle_grad.astype(bf16), spot[2])
     middle_blocks[2] = after(middle_blocks[2], layer_shares)
     middle_wide = jnp.concatenate(middle_blocks, axis=0)
     mixture_grad = product(middle_wide, out_turned)
-    branch_grad, sgrad, local_back, cum_back, back_edges = in_vmem(
+    branch = in_hbm(branch)
+    branch_grad, back_edges = by_slot(
         local_backward_kernel,
-        [((total_rows, channels), bf16)] + [state_shape] * 3 + [((8, channels), f32)],
-        count=6,
-        moved=9_500_000,
-    )(mixture_grad, branch, states, rates, places, soft)
+        [(OWN, (total_rows, channels), bf16), (None, (8, channels), f32)],
+        [soft] + [(a, OWN, 0) for a in (mixture_grad, branch, states, rates, places)],
+        (),
+        (),
+        9_500_000,
+    )
     chains_back, near_back = exchange_edges(back_edges, spots, True)
-    pregrads, igrad, owed, sums = in_vmem(
+    pregrads, igrad, owed, sums = by_slot(
         finish_backward_kernel,
         [
-            ((total_rows, 2 * channels), bf16),
-            state_shape,
-            ((MEMBERS * HALO, channels), f32),
-            ((8, channels), f32),
+            (OWN, (total_rows, 2 * channels), bf16),
+            (OWN, (total_rows, channels), f32),
+            (HALO, (MEMBERS * HALO, channels), f32),
+            (None, (8, channels), f32),
         ],
+        [*chains_back, carried, soft, taps, gates]
+        + [(a, OWN, 0) for a in (mixture_grad, branch, states, conv, rates, entries)]
+        + [(places, OWN, 0), (conv_input, OWN, 0), (conv_input, HALO, halo_first)],
         [
-            ((total_rows, channels), f32),
+            ((OWN, channels), f32),
             ((MEMBERS, channels), f32),
             ((4, 8, channels), f32),
         ],
-        scalars=1,
-        count=18,
-        moved=40_000_000,
-    )(
-        spots,
-        *chains_back,
-        sgrad,
-        local_back,
-        cum_back,
-        states,
-        carried,
-        conv,
-        rates,
-        entries,
-        places,
-        soft,
-        conv_input,
-        taps,
-        gates,
+        (spots,),
+        40_000_000,
     )
     returned = lax.ppermute(
         owed.reshape(MEMBERS, HALO, channels)[:, HALO - 3 :],
@@ -939,12 +934,14 @@
     weight_other = hop(weight_theirs, "core", 1)
     late = after(input_low, weight_theirs)
     one_shares = product_back(jnp.concatenate([late, branch_grad], axis=1), project_all, bf16)
+    weight_chip = narrow_sum(weight_mine, weight_other)
+    one_shares = after(one_shares, weight_chip)
     one_parts = rows_of(one_shares)
     one_grad = ring_scatter(one_parts, core)
     factor_one = norm_factor(own_values)
     first_grad = normalize_back(one_grad, own_values, factor_one, mix_gain)
     inputs_grad = (middle_grad + first_grad).astype(bf16)
-    settled = chips_sum(narrow_sum(weight_mine, weight_other))
+    settled = chips_sum(weight_chip)
     layer_out = middle + ring_scatter(rows_of(after(layer_shares, one_grad)), core)
     grad_out, grad_branch, grad_input = [
         settled[i * slice_rows : (i + 1) * slice_rows] for i in range(3)

time: 418 us -> 413 us (0.988)
  the two profiles are of different devices: /device:TPU:68 before, /device:TPU:80 now
where the time goes in v1:
time: 413 us; the launch traced here: 405 us
  waiting for transfers between devices  160 us (39%)
  starting transfers between devices  70.2 us (17%)
  matrix products  49.1 us (12%)
  other arithmetic  47.4 us (11%)
  Pallas kernels  46.7 us (11%)
  local copies, waits for them, and re-layouts  16.3 us (4%)
  between operations  15.4 us (4%)
    ppermute x24, waiting for transfers between devices, hop_apart(): return lax.ppermute(values, ('blk', 'tok'), route)  106 us
    ppermute x24, starting transfers between devices, hop_apart(): return lax.ppermute(values, ('blk', 'tok'), route)  28.6 us
    ppermute x22, waiting for transfers between devices, hop_tok(): return lax.ppermute(values, 'tok', route)  27.6 us
    ppermute x22, starting transfers between devices, hop_tok(): return lax.ppermute(values, 'tok', route)  27.1 us
    dot_general x5, matrix products, product(): return jnp.dot(operand, weight, preferred_element_type=f32).astype(out)  25.3 us
    dot_general x4, matrix products, product_back(): lax.dot_general(operand, weight, (((1,), (1,)), ((), ())), preferred_elem...  23.7 us
    pallas_call x4, Pallas kernels, by_slot(): pl.pallas_call(kernel, grid=(MEMBERS,), in_specs=[pl.BlockSpec(memory_spa...  23.2 us
    all_to_all x1, waiting for transfers between devices, chips_sum(): lax.all_to_all(values, 'tok', 0, 0, axis_index_groups=cores, tiled=True)  21.5 us
  transfers between devices with their start and end apart: 58, of which 35 were waited for; matrix products, arithmetic and copies ran while one was open for 22% of the time, Pallas kernels for 8%

profile of v1, /device:TPU:80, one launch (start us, length us, event | category | flops | bytes accessed | tf_op | source)
XLA Modules:
  0.0 405.0 jit_solution(12573915662008082188)
XLA Ops:
  9.0 2.8 collective-permute-start.4
  15.1 2.0 pad_maximum_fusion.4
  26.7 2.0 collective-permute-done.12
  31.2 4.8 %collective-permute-done.9 = bf16[128,2048]{1,0:T(8,128)(2,1)S(1)} collective-permute-done((bf16[128,2048]{1,0:T(8,128)(2,1)S(1)}, bf16[128,2048]{1,0:T(8,128)(2,1)S(1)}, u32[]{:S(2)}, u32[]{:S(2)}) %collective-permute-start.9) | collective-permute-done | bytes 524320 | tf_op jit(solution)/shard_map/ppermute | solution.py:60
  40.3 4.4 %collective-permute-done.8 = bf16[4,2,16,640]{3,2,1,0:T(8,128)(2,1)S(1)} collective-permute-done((bf16[4,2,16,640]{3,2,1,0:T(8,128)(2,1)S(1)}, bf16[4,2,16,640]{3,2,1,0:T(8,128)(2,1)S(1)}, u32[]{:S(2)}, u32[]{:S(2)}) %collective-permute-start.8) | collective-permute-done | bytes 163872 | tf_op jit(solution)/shard_map/ppermute | solution.py:42
  44.7 2.4 collective-permute-done.7
  47.1 3.9 collective-permute-done.6
  53.4 2.3 fusion.12.refs_2_.refs_3_
  55.7 8.4 %collective-permute-done.11 = bf16[128,2048]{1,0:T(8,128)(2,1)} collective-permute-done((bf16[128,2048]{1,0:T(8,128)(2,1)}, bf16[128,2048]{1,0:T(8,128)(2,1)}, u32[]{:S(2)}, u32[]{:S(2)}) %collective-permute-start.11) | collective-permute-done | bytes 524320 | tf_op jit(solution)/shard_map/ppermute | solution.py:60
  66.4 3.9 fusion.32.ci_ref.halo_ref
  70.3 7.5 %shard_map.305 = (f32[512,640]{1,0:T(8,128)}, f32[512,640]{1,0:T(8,128)}, f32[512,640]{1,0:T(8,128)}, f32[512,640]{1,0:T(8,128)S(1)}, f32[512,640]{1,0:T(8,128)S...) custom-call(f32[4,640]{1,0:T(4,128)S(1)} %slice.203.taps_ref, f32[1,640]{1,0:T(1,128)S(1)} %slice.205.shift_ref, ...), custom_call_target="tpu_custom_call" | custom-call | bytes 30000000 | tf_op jit(solution)/shard_map/pallas_call | solution.py:567
  79.2 3.2 collective-permute-start.18
  82.4 2.6 collective-permute-start.19
  85.4 1.9 collective-permute-done.19.refs_3_
  88.8 3.7 collective-permute-start.21
  94.4 1.9 collective-permute-done.22.piece3
  99.8 3.2 collective-permute-start.23
  103.1 10.7 %collective-permute-done.24 = bf16[128,2048]{1,0:T(8,128)(2,1)S(1)} collective-permute-done((bf16[128,2048]{1,0:T(8,128)(2,1)S(1)}, bf16[128,2048]{1,0:T(8,128)(2,1)S(1)}, u32[]{:S(2)}, u32[]{:S(2)}) %collective-permute-start.24) | collective-permute-done | bytes 524320 | tf_op jit(solution)/shard_map/ppermute | solution.py:60
  114.8 3.2 collective-permute-start.29
  118.9 9.2 %collective-permute-done.25 = bf16[128,2048]{1,0:T(8,128)(2,1)} collective-permute-done((bf16[128,2048]{1,0:T(8,128)(2,1)}, bf16[128,2048]{1,0:T(8,128)(2,1)}, u32[]{:S(2)}, u32[]{:S(2)}) %collective-permute-start.25) | collective-permute-done | bytes 524320 | tf_op jit(solution)/shard_map/ppermute | solution.py:60
  128.1 2.3 multiply_reduce_fusion.2
  130.7 2.0 collective-permute-start.27
  134.0 2.8 pad_maximum_fusion.lhs_two
  136.8 3.0 collective-permute-done.26
  143.0 2.4 all-gather.5.cloned.1.call-done
  147.0 6.2 %fusion.6 = f32[512,1536]{1,0:T(8,128)S(1)} fusion(bf16[512,2048]{1,0:T(8,128)(2,1)} %pad_maximum_fusion.lhs_two, bf16[2048,4608]{1,0:T(8,128)(2,1)} %all-gather.5.cloned.1.call-done), kind=kOutput, calls=%fused_computation.10 | convolution fusion | flops 3221225472 | bytes 11534336 | tf_op jit(solution)/shard_map/dot_general | solution.py:152
  153.2 3.0 collective-permute-done.28
  156.4 9.7 %fusion.2 = f32[512,3072]{1,0:T(8,128)S(1)} fusion(bf16[2048,4608]{1,0:T(8,128)(2,1)} %all-gather.5.cloned.1.call-done, bf16[128,2048]{1,0:T(8,128)(2,1)S(1)} %copy-done.30, bf16[128,2048]{1,0:T(8,128)(2,1)S(1)} %collective-permute-done.28, bf16[128,2048]{1,0:T(8,128)(2,1)S(1)} %copy-done.29, bf16[128,2048]{1,0:T(8,128)(2,1)S(1)} %copy-done.32), kind=kOutput, calls=%fused_computation.2 | convolution fusion | flops 6450839552 | bytes 20971520 | tf_op jit(solution)/shard_map/dot_general | solution.py:152
  166.1 2.6 multiply_convert_fusion
  168.7 13.5 %shard_map.308 = bf16[2048,4608]{1,0:T(8,128)(2,1)} custom-call(bf16[512,2048]{1,0:T(8,128)(2,1)S(1)} %pad_maximum_fusion.1.lhs_one, bf16[512,2048]{1,0:T(8,128)(2,1)S(1)} %copy-done.6, bf16[512,1536]{1,0:T(8,128)(2,1)S(1)} %get-tuple-element.68.rhs_one, bf16[512,1536]{1,0:T(8,128)(2,1)S(1)} %get-tuple-element.69.rhs_two, ...), custom_call_target="tpu_custom_call" | custom-call | flops 9663676416 | bytes 18874368 | tf_op jit(solution)/shard_map/pallas_call | solution.py:627
  185.8 10.7 %fusion = f32[512,2048]{1,0:T(8,128)S(1)} fusion(bf16[2048,4608]{1,0:T(8,128)(2,1)} %all-gather.5.cloned.1.call-done, bf16[512,1536]{1,0:T(8,128)(2,1)} %copy-done.10, bf16[512,1536]{1,0:T(8,128)(2,1)} %copy-done.11), kind=kOutput, calls=%fused_computation | convolution fusion | flops 6448742400 | bytes 19922944 | tf_op jit(solution)/shard_map/dot_general | solution.py:156
  197.2 3.0 collective-permute-start.31
  200.2 12.3 %collective-permute-done.30 = bf16[128,2048]{1,0:T(8,128)(2,1)S(1)} collective-permute-done((bf16[128,2048]{1,0:T(8,128)(2,1)S(1)}, bf16[128,2048]{1,0:T(8,128)(2,1)S(1)}, u32[]{:S(2)}, u32[]{:S(2)}) %collective-permute-start.30) | collective-permute-done | bytes 524320 | tf_op jit(solution)/shard_map/ppermute | solution.py:60
  212.8 10.4 %collective-permute-done.32 = bf16[128,2048]{1,0:T(8,128)(2,1)S(1)} collective-permute-done((bf16[128,2048]{1,0:T(8,128)(2,1)S(1)}, bf16[128,2048]{1,0:T(8,128)(2,1)S(1)}, u32[]{:S(2)}, u32[]{:S(2)}) %collective-permute-start.32) | collective-permute-done | bytes 524320 | tf_op jit(solution)/shard_map/ppermute | solution.py:60
  223.7 2.7 fusion.69
  226.4 3.2 collective-permute-start.33
  229.6 9.3 %collective-permute-done.34 = bf16[128,2048]{1,0:T(8,128)(2,1)S(1)} collective-permute-done((bf16[128,2048]{1,0:T(8,128)(2,1)S(1)}, bf16[128,2048]{1,0:T(8,128)(2,1)S(1)}, u32[]{:S(2)}, u32[]{:S(2)}) %collective-permute-start.34) | collective-permute-done | bytes 524320 | tf_op jit(solution)/shard_map/ppermute | solution.py:60
  239.0 8.1 %fusion.20 = bf16[512,2048]{1,0:T(8,128)(2,1)} fusion(bf16[512,1536]{1,0:T(8,128)(2,1)S(1)} %copy-done.9, bf16[2048,4608]{1,0:T(8,128)(2,1)} %all-gather.5.cloned.1.call-done), kind=kOutput, calls=%fused_computation.27 | convolution fusion | flops 3222274048 | bytes 9961472 | tf_op jit(solution)/shard_map/dot_general | solution.py:156
  247.1 2.2 collective-permute-done.35
  249.4 3.8 fusion.27.grad_ref
  253.2 4.1 %shard_map.309 = (bf16[512,640]{1,0:T(8,128)(2,1)S(1)}, f32[8,640]{1,0:T(8,128)S(1)}) custom-call(f32[1,640]{1,0:T(1,128)S(1)} %fusion.58.soft_ref, f32[512,640]{1,0:T(8,128)S(1)} %fusion.27.grad_ref, f32[512,640]{1,0:T(8,128)} %copy-done, f32[512,640]{1,0:T(8,128)S(1)} %get-tuple-element.72.state_ref, f32[512,640]{1,0:T(8,128)} %get-tuple-element.73.rate_ref, ...), custom_call_target="tpu_custom_call" | custom-call | bytes 9500000 | tf_op jit(solution)/shard_map/pallas_call | solution.py:567
  260.1 2.2 collective-permute-start.38
  262.4 1.9 collective-permute-start.39
  264.4 2.4 collective-permute-done.38.refs_2_
  268.8 2.7 collective-permute-start.41
  276.9 10.1 %shard_map.311 = (bf16[512,1280]{1,0:T(8,128)(2,1)S(1)}, f32[512,640]{1,0:T(8,128)S(1)}, f32[64,640]{1,0:T(8,128)S(1)}, f32[8,640]{1,0:T(8,128)S(1)}) custom-call(s32[4]{0:T(128)S(1)} %pad_add_fusion.spot_ref, f32[8,640]{1,0:T(8,128)S(1)} %get-tuple-element.75.piece0, f32[8,640]{1,0:T(8,128)S(1)} %collective-permute-done.40.piece1, ...), custom_call_target="tpu_custom_call" | custom-call | bytes 40000000 | tf_op jit(solution)/shard_map/pallas_call | solution.py:567
  287.7 2.6 shard_map.312.refs_0_
  290.4 6.2 %shard_map.313 = (bf16[16,216,640]{2,1,0:T(8,128)(2,1)S(1)}, bf16[16,216,640]{2,1,0:T(8,128)(2,1)S(1)}) custom-call(s32[4]{0:T(128)S(1)} %pad_add_fusion.spot_ref, bf16[32,24,640]{2,1,0:T(8,128)(2,1)S(1)} %shard_map.312.refs_0_, bf16[512,2048]{1,0:T(8,128)(2,1)S(1)} %pad_maximum_fusion.2.refs_1_, bf16[576,2048]{1,0:T(8,128)(2,1)S(1)} %copy-done.5, ...), custom_call_target="tpu_custom_call" | custom-call | flops 4026531840 | tf_op jit(solution)/shard_map/pallas_call | solution.py:708
  297.4 3.1 fusion.17
  300.5 4.0 collective-permute-done.44
  304.5 3.4 add_convert_fusion
  308.1 9.1 %all-to-all-start = ((bf16[16,216,640]{2,1,0:T(8,128)(2,1)}), bf16[16,216,640]{2,1,0:T(8,128)(2,1)}, u32[]{:S(2)}, u32[]{:S(2)}) async-start(bf16[16,216,640]{2,1,0:T(8,128)(2,1)} %add_convert_fusion), calls=%async_computation | async-start | bytes 8847360 | tf_op jit(solution)/shard_map/all_to_all | solution.py:137
  317.2 3.1 collective-permute-start.45
  321.9 9.2 %collective-permute-done.45 = bf16[128,2048]{1,0:T(8,128)(2,1)S(1)} collective-permute-done((bf16[128,2048]{1,0:T(8,128)(2,1)S(1)}, bf16[128,2048]{1,0:T(8,128)(2,1)S(1)}, u32[]{:S(2)}, u32[]{:S(2)}) %collective-permute-start.45) | collective-permute-done | bytes 524320 | tf_op jit(solution)/shard_map/ppermute | solution.py:60
  331.1 2.2 collective-permute-done.47
  335.9 3.2 collective-permute-start.48
  339.2 10.9 %collective-permute-done.49 = bf16[128,2048]{1,0:T(8,128)(2,1)S(1)} collective-permute-done((bf16[128,2048]{1,0:T(8,128)(2,1)}, bf16[128,2048]{1,0:T(8,128)(2,1)S(1)}, u32[]{:S(2)}, u32[]{:S(2)}) %collective-permute-start.49) | collective-permute-done | bytes 524320 | tf_op jit(solution)/shard_map/ppermute | solution.py:60
  351.6 2.5 fusion.42
  354.1 7.9 %collective-permute-done.50 = bf16[128,2048]{1,0:T(8,128)(2,1)S(1)} collective-permute-done((bf16[128,2048]{1,0:T(8,128)(2,1)S(1)}, bf16[128,2048]{1,0:T(8,128)(2,1)S(1)}, u32[]{:S(2)}, u32[]{:S(2)}) %collective-permute-start.50) | collective-permute-done | bytes 524320 | tf_op jit(solution)/shard_map/ppermute | solution.py:60
  362.0 2.1 add_convert_fusion.2
  364.1 21.5 %all-to-all-done = bf16[16,216,640]{2,1,0:T(8,128)(2,1)} async-done(((bf16[16,216,640]{2,1,0:T(8,128)(2,1)}), bf16[16,216,640]{2,1,0:T(8,128)(2,1)}, u32[]{:S(2)}, u32[]{:S(2)}) %all-to-all-start) | async-done | bytes 4423712 | tf_op jit(solution)/shard_map/all_to_all | solution.py:137
  385.6 3.0 convert_reduce_fusion
  389.8 2.0 collective-permute-start.51
  395.9 2.1 convert_bitcast_fusion
  (275 shorter events, 70.6 us)
Async XLA Ops:
  7.2 59.2 %all-gather.3.cloned.1.call-start = ((), (), s32[]{:S(2)}) async-start(), calls=%async_computation.2 | async-start | bytes 8110080 | tf_op jit(solution)/shard_map/all_gather | solution.py:769
  8.9 136.5 %all-gather.5.cloned.1.call-start = ((), (), s32[]{:S(2)}) async-start(), calls=%async_computation.3 | async-start | bytes 19464192 | tf_op jit(solution)/shard_map/all_gather | solution.py:794
  9.0 22.1 %collective-permute-start.4 = (bf16[128,2048]{1,0:T(8,128)(2,1)}, bf16[128,2048]{1,0:T(8,128)(2,1)S(1)}, u32[]{:S(2)}, u32[]{:S(2)}) collective-permute-start(bf16[128,2048]{1,0:T(8,128)(2,1)} %param.18), channel_id=1, source_target_pairs={{0,96},{1,33},{2,98},{3,35},{4,100},{5,37},{6,102},{7,39},{8,104},... | collective-permute-start | bytes 1572872 | tf_op jit(solution)/shard_map/ppermute | solution.py:60
  11.8 12.3 %collective-permute-start.5 = (bf16[128,2048]{1,0:T(8,128)(2,1)}, bf16[128,2048]{1,0:T(8,128)(2,1)S(1)}, u32[]{:S(2)}, u32[]{:S(2)}) collective-permute-start(bf16[128,2048]{1,0:T(8,128)(2,1)} %param.18), channel_id=1, source_target_pairs={{0,32},{1,97},{2,34},{3,99},{4,36},{5,101},{6,38},{7,103},{8,40},{... | collective-permute-start | bytes 1572872 | tf_op jit(solution)/shard_map/ppermute | solution.py:60
  15.0 2.1 collective-permute-start
  17.8 6.4 %collective-permute-start.3 = (bf16[2,16,640]{2,1,0:T(8,128)(2,1)}, bf16[2,16,640]{2,1,0:T(8,128)(2,1)S(1)}, u32[]{:S(2)}, u32[]{:S(2)}) collective-permute-start(bf16[2,16,640]{2,1,0:T(8,128)(2,1)} %get-tuple-element.137), channel_id=1, source_target_pairs={{0,2},{1,3},{2,4},{3,5},{4,6},{5,7},{6,0},{7,1},{8,10},{9,11},{10,... | collective-permute-start | bytes 122888 | tf_op jit(solution)/shard_map/ppermute | solution.py:42
  19.4 6.5 %collective-permute-start.2 = (bf16[2,16,640]{2,1,0:T(8,128)(2,1)}, bf16[2,16,640]{2,1,0:T(8,128)(2,1)}, u32[]{:S(2)}, u32[]{:S(2)}) collective-permute-start(bf16[2,16,640]{2,1,0:T(8,128)(2,1)} %get-tuple-element.137), channel_id=1, source_target_pairs={{0,4},{1,5},{2,6},{3,7},{4,0},{5,1},{6,2},{7,3},{8,12},{9,13},{10,... | collective-permute-start | bytes 122888 | tf_op jit(solution)/shard_map/ppermute | solution.py:42
  19.4 6.5 %collective-permute-start.1 = (bf16[2,16,640]{2,1,0:T(8,128)(2,1)}, bf16[2,16,640]{2,1,0:T(8,128)(2,1)}, u32[]{:S(2)}, u32[]{:S(2)}) collective-permute-start(bf16[2,16,640]{2,1,0:T(8,128)(2,1)} %get-tuple-element.137), channel_id=1, source_target_pairs={{0,6},{1,7},{2,0},{3,1},{4,2},{5,3},{6,4},{7,5},{8,14},{9,15},{10,... | collective-permute-start | bytes 122888 | tf_op jit(solution)/shard_map/ppermute | solution.py:42
  24.1 4.5 %collective-permute-start.12 = (bf16[16,2048]{1,0:T(8,128)(2,1)S(1)}, bf16[16,2048]{1,0:T(8,128)(2,1)S(1)}, u32[]{:S(2)}, u32[]{:S(2)}) collective-permute-start(bf16[16,2048]{1,0:T(8,128)(2,1)S(1)} %slice.213), channel_id=1, source_target_pairs={{0,1},{1,2},{2,3},{3,4},{4,5},{5,6},{6,7},{7,8},{8,9},{9,10},{10,1... | collective-permute-start | bytes 196616 | tf_op jit(solution)/shard_map/ppermute | solution.py:773
  24.2 11.8 %collective-permute-start.9 = (bf16[128,2048]{1,0:T(8,128)(2,1)S(1)}, bf16[128,2048]{1,0:T(8,128)(2,1)S(1)}, u32[]{:S(2)}, u32[]{:S(2)}) collective-permute-start(bf16[128,2048]{1,0:T(8,128)(2,1)S(1)} %collective-permute-done.5), channel_id=1, source_target_pairs={{0,32},{1,97},{2,34},{3,99},{4,36},{5,101},{6,38},{7,103},{8,40},{... | collective-permute-start | bytes 1572872 | tf_op jit(solution)/shard_map/ppermute | solution.py:60
  28.7 9.5 %collective-permute-start.13 = (bf16[16,2048]{1,0:T(8,128)(2,1)S(1)}, bf16[16,2048]{1,0:T(8,128)(2,1)S(1)}, u32[]{:S(2)}, u32[]{:S(2)}) collective-permute-start(bf16[16,2048]{1,0:T(8,128)(2,1)S(1)} %collective-permute-done.12), channel_id=1, source_target_pairs={{0,96},{32,0},{64,32},{96,64},{1,97},{33,1},{65,33},{97,65},{2,98}... | collective-permute-start | bytes 196616 | tf_op jit(solution)/shard_map/ppermute | solution.py:25
  30.1 9.1 %collective-permute-start.14 = (bf16[16,2048]{1,0:T(8,128)(2,1)S(1)}, bf16[16,2048]{1,0:T(8,128)(2,1)S(1)}, u32[]{:S(2)}, u32[]{:S(2)}) collective-permute-start(bf16[16,2048]{1,0:T(8,128)(2,1)S(1)} %collective-permute-done.12), channel_id=1, source_target_pairs={{0,64},{32,96},{64,0},{96,32},{1,65},{33,97},{65,1},{97,33},{2,66}... | collective-permute-start | bytes 196616 | tf_op jit(solution)/shard_map/ppermute | solution.py:25
  30.2 9.6 %collective-permute-start.15 = (bf16[16,2048]{1,0:T(8,128)(2,1)S(1)}, bf16[16,2048]{1,0:T(8,128)(2,1)S(1)}, u32[]{:S(2)}, u32[]{:S(2)}) collective-permute-start(bf16[16,2048]{1,0:T(8,128)(2,1)S(1)} %collective-permute-done.12), channel_id=1, source_target_pairs={{0,32},{32,64},{64,96},{96,0},{1,33},{33,65},{65,97},{97,1},{2,34}... | collective-permute-start | bytes 196616 | tf_op jit(solution)/shard_map/ppermute | solution.py:25
  36.2 8.5 %collective-permute-start.8 = (bf16[4,2,16,640]{3,2,1,0:T(8,128)(2,1)S(1)}, bf16[4,2,16,640]{3,2,1,0:T(8,128)(2,1)S(1)}, u32[]{:S(2)}, u32[]{:S(2)}) collective-permute-start(bf16[4,2,16,640]{3,2,1,0:T(8,128)(2,1)S(1)} %pad_maximum_fusion.7), channel_id=1, source_target_pairs={{0,8},{1,9},{2,10},{3,11},{4,12},{5,13},{6,14},{7,15},{8,16},{9,17... | collective-permute-start | bytes 491528 | tf_op jit(solution)/shard_map/ppermute | solution.py:42
  37.6 9.5 %collective-permute-start.7 = (bf16[4,2,16,640]{3,2,1,0:T(8,128)(2,1)S(1)}, bf16[4,2,16,640]{3,2,1,0:T(8,128)(2,1)S(1)}, u32[]{:S(2)}, u32[]{:S(2)}) collective-permute-start(bf16[4,2,16,640]{3,2,1,0:T(8,128)(2,1)S(1)} %pad_maximum_fusion.7), channel_id=1, source_target_pairs={{0,16},{1,17},{2,18},{3,19},{4,20},{5,21},{6,22},{7,23},{8,24},{9,... | collective-permute-start | bytes 491528 | tf_op jit(solution)/shard_map/ppermute | solution.py:42
  38.2 12.8 %collective-permute-start.6 = (bf16[4,2,16,640]{3,2,1,0:T(8,128)(2,1)S(1)}, bf16[4,2,16,640]{3,2,1,0:T(8,128)(2,1)S(1)}, u32[]{:S(2)}, u32[]{:S(2)}) collective-permute-start(bf16[4,2,16,640]{3,2,1,0:T(8,128)(2,1)S(1)} %pad_maximum_fusion.7), channel_id=1, source_target_pairs={{0,24},{1,25},{2,26},{3,27},{4,28},{5,29},{6,30},{7,31},{8,0},{9,1... | collective-permute-start | bytes 491528 | tf_op jit(solution)/shard_map/ppermute | solution.py:42
  39.3 14.1 %collective-permute-start.10 = (bf16[128,2048]{1,0:T(8,128)(2,1)}, bf16[128,2048]{1,0:T(8,128)(2,1)}, u32[]{:S(2)}, u32[]{:S(2)}) collective-permute-start(bf16[128,2048]{1,0:T(8,128)(2,1)} %param.35), channel_id=1, source_target_pairs={{0,32},{1,97},{2,34},{3,99},{4,36},{5,101},{6,38},{7,103},{8,40},{... | collective-permute-start | bytes 1572872 | tf_op jit(solution)/shard_map/ppermute | solution.py:60
  53.4 10.7 %collective-permute-start.11 = (bf16[128,2048]{1,0:T(8,128)(2,1)}, bf16[128,2048]{1,0:T(8,128)(2,1)}, u32[]{:S(2)}, u32[]{:S(2)}) collective-permute-start(bf16[128,2048]{1,0:T(8,128)(2,1)} %collective-permute-done.10), channel_id=1, source_target_pairs={{0,32},{1,97},{2,34},{3,99},{4,36},{5,101},{6,38},{7,103},{8,40},{... | collective-permute-start | bytes 1572872 | tf_op jit(solution)/shard_map/ppermute | solution.py:60
  55.7 36.8 %copy-start.4 = (bf16[576,2048]{1,0:T(8,128)(2,1)}, bf16[576,2048]{1,0:T(8,128)(2,1)S(1)}, u32[]{:S(2)}) copy-start(bf16[576,2048]{1,0:T(8,128)(2,1)S(1)} %fusion.12.refs_2_.refs_3_) | copy-start | bytes 7077892
  64.1 331.7 %reduce-scatter.2.cloned.1.call-start = ((), (), s32[]{:S(2)}) async-start(), calls=%async_computation.4 | async-start | bytes 19464192 | tf_op jit(solution)/shard_map/reduce_scatter | solution.py:867
  66.4 26.1 %copy-start.41 = (bf16[2048,1920]{1,0:T(8,128)(2,1)S(1)}, bf16[2048,1920]{1,0:T(8,128)(2,1)}, u32[]{:S(2)}) copy-start(bf16[2048,1920]{1,0:T(8,128)(2,1)} %all-gather.3.cloned.1.call-done) | copy-start | bytes 23592964
  77.8 1.3 collective-permute-start.16
  79.1 6.0 %collective-permute-start.17 = (f32[2,8,640]{2,1,0:T(8,128)S(1)}, f32[2,8,640]{2,1,0:T(8,128)S(1)}, u32[]{:S(2)}, u32[]{:S(2)}) collective-permute-start(f32[2,8,640]{2,1,0:T(8,128)S(1)} %pad_maximum_fusion.9.refs_0_), channel_id=1, source_target_pairs={{0,6},{1,7},{2,0},{3,1},{4,2},{5,3},{6,4},{7,5},{8,14},{9,15},{10,... | collective-permute-start | bytes 122888 | tf_op jit(solution)/shard_map/ppermute | solution.py:42
  79.2 6.2 %collective-permute-start.18 = (f32[2,8,640]{2,1,0:T(8,128)S(1)}, f32[2,8,640]{2,1,0:T(8,128)S(1)}, u32[]{:S(2)}, u32[]{:S(2)}) collective-permute-start(f32[2,8,640]{2,1,0:T(8,128)S(1)} %pad_maximum_fusion.9.refs_0_), channel_id=1, source_target_pairs={{0,4},{1,5},{2,6},{3,7},{4,0},{5,1},{6,2},{7,3},{8,12},{9,13},{10,... | collective-permute-start | bytes 122888 | tf_op jit(solution)/shard_map/ppermute | solution.py:42
  82.4 4.9 %collective-permute-start.19 = (f32[2,8,640]{2,1,0:T(8,128)S(1)}, f32[2,8,640]{2,1,0:T(8,128)S(1)}, u32[]{:S(2)}, u32[]{:S(2)}) collective-permute-start(f32[2,8,640]{2,1,0:T(8,128)S(1)} %pad_maximum_fusion.9.refs_0_), channel_id=1, source_target_pairs={{0,2},{1,3},{2,4},{3,5},{4,6},{5,7},{6,0},{7,1},{8,10},{9,11},{10,... | collective-permute-start | bytes 122888 | tf_op jit(solution)/shard_map/ppermute | solution.py:42
  87.9 6.4 %collective-permute-start.20 = (f32[8,640]{1,0:T(8,128)S(1)}, f32[8,640]{1,0:T(8,128)S(1)}, u32[]{:S(2)}, u32[]{:S(2)}) collective-permute-start(f32[8,640]{1,0:T(8,128)S(1)} %get-tuple-element.59.piece0), channel_id=1, source_target_pairs={{0,24},{1,25},{2,26},{3,27},{4,28},{5,29},{6,30},{7,31},{8,0},{9,1... | collective-permute-start | bytes 61448 | tf_op jit(solution)/shard_map/ppermute | solution.py:42
  88.8 5.6 %collective-permute-start.21 = (f32[8,640]{1,0:T(8,128)S(1)}, f32[8,640]{1,0:T(8,128)S(1)}, u32[]{:S(2)}, u32[]{:S(2)}) collective-permute-start(f32[8,640]{1,0:T(8,128)S(1)} %get-tuple-element.59.piece0), channel_id=1, source_target_pairs={{0,16},{1,17},{2,18},{3,19},{4,20},{5,21},{6,22},{7,23},{8,24},{9,... | collective-permute-start | bytes 61448 | tf_op jit(solution)/shard_map/ppermute | solution.py:42
  92.5 3.8 collective-permute-start.22
  99.8 14.0 %collective-permute-start.24 = (bf16[128,2048]{1,0:T(8,128)(2,1)S(1)}, bf16[128,2048]{1,0:T(8,128)(2,1)S(1)}, u32[]{:S(2)}, u32[]{:S(2)}) collective-permute-start(bf16[128,2048]{1,0:T(8,128)(2,1)S(1)} %get-tuple-element.117), channel_id=1, source_target_pairs={{0,32},{1,97},{2,34},{3,99},{4,36},{5,101},{6,38},{7,103},{8,40},{... | collective-permute-start | bytes 1572872 | tf_op jit(solution)/shard_map/ppermute | solution.py:60
  99.8 18.2 %collective-permute-start.23 = (bf16[128,2048]{1,0:T(8,128)(2,1)S(1)}, bf16[128,2048]{1,0:T(8,128)(2,1)S(1)}, u32[]{:S(2)}, u32[]{:S(2)}) collective-permute-start(bf16[128,2048]{1,0:T(8,128)(2,1)S(1)} %get-tuple-element.116), channel_id=1, source_target_pairs={{0,96},{1,33},{2,98},{3,35},{4,100},{5,37},{6,102},{7,39},{8,104},... | collective-permute-start | bytes 1572872 | tf_op jit(solution)/shard_map/ppermute | solution.py:60
  114.8 13.3 %collective-permute-start.25 = (bf16[128,2048]{1,0:T(8,128)(2,1)}, bf16[128,2048]{1,0:T(8,128)(2,1)}, u32[]{:S(2)}, u32[]{:S(2)}) collective-permute-start(bf16[128,2048]{1,0:T(8,128)(2,1)} %add_convert_fusion.6), channel_id=1, source_target_pairs={{0,32},{1,97},{2,34},{3,99},{4,36},{5,101},{6,38},{7,103},{8,40},{... | collective-permute-start | bytes 1572872 | tf_op jit(solution)/shard_map/ppermute | solution.py:60
  114.8 17.9 %collective-permute-start.29 = (bf16[128,2048]{1,0:T(8,128)(2,1)}, bf16[128,2048]{1,0:T(8,128)(2,1)}, u32[]{:S(2)}, u32[]{:S(2)}) collective-permute-start(bf16[128,2048]{1,0:T(8,128)(2,1)} %param.35), channel_id=1, source_target_pairs={{0,96},{1,33},{2,98},{3,35},{4,100},{5,37},{6,102},{7,39},{8,104},... | collective-permute-start | bytes 1572872 | tf_op jit(solution)/shard_map/ppermute | solution.py:60
  130.4 93.2 %copy-start.16 = (f32[128,2048]{1,0:T(8,128)}, f32[128,2048]{1,0:T(8,128)S(1)}, u32[]{:S(2)}) copy-start(f32[128,2048]{1,0:T(8,128)S(1)} %get-tuple-element.106) | copy-start | bytes 3145732
  130.6 9.2 %collective-permute-start.26 = (bf16[128,2048]{1,0:T(8,128)(2,1)S(1)}, bf16[128,2048]{1,0:T(8,128)(2,1)S(1)}, u32[]{:S(2)}, u32[]{:S(2)}) collective-permute-start(bf16[128,2048]{1,0:T(8,128)(2,1)S(1)} %multiply_convert_fusion.3), channel_id=1, source_target_pairs={{0,96},{1,33},{2,98},{3,35},{4,100},{5,37},{6,102},{7,39},{8,104},... | collective-permute-start | bytes 1572872 | tf_op jit(solution)/shard_map/ppermute | solution.py:60
  130.7 10.5 %collective-permute-start.27 = (bf16[128,2048]{1,0:T(8,128)(2,1)S(1)}, bf16[128,2048]{1,0:T(8,128)(2,1)S(1)}, u32[]{:S(2)}, u32[]{:S(2)}) collective-permute-start(bf16[128,2048]{1,0:T(8,128)(2,1)S(1)} %multiply_convert_fusion.3), channel_id=1, source_target_pairs={{0,32},{1,97},{2,34},{3,99},{4,36},{5,101},{6,38},{7,103},{8,40},{... | collective-permute-start | bytes 1572872 | tf_op jit(solution)/shard_map/ppermute | solution.py:60
  145.4 10.8 %collective-permute-start.28 = (bf16[128,2048]{1,0:T(8,128)(2,1)}, bf16[128,2048]{1,0:T(8,128)(2,1)S(1)}, u32[]{:S(2)}, u32[]{:S(2)}) collective-permute-start(bf16[128,2048]{1,0:T(8,128)(2,1)} %copy-done.33), channel_id=1, source_target_pairs={{0,32},{1,97},{2,34},{3,99},{4,36},{5,101},{6,38},{7,103},{8,40},{... | collective-permute-start | bytes 1572872 | tf_op jit(solution)/shard_map/ppermute | solution.py:60
  196.7 15.8 %collective-permute-start.30 = (bf16[128,2048]{1,0:T(8,128)(2,1)S(1)}, bf16[128,2048]{1,0:T(8,128)(2,1)S(1)}, u32[]{:S(2)}, u32[]{:S(2)}) collective-permute-start(bf16[128,2048]{1,0:T(8,128)(2,1)S(1)} %get-tuple-element.115), channel_id=1, source_target_pairs={{0,32},{1,97},{2,34},{3,99},{4,36},{5,101},{6,38},{7,103},{8,40},{... | collective-permute-start | bytes 1572872 | tf_op jit(solution)/shard_map/ppermute | solution.py:60
  197.2 15.6 %collective-permute-start.31 = (bf16[128,2048]{1,0:T(8,128)(2,1)S(1)}, bf16[128,2048]{1,0:T(8,128)(2,1)S(1)}, u32[]{:S(2)}, u32[]{:S(2)}) collective-permute-start(bf16[128,2048]{1,0:T(8,128)(2,1)S(1)} %get-tuple-element.114), channel_id=1, source_target_pairs={{0,96},{1,33},{2,98},{3,35},{4,100},{5,37},{6,102},{7,39},{8,104},... | collective-permute-start | bytes 1572872 | tf_op jit(solution)/shard_map/ppermute | solution.py:60
  212.7 10.5 %collective-permute-start.32 = (bf16[128,2048]{1,0:T(8,128)(2,1)S(1)}, bf16[128,2048]{1,0:T(8,128)(2,1)S(1)}, u32[]{:S(2)}, u32[]{:S(2)}) collective-permute-start(bf16[128,2048]{1,0:T(8,128)(2,1)S(1)} %add_convert_fusion.5), channel_id=1, source_target_pairs={{0,32},{1,97},{2,34},{3,99},{4,36},{5,101},{6,38},{7,103},{8,40},{... | collective-permute-start | bytes 1572872 | tf_op jit(solution)/shard_map/ppermute | solution.py:60
  226.4 12.6 %collective-permute-start.34 = (bf16[128,2048]{1,0:T(8,128)(2,1)S(1)}, bf16[128,2048]{1,0:T(8,128)(2,1)S(1)}, u32[]{:S(2)}, u32[]{:S(2)}) collective-permute-start(bf16[128,2048]{1,0:T(8,128)(2,1)S(1)} %get-tuple-element.103), channel_id=1, source_target_pairs={{0,32},{1,97},{2,34},{3,99},{4,36},{5,101},{6,38},{7,103},{8,40},{... | collective-permute-start | bytes 1572872 | tf_op jit(solution)/shard_map/ppermute | solution.py:60
  226.4 20.6 %collective-permute-start.33 = (bf16[128,2048]{1,0:T(8,128)(2,1)S(1)}, bf16[128,2048]{1,0:T(8,128)(2,1)S(1)}, u32[]{:S(2)}, u32[]{:S(2)}) collective-permute-start(bf16[128,2048]{1,0:T(8,128)(2,1)S(1)} %get-tuple-element.103), channel_id=1, source_target_pairs={{0,96},{1,33},{2,98},{3,35},{4,100},{5,37},{6,102},{7,39},{8,104},... | collective-permute-start | bytes 1572872 | tf_op jit(solution)/shard_map/ppermute | solution.py:60
  239.0 10.4 %collective-permute-start.35 = (bf16[128,2048]{1,0:T(8,128)(2,1)S(1)}, bf16[128,2048]{1,0:T(8,128)(2,1)S(1)}, u32[]{:S(2)}, u32[]{:S(2)}) collective-permute-start(bf16[128,2048]{1,0:T(8,128)(2,1)S(1)} %collective-permute-done.34), channel_id=1, source_target_pairs={{0,32},{1,97},{2,34},{3,99},{4,36},{5,101},{6,38},{7,103},{8,40},{... | collective-permute-start | bytes 1572872 | tf_op jit(solution)/shard_map/ppermute | solution.py:60
  258.2 1.2 collective-permute-start.36
  259.4 5.0 %collective-permute-start.37 = (f32[2,8,640]{2,1,0:T(8,128)S(1)}, f32[2,8,640]{2,1,0:T(8,128)S(1)}, u32[]{:S(2)}, u32[]{:S(2)}) collective-permute-start(f32[2,8,640]{2,1,0:T(8,128)S(1)} %pad_maximum_fusion.10.refs_0_), channel_id=1, source_target_pairs={{0,6},{1,7},{2,0},{3,1},{4,2},{5,3},{6,4},{7,5},{8,14},{9,15},{10,... | collective-permute-start | bytes 122888 | tf_op jit(solution)/shard_map/ppermute | solution.py:42
  260.1 6.7 %collective-permute-start.38 = (f32[2,8,640]{2,1,0:T(8,128)S(1)}, f32[2,8,640]{2,1,0:T(8,128)S(1)}, u32[]{:S(2)}, u32[]{:S(2)}) collective-permute-start(f32[2,8,640]{2,1,0:T(8,128)S(1)} %pad_maximum_fusion.10.refs_0_), channel_id=1, source_target_pairs={{0,4},{1,5},{2,6},{3,7},{4,0},{5,1},{6,2},{7,3},{8,12},{9,13},{10,... | collective-permute-start | bytes 122888 | tf_op jit(solution)/shard_map/ppermute | solution.py:42
  262.4 5.2 %collective-permute-start.39 = (f32[2,8,640]{2,1,0:T(8,128)S(1)}, f32[2,8,640]{2,1,0:T(8,128)S(1)}, u32[]{:S(2)}, u32[]{:S(2)}) collective-permute-start(f32[2,8,640]{2,1,0:T(8,128)S(1)} %pad_maximum_fusion.10.refs_0_), channel_id=1, source_target_pairs={{0,2},{1,3},{2,4},{3,5},{4,6},{5,7},{6,0},{7,1},{8,10},{9,11},{10,... | collective-permute-start | bytes 122888 | tf_op jit(solution)/shard_map/ppermute | solution.py:42
  268.2 4.7 %collective-permute-start.40 = (f32[8,640]{1,0:T(8,128)S(1)}, f32[8,640]{1,0:T(8,128)S(1)}, u32[]{:S(2)}, u32[]{:S(2)}) collective-permute-start(f32[8,640]{1,0:T(8,128)S(1)} %get-tuple-element.75.piece0), channel_id=1, source_target_pairs={{0,24},{1,25},{2,26},{3,27},{4,28},{5,29},{6,30},{7,31},{8,0},{9,1... | collective-permute-start | bytes 61448 | tf_op jit(solution)/shard_map/ppermute | solution.py:42
  268.8 5.9 %collective-permute-start.41 = (f32[8,640]{1,0:T(8,128)S(1)}, f32[8,640]{1,0:T(8,128)S(1)}, u32[]{:S(2)}, u32[]{:S(2)}) collective-permute-start(f32[8,640]{1,0:T(8,128)S(1)} %get-tuple-element.75.piece0), channel_id=1, source_target_pairs={{0,16},{1,17},{2,18},{3,19},{4,20},{5,21},{6,22},{7,23},{8,24},{9,... | collective-permute-start | bytes 61448 | tf_op jit(solution)/shard_map/ppermute | solution.py:42
  271.5 4.4 %collective-permute-start.42 = (f32[8,640]{1,0:T(8,128)S(1)}, f32[8,640]{1,0:T(8,128)S(1)}, u32[]{:S(2)}, u32[]{:S(2)}) collective-permute-start(f32[8,640]{1,0:T(8,128)S(1)} %get-tuple-element.75.piece0), channel_id=1, source_target_pairs={{0,8},{1,9},{2,10},{3,11},{4,12},{5,13},{6,14},{7,15},{8,16},{9,17... | collective-permute-start | bytes 61448 | tf_op jit(solution)/shard_map/ppermute | solution.py:42
  287.0 3.2 collective-permute-start.43
  296.7 7.8 %collective-permute-start.44 = (bf16[16,216,640]{2,1,0:T(8,128)(2,1)S(1)}, bf16[16,216,640]{2,1,0:T(8,128)(2,1)S(1)}, u32[]{:S(2)}, u32[]{:S(2)}) collective-permute-start(bf16[16,216,640]{2,1,0:T(8,128)(2,1)S(1)} %get-tuple-element.86), channel_id=1, source_target_pairs={{0,1},{1,0},{2,3},{3,2},{4,5},{5,4},{6,7},{7,6},{8,9},{9,8},{10,11... | collective-permute-start | bytes 13271048 | tf_op jit(solution)/shard_map/ppermute | solution.py:42
  308.0 12.4 %collective-permute-start.46 = (bf16[128,2048]{1,0:T(8,128)(2,1)S(1)}, bf16[128,2048]{1,0:T(8,128)(2,1)S(1)}, u32[]{:S(2)}, u32[]{:S(2)}) collective-permute-start(bf16[128,2048]{1,0:T(8,128)(2,1)S(1)} %get-tuple-element.121), channel_id=1, source_target_pairs={{0,32},{1,97},{2,34},{3,99},{4,36},{5,101},{6,38},{7,103},{8,40},{... | collective-permute-start | bytes 1572872 | tf_op jit(solution)/shard_map/ppermute | solution.py:60
  308.1 77.6 %all-to-all-start = ((bf16[16,216,640]{2,1,0:T(8,128)(2,1)}), bf16[16,216,640]{2,1,0:T(8,128)(2,1)}, u32[]{:S(2)}, u32[]{:S(2)}) async-start(bf16[16,216,640]{2,1,0:T(8,128)(2,1)} %add_convert_fusion), calls=%async_computation | async-start | bytes 8847360 | tf_op jit(solution)/shard_map/all_to_all | solution.py:137
  317.2 13.9 %collective-permute-start.45 = (bf16[128,2048]{1,0:T(8,128)(2,1)S(1)}, bf16[128,2048]{1,0:T(8,128)(2,1)S(1)}, u32[]{:S(2)}, u32[]{:S(2)}) collective-permute-start(bf16[128,2048]{1,0:T(8,128)(2,1)S(1)} %get-tuple-element.120), channel_id=1, source_target_pairs={{0,96},{1,33},{2,98},{3,35},{4,100},{5,37},{6,102},{7,39},{8,104},... | collective-permute-start | bytes 1572872 | tf_op jit(solution)/shard_map/ppermute | solution.py:60
  321.8 11.5 %collective-permute-start.47 = (bf16[128,2048]{1,0:T(8,128)(2,1)S(1)}, bf16[128,2048]{1,0:T(8,128)(2,1)S(1)}, u32[]{:S(2)}, u32[]{:S(2)}) collective-permute-start(bf16[128,2048]{1,0:T(8,128)(2,1)S(1)} %add_convert_fusion.4), channel_id=1, source_target_pairs={{0,32},{1,97},{2,34},{3,99},{4,36},{5,101},{6,38},{7,103},{8,40},{... | collective-permute-start | bytes 1572872 | tf_op jit(solution)/shard_map/ppermute | solution.py:60
  335.9 26.1 %copy-start.17 = (f32[128,2048]{1,0:T(8,128)S(1)}, f32[128,2048]{1,0:T(8,128)}, u32[]{:S(2)}) copy-start(f32[128,2048]{1,0:T(8,128)} %copy-done.16) | copy-start | bytes 3145732
  335.9 14.2 %collective-permute-start.49 = (bf16[128,2048]{1,0:T(8,128)(2,1)}, bf16[128,2048]{1,0:T(8,128)(2,1)S(1)}, u32[]{:S(2)}, u32[]{:S(2)}) collective-permute-start(bf16[128,2048]{1,0:T(8,128)(2,1)} %get-tuple-element.119), channel_id=1, source_target_pairs={{0,32},{1,97},{2,34},{3,99},{4,36},{5,101},{6,38},{7,103},{8,40},{... | collective-permute-start | bytes 1572872 | tf_op jit(solution)/shard_map/ppermute | solution.py:60
  335.9 18.2 %collective-permute-start.48 = (bf16[128,2048]{1,0:T(8,128)(2,1)}, bf16[128,2048]{1,0:T(8,128)(2,1)S(1)}, u32[]{:S(2)}, u32[]{:S(2)}) collective-permute-start(bf16[128,2048]{1,0:T(8,128)(2,1)} %get-tuple-element.118), channel_id=1, source_target_pairs={{0,96},{1,33},{2,98},{3,35},{4,100},{5,37},{6,102},{7,39},{8,104},... | collective-permute-start | bytes 1572872 | tf_op jit(solution)/shard_map/ppermute | solution.py:60
  351.5 10.5 %collective-permute-start.50 = (bf16[128,2048]{1,0:T(8,128)(2,1)S(1)}, bf16[128,2048]{1,0:T(8,128)(2,1)S(1)}, u32[]{:S(2)}, u32[]{:S(2)}) collective-permute-start(bf16[128,2048]{1,0:T(8,128)(2,1)S(1)} %add_convert_fusion.3), channel_id=1, source_target_pairs={{0,32},{1,97},{2,34},{3,99},{4,36},{5,101},{6,38},{7,103},{8,40},{... | collective-permute-start | bytes 1572872 | tf_op jit(solution)/shard_map/ppermute | solution.py:60
  364.1 25.4 %copy-start.39 = (bf16[64]{0:T(256)(128)(2,1)S(1)}, bf16[64]{0:T(256)(128)(2,1)}, u32[]{:S(2)}) copy-start(bf16[64]{0:T(256)(128)(2,1)} %param.19) | copy-start | bytes 388
  364.1 28.2 %copy-start.40 = (bf16[20]{0:T(256)(128)(2,1)S(1)}, bf16[20]{0:T(256)(128)(2,1)}, u32[]{:S(2)}) copy-start(bf16[20]{0:T(256)(128)(2,1)} %param.28) | copy-start | bytes 124
  389.6 5.2 %collective-permute-start.53 = (f32[1,128]{1,0:T(1,128)S(1)}, f32[1,128]{1,0:T(1,128)S(1)}, u32[]{:S(2)}, u32[]{:S(2)}) collective-permute-start(f32[1,128]{1,0:T(1,128)S(1)} %maximum_bitcast_fusion), channel_id=1, source_target_pairs={{0,64},{32,96},{64,0},{96,32},{1,65},{33,97},{65,1},{97,33},{2,66}... | collective-permute-start | bytes 1544 | tf_op jit(solution)/shard_map/ppermute | solution.py:25
  389.7 5.2 %collective-permute-start.52 = (f32[1,128]{1,0:T(1,128)S(1)}, f32[1,128]{1,0:T(1,128)S(1)}, u32[]{:S(2)}, u32[]{:S(2)}) collective-permute-start(f32[1,128]{1,0:T(1,128)S(1)} %maximum_bitcast_fusion), channel_id=1, source_target_pairs={{0,96},{32,0},{64,32},{96,64},{1,97},{33,1},{65,33},{97,65},{2,98}... | collective-permute-start | bytes 1544 | tf_op jit(solution)/shard_map/ppermute | solution.py:25
  389.8 5.5 %collective-permute-start.51 = (f32[1,128]{1,0:T(1,128)S(1)}, f32[1,128]{1,0:T(1,128)S(1)}, u32[]{:S(2)}, u32[]{:S(2)}) collective-permute-start(f32[1,128]{1,0:T(1,128)S(1)} %maximum_bitcast_fusion), channel_id=1, source_target_pairs={{0,32},{32,64},{64,96},{96,0},{1,33},{33,65},{65,97},{97,1},{2,34}... | collective-permute-start | bytes 1544 | tf_op jit(solution)/shard_map/ppermute | solution.py:25
  (39 other events, 326.8 us)
Sparse Core Ops, SparseCore 0:
  10.8 53.8 all-gather.2
  67.0 78.3 all-gather.4
  185.9 121.1 reduce-scatter.1

commit v2 on v1

--- a/solution.py
+++ b/solution.py
@@ -12,7 +12,7 @@
 TOKS = 32
 OWN = 128
 HALO = 16
-SMALL = 24
+SMALL = 16
 FIRST = 104
 
 eps_norm = 1e-06
@@ -226,7 +226,7 @@
     edge_ref,
     gates_ref,
     pre_ref,
-    high_ref,
+    exact_ref,
 ):
     slot = pl.program_id(0)
     channels = conv_ref.shape[1]
@@ -252,41 +252,45 @@
         for tap in range(1, CONV):
             lagged = pltpu.roll(rows, tap, 0)[HALO:]
             total = total + taps_ref[tap : tap + 1, :] * jnp.where(places >= tap, lagged, 0.0)
-        conv_ref[at, :] = total
-        high_ref[at, :] = total.astype(bf16)
+        exact_ref[at, :] = total
+        conv_ref[at, :] = total.astype(bf16)
     for step in range(0, width, 256):
         columns = slice(step, step + 256)
         pre_ref[:, columns] = (
-            jnp.dot(high_ref[...], gates_ref[:, columns], preferred_element_type=f32)
+            jnp.dot(conv_ref[...], gates_ref[:, columns], preferred_element_type=f32)
             + bias_ref[:, columns]
         )
 
     row_ids = lax.broadcasted_iota(jnp.int32, (8, channels), 0)
 
-    def scan(tile, carry):
-        rows = rows_at(tile * 8, 8)
-        rates = sigmoid(pre_ref[rows, :channels])
-        entries = 0.5 * jnp.tanh(0.5 * pre_ref[rows, channels:]) + 0.5
-        log_keep = -soft_ref[...] * rates
-        resets = place_ref[rows, :] == 0
-        coeff = jnp.where(resets, 0.0, jnp.exp(log_keep))
-        squared = one_minus_exp(2.0 * log_keep)
-        scaling = jnp.where(resets, 1.0, squared * inverse_root(squared))
-        value = entries * conv_ref[rows, :] * scaling
-        for distance in (1, 2, 4):
-            reach = row_ids >= distance
-            value = value + coeff * jnp.where(reach, pltpu.roll(value, distance, 0), 0.0)
-            coeff = coeff * jnp.where(reach, pltpu.roll(coeff, distance, 0), 1.0)
-        value = value + coeff * carry[1]
-        coeff = coeff * carry[0]
-        rate_ref[rows, :] = rates
-        entry_ref[rows, :] = entries
-        local_ref[rows, :] = value
-        cum_ref[rows, :] = coeff
-        return coeff[7:8], value[7:8]
+    def scan(step, carry):
+        halves = []
+        for part in range(2):
+            rows = rows_at(step * HALO + 8 * part, 8)
+            rates = sigmoid(pre_ref[rows, :channels])
+            entries = 0.5 * jnp.tanh(0.5 * pre_ref[rows, channels:]) + 0.5
+            log_keep = -soft_ref[...] * rates
+            resets = place_ref[rows, :] == 0
+            coeff = jnp.where(resets, 0.0, jnp.exp(log_keep))
+            squared = one_minus_exp(2.0 * log_keep)
+            scaling = jnp.where(resets, 1.0, squared * inverse_root(squared))
+            value = entries * exact_ref[rows, :] * scaling
+            for distance in (1, 2, 4):
+                reach = row_ids >= distance
+                value = value + coeff * jnp.where(reach, pltpu.roll(value, distance, 0), 0.0)
+                coeff = coeff * jnp.where(reach, pltpu.roll(coeff, distance, 0), 1.0)
+            value = value + coeff * carry[1]
+            coeff = coeff * carry[0]
+            rate_ref[rows, :] = rates
+            local_ref[rows, :] = value
+            cum_ref[rows, :] = coeff
+            halves.append(entries)
+            carry = coeff[7:8], value[7:8]
+        entry_ref[rows_at(step * HALO, HALO), :] = jnp.concatenate(halves, axis=0).astype(bf16)
+        return carry
 
     start = (jnp.ones((1, channels), f32), jnp.zeros((1, channels), f32))
-    coeff, value = lax.fori_loop(0, OWN // 8, scan, start, unroll=4)
+    coeff, value = lax.fori_loop(0, OWN // HALO, scan, start, unroll=2)
     edge_ref[pl.ds(slot, 1), :] = coeff
     edge_ref[pl.ds(slot + MEMBERS, 1), :] = value
 
@@ -365,7 +369,7 @@
     def apply(tile, token):
         rows = rows_at(tile * HALO, HALO)
         states = local_ref[rows, :] + cum_ref[rows, :] * carry
-        state_ref[rows, :] = states
+        state_ref[rows, :] = states.astype(bf16)
         mixed_ref[rows, :] = (states * gelu_parts(branch_ref[rows, :])[0]).astype(bf16)
         return token
 
@@ -402,10 +406,11 @@
         base = OWN - HALO - step * HALO
         cum, later = carry
         slopes = []
+        states = state_ref[rows_at(base, HALO), :].astype(f32)
         for part in (1, 0):
             rows = rows_at(base + 8 * part, 8)
             gated, slope = gelu_parts(branch_ref[rows, :])
-            slopes.append(slope * grad_ref[rows, :] * state_ref[rows, :])
+            slopes.append(slope * grad_ref[rows, :] * states[8 * part : 8 * part + 8])
             held, _, coeff = reverse_scan(
                 rows, later, gated, grad_ref, rate_ref, place_ref, soft_ref, row_ids
             )
@@ -465,6 +470,11 @@
         later, logit_sum, rate_sum, entry_sum = carry
         base = OWN - HALO - step * HALO
         low_rate, low_entry = [], []
+        both = rows_at(base, HALO)
+        states, convs = state_ref[both, :].astype(f32), conv_ref[both, :].astype(f32)
+        all_entries = entry_ref[both, :].astype(f32)
+        before = state_ref[rows_at(jnp.maximum(base - HALO, 0), HALO), :].astype(f32)[HALO - 1 :]
+        before = jnp.where(base == 0, ahead_first, before)
         for part in (1, 0):
             first = base + 8 * part
             rows = rows_at(first, 8)
@@ -474,10 +484,10 @@
             )
             adjoint = sgrad + jnp.where(row_ids == 7, later, pltpu.roll(held, 7, 0))
             later = held[0:1]
-            ahead = state_ref[rows_at(jnp.maximum(first - 8, 0), 8), :][7:8]
-            ahead = jnp.where(first == 0, ahead_first, ahead)
-            previous = jnp.where(row_ids == 0, ahead, pltpu.roll(state_ref[rows, :], 1, 0))
-            rates, entries, conv = rate_ref[rows, :], entry_ref[rows, :], conv_ref[rows, :]
+            half = slice(8 * part, 8 * part + 8)
+            ahead = states[7:8] if part else before
+            previous = jnp.where(row_ids == 0, ahead, pltpu.roll(states[half], 1, 0))
+            rates, entries, conv = rate_ref[rows, :], all_entries[half], convs[half]
             resets = place_ref[rows, :] == 0
             log_keep = -soft_ref[...] * rates
             squared = one_minus_exp(2.0 * log_keep)
@@ -623,7 +633,9 @@
     rows, features = lhs_one.shape
     columns = rhs[0].shape[1]
     height = 1024
-    whole = pl.BlockSpec((rows, columns), lambda j, i: (0, 0))
+    whole = pl.BlockSpec(
+        (rows, columns), lambda j, i: (0, 0), pipeline_mode=pl.Buffered(buffer_count=1)
+    )
     return pl.pallas_call(
         outer_kernel,
         grid=(3, features // height),
@@ -635,8 +647,8 @@
             whole,
         ],
         out_specs=pl.BlockSpec((height, columns), lambda j, i: (i, j)),
-        out_shape=jax.ShapeDtypeStruct((features, 3 * columns), bf16),
-        compiler_params=pltpu.CompilerParams(vmem_limit_bytes=32 * 1024 * 1024),
+        out_shape=pltpu.HBM((features, 3 * columns), bf16),
+        compiler_params=pltpu.CompilerParams(vmem_limit_bytes=26 * 1024 * 1024),
         cost_estimate=pl.CostEstimate(
             flops=6 * rows * features * columns,
             bytes_accessed=6 * features * columns,
@@ -650,7 +662,7 @@
     width = 2 * channels
     block = cut * TOKS
     dense = lax.dot_general(
-        conv_ref[...].astype(bf16),
+        conv_ref[...],
         pregrad_ref[...],
         (((0,), (0,)), ((), ())),
         preferred_element_type=f32,
@@ -661,10 +673,15 @@
     for group in range(channels // block):
         inside = (columns >= group * block) & (columns < (group + 1) * block)
         gates = jnp.where(inside, dense[group * block : (group + 1) * block], gates)
-    spare = jnp.zeros((SMALL - 2 * cut - 9, channels), f32)
+    own = channels // TOKS
+    sums = sums_ref[...]
+    blank = jnp.zeros((4, channels - 256), f32)
+    spare = jnp.zeros((SMALL - 2 * cut - 5, channels), f32)
     for tok in range(TOKS):
         rows = gates[tok * cut : (tok + 1) * cut]
-        pieces = [rows[:, :channels], rows[:, channels:], sums_ref[...]]
+        turned_sums = pltpu.roll(sums, channels - tok * own, 1) if tok else sums
+        vectors = [turned_sums[:4, :128], turned_sums[4:, :128], blank]
+        pieces = [rows[:, :channels], rows[:, channels:], jnp.concatenate(vectors, axis=1)]
         pieces += [extra_ref[tok : tok + 1, :], spare]
         out_ref[tok] = jnp.concatenate(pieces, axis=0).astype(bf16)
 
@@ -813,7 +830,7 @@
     halo_first = total_rows // HALO
     conv, rates, entries, local, cum, edges, gates = by_slot(
         local_forward_kernel,
-        [(OWN, (total_rows, channels), f32)] * 5
+        [(OWN, (total_rows, channels), kind) for kind in (bf16, f32, bf16, f32, f32)]
         + [(None, (8, channels), f32), (None, (channels, 2 * channels), bf16)],
         [
             taps,
@@ -825,7 +842,7 @@
             (conv_input, HALO, halo_first),
             (places, OWN, 0),
         ],
-        [((OWN, 2 * channels), f32), ((OWN, channels), bf16)],
+        [((OWN, 2 * channels), f32), ((OWN, channels), f32)],
         (),
         30_000_000,
         [True, True, True, False, False, False, True],
@@ -835,7 +852,7 @@
     states, mixture, carried = by_slot(
         mix_kernel,
         [
-            (OWN, (total_rows, channels), f32),
+            (OWN, (total_rows, channels), bf16),
             (OWN, (total_rows, channels), bf16),
             (None, (MEMBERS, channels), f32),
         ],
@@ -854,7 +871,7 @@
     factor_two = norm_factor(middle)
     normed_two = (middle * factor_two * feed_gain).astype(bf16)
     hidden_grad = product(after(cotangent_all, mixture), down_turned)
-    blocks_two = ring_gather(normed_two, spot[2], (feed_all,))
+    blocks_two = ring_gather(normed_two, spot[2])
     blocks_two[2] = after(blocks_two[2], hidden_grad)
     wide_two = jnp.concatenate(blocks_two, axis=0)
     gate_up = product(wide_two, gate_up_all)
@@ -950,15 +967,15 @@
     grad_mix_scale = jnp.sum(
         grad_branch * branch_mat.astype(f32) + grad_input * input_mat.astype(f32), axis=1
     ) / mix_scale.astype(f32)
-    gains_own = jnp.concatenate([grad_mix_scale, settled[2 * cut + 8, :slice_rows]])
+    gains_own = jnp.concatenate([grad_mix_scale, settled[2 * cut + 4, :slice_rows]])
     gains_own = hop_sum(gains_own.reshape(1, -1), "blk")[0]
     gate_own = [
         jnp.moveaxis(settled[i * cut : (i + 1) * cut].reshape(cut, groups, block), 1, 0)
         for i in range(2)
     ]
-    sums_own = lax.dynamic_slice(
-        settled[2 * cut : 2 * cut + 8], (0, tok * own_channels), (8, own_channels)
-    )
+    sums_own = settled[2 * cut : 2 * cut + 4]
+    taps_own = sums_own[:, 128 : 128 + own_channels]
+    sums_own = sums_own[:, :own_channels]
     own_logits = decay_logit.astype(f32)
     return (
         layer_out.astype(bf16),
@@ -966,7 +983,7 @@
         gains_own[:slice_rows],
         grad_branch,
         grad_input,
-        sums_own[4:],
+        taps_own,
         sums_own[0],
         gate_own[0],
         sums_own[1],

time: 413 us -> 407 us (0.985)
  other arithmetic: 47.4 us -> 42.1 us
  transfers between devices with their start and end apart: 58 -> 58, of which waited for: 35 -> 37; matrix products, arithmetic and copies ran while one was open for 22% -> 22% of each run, Pallas kernels for 8% -> 8%
where the time goes in v2:
time: 407 us; the launch traced here: 399 us
  waiting for transfers between devices  159 us (39%)
  starting transfers between devices  71.1 us (17%)
  matrix products  52 us (13%)
  Pallas kernels  46.3 us (11%)
  other arithmetic  42.1 us (10%)
  between operations  15.4 us (4%)
  local copies, waits for them, and re-layouts  13.3 us (3%)
    ppermute x24, waiting for transfers between devices, hop_apart(): return lax.ppermute(values, ('blk', 'tok'), route)  102 us
    ppermute x24, starting transfers between devices, hop_apart(): return lax.ppermute(values, ('blk', 'tok'), route)  30 us
    ppermute x22, waiting for transfers between devices, hop_tok(): return lax.ppermute(values, 'tok', route)  27.9 us
    dot_general x4, matrix products, product_back(): lax.dot_general(operand, weight, (((1,), (1,)), ((), ())), preferred_elem...  26.6 us
    dot_general x5, matrix products, product(): return jnp.dot(operand, weight, preferred_element_type=f32).astype(out)  25.4 us
    ppermute x22, starting transfers between devices, hop_tok(): return lax.ppermute(values, 'tok', route)  23.9 us
    pallas_call x4, Pallas kernels, by_slot(): pl.pallas_call(kernel, grid=(MEMBERS,), in_specs=[pl.BlockSpec(memory_spa...  23.1 us
    all_to_all x1, waiting for transfers between devices, chips_sum(): lax.all_to_all(values, 'tok', 0, 0, axis_index_groups=cores, tiled=True)  23 us
  transfers between devices with their start and end apart: 58, of which 37 were waited for; matrix products, arithmetic and copies ran while one was open for 22% of the time, Pallas kernels for 8%

profile of v2, /device:TPU:80, one launch (start us, length us, event | category | flops | bytes accessed | tf_op | source)
XLA Modules:
  0.0 398.9 jit_solution(15731857644671439478)
XLA Ops:
  7.2 1.7 pad_maximum_fusion.6
  10.6 1.7 collective-permute-start.4
  15.6 2.0 pad_maximum_fusion.4
  18.2 3.1 collective-permute-start.1
  29.6 2.2 collective-permute-start.14
  32.8 2.9 collective-permute-done.9
  40.0 4.4 %collective-permute-done.8 = bf16[4,2,16,640]{3,2,1,0:T(8,128)(2,1)S(1)} collective-permute-done((bf16[4,2,16,640]{3,2,1,0:T(8,128)(2,1)S(1)}, bf16[4,2,16,640]{3,2,1,0:T(8,128)(2,1)S(1)}, u32[]{:S(2)}, u32[]{:S(2)}) %collective-permute-start.8) | collective-permute-done | bytes 163872 | tf_op jit(solution)/shard_map/ppermute | solution.py:42
  44.3 3.2 collective-permute-done.7
  47.5 3.6 collective-permute-done.6
  53.6 2.3 fusion.12.refs_2_.refs_3_
  55.9 8.4 %collective-permute-done.11 = bf16[128,2048]{1,0:T(8,128)(2,1)} collective-permute-done((bf16[128,2048]{1,0:T(8,128)(2,1)}, bf16[128,2048]{1,0:T(8,128)(2,1)}, u32[]{:S(2)}, u32[]{:S(2)}) %collective-permute-start.11) | collective-permute-done | bytes 524320 | tf_op jit(solution)/shard_map/ppermute | solution.py:60
  66.5 3.9 fusion.32.ci_ref.halo_ref
  70.4 7.4 %shard_map.305 = (bf16[512,640]{1,0:T(8,128)(2,1)}, f32[512,640]{1,0:T(8,128)}, bf16[512,640]{1,0:T(8,128)(2,1)}, f32[512,640]{1,0:T(8,128)S(1)}, f32[512,640]{1...) custom-call(f32[4,640]{1,0:T(4,128)S(1)} %slice.208.taps_ref, f32[1,640]{1,0:T(1,128)S(1)} %slice.210.shift_ref, ...), custom_call_target="tpu_custom_call" | custom-call | bytes 30000000 | tf_op jit(solution)/shard_map/pallas_call | solution.py:577
  79.1 2.3 collective-permute-start.19
  84.2 3.4 collective-permute-done.18.refs_2_
  89.7 2.0 collective-permute-start.20
  91.8 1.8 fusion.23.branch_ref
  96.0 1.8 fusion.29
  98.9 3.2 collective-permute-start.23
  102.1 11.9 %collective-permute-done.24 = bf16[128,2048]{1,0:T(8,128)(2,1)S(1)} collective-permute-done((bf16[128,2048]{1,0:T(8,128)(2,1)S(1)}, bf16[128,2048]{1,0:T(8,128)(2,1)S(1)}, u32[]{:S(2)}, u32[]{:S(2)}) %collective-permute-start.24) | collective-permute-done | bytes 524320 | tf_op jit(solution)/shard_map/ppermute | solution.py:60
  114.3 3.2 collective-permute-start.29
  118.4 6.4 %collective-permute-done.25 = bf16[128,2048]{1,0:T(8,128)(2,1)} collective-permute-done((bf16[128,2048]{1,0:T(8,128)(2,1)S(1)}, bf16[128,2048]{1,0:T(8,128)(2,1)}, u32[]{:S(2)}, u32[]{:S(2)}) %collective-permute-start.25) | collective-permute-done | bytes 524320 | tf_op jit(solution)/shard_map/ppermute | solution.py:60
  124.9 2.0 multiply_reduce_fusion.2
  127.1 3.2 collective-permute-start.26
  131.6 2.9 pad_maximum_fusion.lhs_two
  134.5 3.1 collective-permute-done.27
  137.8 2.1 collective-permute-done.26
  141.0 3.9 all-gather.5.cloned.1.call-done
  144.9 6.2 %fusion.6 = f32[512,1536]{1,0:T(8,128)S(1)} fusion(bf16[512,2048]{1,0:T(8,128)(2,1)} %pad_maximum_fusion.lhs_two, bf16[2048,4608]{1,0:T(8,128)(2,1)} %all-gather.5.cloned.1.call-done), kind=kOutput, calls=%fused_computation.10 | convolution fusion | flops 3221225472 | bytes 11534336 | tf_op jit(solution)/shard_map/dot_general | solution.py:152
  152.4 9.7 %fusion.2 = f32[512,3072]{1,0:T(8,128)S(1)} fusion(bf16[2048,4608]{1,0:T(8,128)(2,1)} %all-gather.5.cloned.1.call-done, bf16[128,2048]{1,0:T(8,128)(2,1)S(1)} %get-tuple-element.123, bf16[128,2048]{1,0:T(8,128)(2,1)} %collective-permute-done.28, bf16[128,2048]{1,0:T(8,128)(2,1)S(1)} %get-tuple-element.122, bf16[128,2048]{1,0:T(8,128)(2,1)S(1)} %copy-done.27), kind=kOutput, calls=%fused_computation.2 | convolution fusion | flops 6450839552 | bytes 20971520 | tf_op jit(solution)/shard_map/dot_general | solution.py:152
  162.2 2.6 multiply_convert_fusion
  164.8 13.6 %shard_map.308 = bf16[2048,4608]{1,0:T(8,128)(2,1)} custom-call(bf16[512,2048]{1,0:T(8,128)(2,1)S(1)} %pad_maximum_fusion.1.lhs_one, bf16[512,2048]{1,0:T(8,128)(2,1)S(1)} %copy-done.3, bf16[512,1536]{1,0:T(8,128)(2,1)S(1)} %get-tuple-element.66.rhs_one, bf16[512,1536]{1,0:T(8,128)(2,1)S(1)} %get-tuple-element.67.rhs_two, ...), custom_call_target="tpu_custom_call" | custom-call | flops 9663676416 | bytes 18874368 | tf_op jit(solution)/shard_map/pallas_call | solution.py:639
  180.7 10.7 %fusion = f32[512,2048]{1,0:T(8,128)S(1)} fusion(bf16[2048,4608]{1,0:T(8,128)(2,1)} %all-gather.5.cloned.1.call-done, bf16[512,1536]{1,0:T(8,128)(2,1)} %copy-done.5, bf16[512,1536]{1,0:T(8,128)(2,1)} %copy-done.6), kind=kOutput, calls=%fused_computation | convolution fusion | flops 6448742400 | bytes 19922944 | tf_op jit(solution)/shard_map/dot_general | solution.py:156
  191.6 1.7 collective-permute-start.30
  193.4 1.8 collective-permute-start.31
  195.2 11.0 %collective-permute-done.30 = bf16[128,2048]{1,0:T(8,128)(2,1)S(1)} collective-permute-done((bf16[128,2048]{1,0:T(8,128)(2,1)S(1)}, bf16[128,2048]{1,0:T(8,128)(2,1)S(1)}, u32[]{:S(2)}, u32[]{:S(2)}) %collective-permute-start.30) | collective-permute-done | bytes 524320 | tf_op jit(solution)/shard_map/ppermute | solution.py:60
  206.4 1.6 collective-permute-start.32
  208.0 8.8 %collective-permute-done.32 = bf16[128,2048]{1,0:T(8,128)(2,1)S(1)} collective-permute-done((bf16[128,2048]{1,0:T(8,128)(2,1)S(1)}, bf16[128,2048]{1,0:T(8,128)(2,1)S(1)}, u32[]{:S(2)}, u32[]{:S(2)}) %collective-permute-start.32) | collective-permute-done | bytes 524320 | tf_op jit(solution)/shard_map/ppermute | solution.py:60
  217.3 2.6 fusion.70
  220.2 2.9 collective-permute-start.33
  223.1 12.6 %collective-permute-done.34 = bf16[128,2048]{1,0:T(8,128)(2,1)S(1)} collective-permute-done((bf16[128,2048]{1,0:T(8,128)(2,1)S(1)}, bf16[128,2048]{1,0:T(8,128)(2,1)S(1)}, u32[]{:S(2)}, u32[]{:S(2)}) %collective-permute-start.34) | collective-permute-done | bytes 524320 | tf_op jit(solution)/shard_map/ppermute | solution.py:60
  235.7 8.3 %fusion.20 = bf16[512,2048]{1,0:T(8,128)(2,1)} fusion(bf16[512,1536]{1,0:T(8,128)(2,1)S(1)} %get-tuple-element.68.rhs_three, bf16[2048,4608]{1,0:T(8,128)(2,1)} %all-gather.5.cloned.1.call-done), kind=kOutput, calls=%fused_computation.27 | convolution fusion | flops 3222274048 | bytes 9961472 | tf_op jit(solution)/shard_map/dot_general | solution.py:156
  244.1 2.0 collective-permute-done.35
  246.1 3.8 fusion.27.grad_ref
  250.0 4.2 %shard_map.309 = (bf16[512,640]{1,0:T(8,128)(2,1)S(1)}, f32[8,640]{1,0:T(8,128)S(1)}) custom-call(f32[1,640]{1,0:T(1,128)S(1)} %fusion.58.soft_ref, f32[512,640]{1,0:T(8,128)S(1)} %fusion.27.grad_ref, f32[512,640]{1,0:T(8,128)} %copy-done, bf16[512,640]{1,0:T(8,128)(2,1)S(1)} %get-tuple-element.70.state_ref, f32[512,640]{1,0:T(8,128)} %get-tuple-element.71.rate_ref, ...), custom_call_target="tpu_custom_call" | custom-call | bytes 9500000 | tf_op jit(solution)/shard_map/pallas_call | solution.py:577
  258.5 2.5 collective-permute-start.37
  261.2 2.5 collective-permute-done.38.refs_2_
  267.6 2.4 collective-permute-start.40
  270.1 2.5 collective-permute-done.41.piece2
  272.7 10.1 %shard_map.311 = (bf16[512,1280]{1,0:T(8,128)(2,1)S(1)}, f32[512,640]{1,0:T(8,128)S(1)}, f32[64,640]{1,0:T(8,128)S(1)}, f32[8,640]{1,0:T(8,128)S(1)}) custom-call(s32[4]{0:T(128)S(1)} %pad_add_fusion.spot_ref, f32[8,640]{1,0:T(8,128)S(1)} %get-tuple-element.73.piece0, f32[8,640]{1,0:T(8,128)S(1)} %collective-permute-done.40.piece1, ...), custom_call_target="tpu_custom_call" | custom-call | bytes 40000000 | tf_op jit(solution)/shard_map/pallas_call | solution.py:577
  283.5 2.4 shard_map.312.refs_0_
  286.0 6.2 %shard_map.313 = (bf16[16,208,640]{2,1,0:T(8,128)(2,1)S(1)}, bf16[16,208,640]{2,1,0:T(8,128)(2,1)S(1)}) custom-call(s32[4]{0:T(128)S(1)} %pad_add_fusion.spot_ref, bf16[32,16,640]{2,1,0:T(8,128)(2,1)S(1)} %shard_map.312.refs_0_, bf16[512,2048]{1,0:T(8,128)(2,1)S(1)} %pad_maximum_fusion.2.refs_1_, bf16[576,2048]{1,0:T(8,128)(2,1)S(1)} %copy-done.2, ...), custom_call_target="tpu_custom_call" | custom-call | flops 4026531840 | tf_op jit(solution)/shard_map/pallas_call | solution.py:725
  293.2 5.7 %fusion.17 = bf16[512,2048]{1,0:T(8,128)(2,1)S(1)} fusion(bf16[2048,1920]{1,0:T(8,128)(2,1)} %all-gather.3.cloned.1.call-done, bf16[512,640]{1,0:T(8,128)(2,1)S(1)} %copy-done.10, bf16[512,640]{1,0:T(8,128)(2,1)S(1)} %bitcast.73), kind=kOutput, calls=%fused_computation.26 | convolution fusion | flops 2688024576 | bytes 8650752 | tf_op jit(solution)/shard_map/dot_general | solution.py:156
  300.1 3.2 add_convert_fusion
  304.4 9.5 %all-to-all-start = ((bf16[16,208,640]{2,1,0:T(8,128)(2,1)}), bf16[16,208,640]{2,1,0:T(8,128)(2,1)}, u32[]{:S(2)}, u32[]{:S(2)}) async-start(bf16[16,208,640]{2,1,0:T(8,128)(2,1)} %add_convert_fusion), calls=%async_computation | async-start | bytes 8519680 | tf_op jit(solution)/shard_map/all_to_all | solution.py:137
  313.9 3.2 collective-permute-start.45
  317.4 12.1 %collective-permute-done.45 = bf16[128,2048]{1,0:T(8,128)(2,1)S(1)} collective-permute-done((bf16[128,2048]{1,0:T(8,128)(2,1)}, bf16[128,2048]{1,0:T(8,128)(2,1)S(1)}, u32[]{:S(2)}, u32[]{:S(2)}) %collective-permute-start.45) | collective-permute-done | bytes 524320 | tf_op jit(solution)/shard_map/ppermute | solution.py:60
  330.8 3.2 collective-permute-start.48
  334.0 10.8 %collective-permute-done.49 = bf16[128,2048]{1,0:T(8,128)(2,1)S(1)} collective-permute-done((bf16[128,2048]{1,0:T(8,128)(2,1)S(1)}, bf16[128,2048]{1,0:T(8,128)(2,1)S(1)}, u32[]{:S(2)}, u32[]{:S(2)}) %collective-permute-start.49) | collective-permute-done | bytes 524320 | tf_op jit(solution)/shard_map/ppermute | solution.py:60
  346.5 9.1 %collective-permute-done.50 = bf16[128,2048]{1,0:T(8,128)(2,1)S(1)} collective-permute-done((bf16[128,2048]{1,0:T(8,128)(2,1)S(1)}, bf16[128,2048]{1,0:T(8,128)(2,1)S(1)}, u32[]{:S(2)}, u32[]{:S(2)}) %collective-permute-start.50) | collective-permute-done | bytes 524320 | tf_op jit(solution)/shard_map/ppermute | solution.py:60
  356.7 23.0 %all-to-all-done = bf16[16,208,640]{2,1,0:T(8,128)(2,1)} async-done(((bf16[16,208,640]{2,1,0:T(8,128)(2,1)}), bf16[16,208,640]{2,1,0:T(8,128)(2,1)}, u32[]{:S(2)}, u32[]{:S(2)}) %all-to-all-start) | async-done | bytes 4259872 | tf_op jit(solution)/shard_map/all_to_all | solution.py:137
  379.7 2.9 convert_reduce_fusion
  383.7 2.0 collective-permute-start.51
  389.8 2.1 convert_bitcast_fusion
  (256 shorter events, 63.9 us)
Async XLA Ops:
  7.2 59.3 %all-gather.3.cloned.1.call-start = ((), (), s32[]{:S(2)}) async-start(), calls=%async_computation.2 | async-start | bytes 8110080 | tf_op jit(solution)/shard_map/all_gather | solution.py:786
  8.9 136.0 %all-gather.5.cloned.1.call-start = ((), (), s32[]{:S(2)}) async-start(), calls=%async_computation.3 | async-start | bytes 19464192 | tf_op jit(solution)/shard_map/all_gather | solution.py:811
  9.0 14.9 %collective-permute-start.5 = (bf16[128,2048]{1,0:T(8,128)(2,1)}, bf16[128,2048]{1,0:T(8,128)(2,1)S(1)}, u32[]{:S(2)}, u32[]{:S(2)}) collective-permute-start(bf16[128,2048]{1,0:T(8,128)(2,1)} %param.18), channel_id=1, source_target_pairs={{0,32},{1,97},{2,34},{3,99},{4,36},{5,101},{6,38},{7,103},{8,40},{... | collective-permute-start | bytes 1572872 | tf_op jit(solution)/shard_map/ppermute | solution.py:60
  10.6 22.2 %collective-permute-start.4 = (bf16[128,2048]{1,0:T(8,128)(2,1)}, bf16[128,2048]{1,0:T(8,128)(2,1)S(1)}, u32[]{:S(2)}, u32[]{:S(2)}) collective-permute-start(bf16[128,2048]{1,0:T(8,128)(2,1)} %param.18), channel_id=1, source_target_pairs={{0,96},{1,33},{2,98},{3,35},{4,100},{5,37},{6,102},{7,39},{8,104},... | collective-permute-start | bytes 1572872 | tf_op jit(solution)/shard_map/ppermute | solution.py:60
  15.5 2.1 collective-permute-start
  18.2 5.7 %collective-permute-start.2 = (bf16[2,16,640]{2,1,0:T(8,128)(2,1)}, bf16[2,16,640]{2,1,0:T(8,128)(2,1)S(1)}, u32[]{:S(2)}, u32[]{:S(2)}) collective-permute-start(bf16[2,16,640]{2,1,0:T(8,128)(2,1)} %get-tuple-element.138), channel_id=1, source_target_pairs={{0,4},{1,5},{2,6},{3,7},{4,0},{5,1},{6,2},{7,3},{8,12},{9,13},{10,... | collective-permute-start | bytes 122888 | tf_op jit(solution)/shard_map/ppermute | solution.py:42
  18.2 7.2 %collective-permute-start.1 = (bf16[2,16,640]{2,1,0:T(8,128)(2,1)}, bf16[2,16,640]{2,1,0:T(8,128)(2,1)}, u32[]{:S(2)}, u32[]{:S(2)}) collective-permute-start(bf16[2,16,640]{2,1,0:T(8,128)(2,1)} %get-tuple-element.138), channel_id=1, source_target_pairs={{0,6},{1,7},{2,0},{3,1},{4,2},{5,3},{6,4},{7,5},{8,14},{9,15},{10,... | collective-permute-start | bytes 122888 | tf_op jit(solution)/shard_map/ppermute | solution.py:42
  21.3 5.0 %collective-permute-start.3 = (bf16[2,16,640]{2,1,0:T(8,128)(2,1)}, bf16[2,16,640]{2,1,0:T(8,128)(2,1)}, u32[]{:S(2)}, u32[]{:S(2)}) collective-permute-start(bf16[2,16,640]{2,1,0:T(8,128)(2,1)} %get-tuple-element.138), channel_id=1, source_target_pairs={{0,2},{1,3},{2,4},{3,5},{4,6},{5,7},{6,0},{7,1},{8,10},{9,11},{10,... | collective-permute-start | bytes 122888 | tf_op jit(solution)/shard_map/ppermute | solution.py:42
  23.9 4.2 %collective-permute-start.12 = (bf16[16,2048]{1,0:T(8,128)(2,1)S(1)}, bf16[16,2048]{1,0:T(8,128)(2,1)S(1)}, u32[]{:S(2)}, u32[]{:S(2)}) collective-permute-start(bf16[16,2048]{1,0:T(8,128)(2,1)S(1)} %slice.218), channel_id=1, source_target_pairs={{0,1},{1,2},{2,3},{3,4},{4,5},{5,6},{6,7},{7,8},{8,9},{9,10},{10,1... | collective-permute-start | bytes 196616 | tf_op jit(solution)/shard_map/ppermute | solution.py:790
  23.9 11.8 %collective-permute-start.9 = (bf16[128,2048]{1,0:T(8,128)(2,1)S(1)}, bf16[128,2048]{1,0:T(8,128)(2,1)S(1)}, u32[]{:S(2)}, u32[]{:S(2)}) collective-permute-start(bf16[128,2048]{1,0:T(8,128)(2,1)S(1)} %collective-permute-done.5), channel_id=1, source_target_pairs={{0,32},{1,97},{2,34},{3,99},{4,36},{5,101},{6,38},{7,103},{8,40},{... | collective-permute-start | bytes 1572872 | tf_op jit(solution)/shard_map/ppermute | solution.py:60
  28.1 11.3 %collective-permute-start.15 = (bf16[16,2048]{1,0:T(8,128)(2,1)S(1)}, bf16[16,2048]{1,0:T(8,128)(2,1)S(1)}, u32[]{:S(2)}, u32[]{:S(2)}) collective-permute-start(bf16[16,2048]{1,0:T(8,128)(2,1)S(1)} %collective-permute-done.12), channel_id=1, source_target_pairs={{0,32},{32,64},{64,96},{96,0},{1,33},{33,65},{65,97},{97,1},{2,34}... | collective-permute-start | bytes 196616 | tf_op jit(solution)/shard_map/ppermute | solution.py:25
  29.6 9.5 %collective-permute-start.14 = (bf16[16,2048]{1,0:T(8,128)(2,1)S(1)}, bf16[16,2048]{1,0:T(8,128)(2,1)S(1)}, u32[]{:S(2)}, u32[]{:S(2)}) collective-permute-start(bf16[16,2048]{1,0:T(8,128)(2,1)S(1)} %collective-permute-done.12), channel_id=1, source_target_pairs={{0,64},{32,96},{64,0},{96,32},{1,65},{33,97},{65,1},{97,33},{2,66}... | collective-permute-start | bytes 196616 | tf_op jit(solution)/shard_map/ppermute | solution.py:25
  31.8 6.1 %collective-permute-start.13 = (bf16[16,2048]{1,0:T(8,128)(2,1)S(1)}, bf16[16,2048]{1,0:T(8,128)(2,1)S(1)}, u32[]{:S(2)}, u32[]{:S(2)}) collective-permute-start(bf16[16,2048]{1,0:T(8,128)(2,1)S(1)} %collective-permute-done.12), channel_id=1, source_target_pairs={{0,96},{32,0},{64,32},{96,64},{1,97},{33,1},{65,33},{97,65},{2,98}... | collective-permute-start | bytes 196616 | tf_op jit(solution)/shard_map/ppermute | solution.py:25
  35.9 8.4 %collective-permute-start.8 = (bf16[4,2,16,640]{3,2,1,0:T(8,128)(2,1)S(1)}, bf16[4,2,16,640]{3,2,1,0:T(8,128)(2,1)S(1)}, u32[]{:S(2)}, u32[]{:S(2)}) collective-permute-start(bf16[4,2,16,640]{3,2,1,0:T(8,128)(2,1)S(1)} %pad_maximum_fusion.7), channel_id=1, source_target_pairs={{0,8},{1,9},{2,10},{3,11},{4,12},{5,13},{6,14},{7,15},{8,16},{9,17... | collective-permute-start | bytes 491528 | tf_op jit(solution)/shard_map/ppermute | solution.py:42
  37.4 10.1 %collective-permute-start.7 = (bf16[4,2,16,640]{3,2,1,0:T(8,128)(2,1)S(1)}, bf16[4,2,16,640]{3,2,1,0:T(8,128)(2,1)S(1)}, u32[]{:S(2)}, u32[]{:S(2)}) collective-permute-start(bf16[4,2,16,640]{3,2,1,0:T(8,128)(2,1)S(1)} %pad_maximum_fusion.7), channel_id=1, source_target_pairs={{0,16},{1,17},{2,18},{3,19},{4,20},{5,21},{6,22},{7,23},{8,24},{9,... | collective-permute-start | bytes 491528 | tf_op jit(solution)/shard_map/ppermute | solution.py:42
  37.9 13.2 %collective-permute-start.6 = (bf16[4,2,16,640]{3,2,1,0:T(8,128)(2,1)S(1)}, bf16[4,2,16,640]{3,2,1,0:T(8,128)(2,1)S(1)}, u32[]{:S(2)}, u32[]{:S(2)}) collective-permute-start(bf16[4,2,16,640]{3,2,1,0:T(8,128)(2,1)S(1)} %pad_maximum_fusion.7), channel_id=1, source_target_pairs={{0,24},{1,25},{2,26},{3,27},{4,28},{5,29},{6,30},{7,31},{8,0},{9,1... | collective-permute-start | bytes 491528 | tf_op jit(solution)/shard_map/ppermute | solution.py:42
  39.2 14.4 %collective-permute-start.10 = (bf16[128,2048]{1,0:T(8,128)(2,1)}, bf16[128,2048]{1,0:T(8,128)(2,1)}, u32[]{:S(2)}, u32[]{:S(2)}) collective-permute-start(bf16[128,2048]{1,0:T(8,128)(2,1)} %param.35), channel_id=1, source_target_pairs={{0,32},{1,97},{2,34},{3,99},{4,36},{5,101},{6,38},{7,103},{8,40},{... | collective-permute-start | bytes 1572872 | tf_op jit(solution)/shard_map/ppermute | solution.py:60
  53.6 10.7 %collective-permute-start.11 = (bf16[128,2048]{1,0:T(8,128)(2,1)}, bf16[128,2048]{1,0:T(8,128)(2,1)}, u32[]{:S(2)}, u32[]{:S(2)}) collective-permute-start(bf16[128,2048]{1,0:T(8,128)(2,1)} %collective-permute-done.10), channel_id=1, source_target_pairs={{0,32},{1,97},{2,34},{3,99},{4,36},{5,101},{6,38},{7,103},{8,40},{... | collective-permute-start | bytes 1572872 | tf_op jit(solution)/shard_map/ppermute | solution.py:60
  55.9 35.9 %copy-start.1 = (bf16[576,2048]{1,0:T(8,128)(2,1)}, bf16[576,2048]{1,0:T(8,128)(2,1)S(1)}, u32[]{:S(2)}) copy-start(bf16[576,2048]{1,0:T(8,128)(2,1)S(1)} %fusion.12.refs_2_.refs_3_) | copy-start | bytes 7077892
  64.3 325.5 %reduce-scatter.2.cloned.1.call-start = ((), (), s32[]{:S(2)}) async-start(), calls=%async_computation.4 | async-start | bytes 19464192 | tf_op jit(solution)/shard_map/reduce_scatter | solution.py:884
  77.9 1.3 collective-permute-start.16
  79.1 5.1 %collective-permute-start.19 = (f32[2,8,640]{2,1,0:T(8,128)S(1)}, f32[2,8,640]{2,1,0:T(8,128)S(1)}, u32[]{:S(2)}, u32[]{:S(2)}) collective-permute-start(f32[2,8,640]{2,1,0:T(8,128)S(1)} %pad_maximum_fusion.9.refs_0_), channel_id=1, source_target_pairs={{0,2},{1,3},{2,4},{3,5},{4,6},{5,7},{6,0},{7,1},{8,10},{9,11},{10,... | collective-permute-start | bytes 122888 | tf_op jit(solution)/shard_map/ppermute | solution.py:42
  81.4 6.1 %collective-permute-start.18 = (f32[2,8,640]{2,1,0:T(8,128)S(1)}, f32[2,8,640]{2,1,0:T(8,128)S(1)}, u32[]{:S(2)}, u32[]{:S(2)}) collective-permute-start(f32[2,8,640]{2,1,0:T(8,128)S(1)} %pad_maximum_fusion.9.refs_0_), channel_id=1, source_target_pairs={{0,4},{1,5},{2,6},{3,7},{4,0},{5,1},{6,2},{7,3},{8,12},{9,13},{10,... | collective-permute-start | bytes 122888 | tf_op jit(solution)/shard_map/ppermute | solution.py:42
  81.6 6.2 %collective-permute-start.17 = (f32[2,8,640]{2,1,0:T(8,128)S(1)}, f32[2,8,640]{2,1,0:T(8,128)S(1)}, u32[]{:S(2)}, u32[]{:S(2)}) collective-permute-start(f32[2,8,640]{2,1,0:T(8,128)S(1)} %pad_maximum_fusion.9.refs_0_), channel_id=1, source_target_pairs={{0,6},{1,7},{2,0},{3,1},{4,2},{5,3},{6,4},{7,5},{8,14},{9,15},{10,... | collective-permute-start | bytes 122888 | tf_op jit(solution)/shard_map/ppermute | solution.py:42
  88.4 5.2 %collective-permute-start.22 = (f32[8,640]{1,0:T(8,128)S(1)}, f32[8,640]{1,0:T(8,128)S(1)}, u32[]{:S(2)}, u32[]{:S(2)}) collective-permute-start(f32[8,640]{1,0:T(8,128)S(1)} %get-tuple-element.58.piece0), channel_id=1, source_target_pairs={{0,8},{1,9},{2,10},{3,11},{4,12},{5,13},{6,14},{7,15},{8,16},{9,17... | collective-permute-start | bytes 61448 | tf_op jit(solution)/shard_map/ppermute | solution.py:42
  89.2 5.3 %collective-permute-start.21 = (f32[8,640]{1,0:T(8,128)S(1)}, f32[8,640]{1,0:T(8,128)S(1)}, u32[]{:S(2)}, u32[]{:S(2)}) collective-permute-start(f32[8,640]{1,0:T(8,128)S(1)} %get-tuple-element.58.piece0), channel_id=1, source_target_pairs={{0,16},{1,17},{2,18},{3,19},{4,20},{5,21},{6,22},{7,23},{8,24},{9,... | collective-permute-start | bytes 61448 | tf_op jit(solution)/shard_map/ppermute | solution.py:42
  89.7 4.9 %collective-permute-start.20 = (f32[8,640]{1,0:T(8,128)S(1)}, f32[8,640]{1,0:T(8,128)S(1)}, u32[]{:S(2)}, u32[]{:S(2)}) collective-permute-start(f32[8,640]{1,0:T(8,128)S(1)} %get-tuple-element.58.piece0), channel_id=1, source_target_pairs={{0,24},{1,25},{2,26},{3,27},{4,28},{5,29},{6,30},{7,31},{8,0},{9,1... | collective-permute-start | bytes 61448 | tf_op jit(solution)/shard_map/ppermute | solution.py:42
  97.9 27.0 %copy-start.15 = (bf16[128,2048]{1,0:T(8,128)(2,1)S(1)}, bf16[128,2048]{1,0:T(8,128)(2,1)}, u32[]{:S(2)}) copy-start(bf16[128,2048]{1,0:T(8,128)(2,1)} %param.18) | copy-start | bytes 1572868
  98.9 15.2 %collective-permute-start.24 = (bf16[128,2048]{1,0:T(8,128)(2,1)S(1)}, bf16[128,2048]{1,0:T(8,128)(2,1)S(1)}, u32[]{:S(2)}, u32[]{:S(2)}) collective-permute-start(bf16[128,2048]{1,0:T(8,128)(2,1)S(1)} %get-tuple-element.115), channel_id=1, source_target_pairs={{0,32},{1,97},{2,34},{3,99},{4,36},{5,101},{6,38},{7,103},{8,40},{... | collective-permute-start | bytes 1572872 | tf_op jit(solution)/shard_map/ppermute | solution.py:60
  98.9 18.8 %collective-permute-start.23 = (bf16[128,2048]{1,0:T(8,128)(2,1)}, bf16[128,2048]{1,0:T(8,128)(2,1)S(1)}, u32[]{:S(2)}, u32[]{:S(2)}) collective-permute-start(bf16[128,2048]{1,0:T(8,128)(2,1)} %get-tuple-element.114), channel_id=1, source_target_pairs={{0,96},{1,33},{2,98},{3,35},{4,100},{5,37},{6,102},{7,39},{8,104},... | collective-permute-start | bytes 1572872 | tf_op jit(solution)/shard_map/ppermute | solution.py:60
  114.3 10.6 %collective-permute-start.25 = (bf16[128,2048]{1,0:T(8,128)(2,1)S(1)}, bf16[128,2048]{1,0:T(8,128)(2,1)}, u32[]{:S(2)}, u32[]{:S(2)}) collective-permute-start(bf16[128,2048]{1,0:T(8,128)(2,1)S(1)} %add_convert_fusion.6), channel_id=1, source_target_pairs={{0,32},{1,97},{2,34},{3,99},{4,36},{5,101},{6,38},{7,103},{8,40},{... | collective-permute-start | bytes 1572872 | tf_op jit(solution)/shard_map/ppermute | solution.py:60
  114.3 16.0 %collective-permute-start.29 = (bf16[128,2048]{1,0:T(8,128)(2,1)}, bf16[128,2048]{1,0:T(8,128)(2,1)}, u32[]{:S(2)}, u32[]{:S(2)}) collective-permute-start(bf16[128,2048]{1,0:T(8,128)(2,1)} %param.35), channel_id=1, source_target_pairs={{0,96},{1,33},{2,98},{3,35},{4,100},{5,37},{6,102},{7,39},{8,104},... | collective-permute-start | bytes 1572872 | tf_op jit(solution)/shard_map/ppermute | solution.py:60
  127.1 10.6 %collective-permute-start.27 = (bf16[128,2048]{1,0:T(8,128)(2,1)S(1)}, bf16[128,2048]{1,0:T(8,128)(2,1)}, u32[]{:S(2)}, u32[]{:S(2)}) collective-permute-start(bf16[128,2048]{1,0:T(8,128)(2,1)S(1)} %multiply_convert_fusion.3), channel_id=1, source_target_pairs={{0,32},{1,97},{2,34},{3,99},{4,36},{5,101},{6,38},{7,103},{8,40},{... | collective-permute-start | bytes 1572872 | tf_op jit(solution)/shard_map/ppermute | solution.py:60
  127.1 12.7 %collective-permute-start.26 = (bf16[128,2048]{1,0:T(8,128)(2,1)S(1)}, bf16[128,2048]{1,0:T(8,128)(2,1)S(1)}, u32[]{:S(2)}, u32[]{:S(2)}) collective-permute-start(bf16[128,2048]{1,0:T(8,128)(2,1)S(1)} %multiply_convert_fusion.3), channel_id=1, source_target_pairs={{0,96},{1,33},{2,98},{3,35},{4,100},{5,37},{6,102},{7,39},{8,104},... | collective-permute-start | bytes 1572872 | tf_op jit(solution)/shard_map/ppermute | solution.py:60
  137.6 13.5 %collective-permute-start.28 = (bf16[128,2048]{1,0:T(8,128)(2,1)}, bf16[128,2048]{1,0:T(8,128)(2,1)}, u32[]{:S(2)}, u32[]{:S(2)}) collective-permute-start(bf16[128,2048]{1,0:T(8,128)(2,1)} %collective-permute-done.27), channel_id=1, source_target_pairs={{0,32},{1,97},{2,34},{3,99},{4,36},{5,101},{6,38},{7,103},{8,40},{... | collective-permute-start | bytes 1572872 | tf_op jit(solution)/shard_map/ppermute | solution.py:60
  191.6 14.5 %collective-permute-start.30 = (bf16[128,2048]{1,0:T(8,128)(2,1)S(1)}, bf16[128,2048]{1,0:T(8,128)(2,1)S(1)}, u32[]{:S(2)}, u32[]{:S(2)}) collective-permute-start(bf16[128,2048]{1,0:T(8,128)(2,1)S(1)} %get-tuple-element.113), channel_id=1, source_target_pairs={{0,32},{1,97},{2,34},{3,99},{4,36},{5,101},{6,38},{7,103},{8,40},{... | collective-permute-start | bytes 1572872 | tf_op jit(solution)/shard_map/ppermute | solution.py:60
  193.4 14.6 %collective-permute-start.31 = (bf16[128,2048]{1,0:T(8,128)(2,1)S(1)}, bf16[128,2048]{1,0:T(8,128)(2,1)S(1)}, u32[]{:S(2)}, u32[]{:S(2)}) collective-permute-start(bf16[128,2048]{1,0:T(8,128)(2,1)S(1)} %get-tuple-element.112), channel_id=1, source_target_pairs={{0,96},{1,33},{2,98},{3,35},{4,100},{5,37},{6,102},{7,39},{8,104},... | collective-permute-start | bytes 1572872 | tf_op jit(solution)/shard_map/ppermute | solution.py:60
  206.4 10.5 %collective-permute-start.32 = (bf16[128,2048]{1,0:T(8,128)(2,1)S(1)}, bf16[128,2048]{1,0:T(8,128)(2,1)S(1)}, u32[]{:S(2)}, u32[]{:S(2)}) collective-permute-start(bf16[128,2048]{1,0:T(8,128)(2,1)S(1)} %add_convert_fusion.5), channel_id=1, source_target_pairs={{0,32},{1,97},{2,34},{3,99},{4,36},{5,101},{6,38},{7,103},{8,40},{... | collective-permute-start | bytes 1572872 | tf_op jit(solution)/shard_map/ppermute | solution.py:60
  219.9 26.2 %copy-start.20 = (bf16[128,2048]{1,0:T(8,128)(2,1)}, bf16[128,2048]{1,0:T(8,128)(2,1)S(1)}, u32[]{:S(2)}) copy-start(bf16[128,2048]{1,0:T(8,128)(2,1)S(1)} %get-tuple-element.101) | copy-start | bytes 1572868
  219.9 15.8 %collective-permute-start.34 = (bf16[128,2048]{1,0:T(8,128)(2,1)S(1)}, bf16[128,2048]{1,0:T(8,128)(2,1)S(1)}, u32[]{:S(2)}, u32[]{:S(2)}) collective-permute-start(bf16[128,2048]{1,0:T(8,128)(2,1)S(1)} %get-tuple-element.101), channel_id=1, source_target_pairs={{0,32},{1,97},{2,34},{3,99},{4,36},{5,101},{6,38},{7,103},{8,40},{... | collective-permute-start | bytes 1572872 | tf_op jit(solution)/shard_map/ppermute | solution.py:60
  220.2 23.8 %collective-permute-start.33 = (bf16[128,2048]{1,0:T(8,128)(2,1)S(1)}, bf16[128,2048]{1,0:T(8,128)(2,1)S(1)}, u32[]{:S(2)}, u32[]{:S(2)}) collective-permute-start(bf16[128,2048]{1,0:T(8,128)(2,1)S(1)} %get-tuple-element.101), channel_id=1, source_target_pairs={{0,96},{1,33},{2,98},{3,35},{4,100},{5,37},{6,102},{7,39},{8,104},... | collective-permute-start | bytes 1572872 | tf_op jit(solution)/shard_map/ppermute | solution.py:60
  235.7 10.4 %collective-permute-start.35 = (bf16[128,2048]{1,0:T(8,128)(2,1)S(1)}, bf16[128,2048]{1,0:T(8,128)(2,1)S(1)}, u32[]{:S(2)}, u32[]{:S(2)}) collective-permute-start(bf16[128,2048]{1,0:T(8,128)(2,1)S(1)} %collective-permute-done.34), channel_id=1, source_target_pairs={{0,32},{1,97},{2,34},{3,99},{4,36},{5,101},{6,38},{7,103},{8,40},{... | collective-permute-start | bytes 1572872 | tf_op jit(solution)/shard_map/ppermute | solution.py:60
  255.0 1.2 collective-permute-start.36
  256.2 5.0 %collective-permute-start.39 = (f32[2,8,640]{2,1,0:T(8,128)S(1)}, f32[2,8,640]{2,1,0:T(8,128)S(1)}, u32[]{:S(2)}, u32[]{:S(2)}) collective-permute-start(f32[2,8,640]{2,1,0:T(8,128)S(1)} %pad_maximum_fusion.10.refs_0_), channel_id=1, source_target_pairs={{0,2},{1,3},{2,4},{3,5},{4,6},{5,7},{6,0},{7,1},{8,10},{9,11},{10,... | collective-permute-start | bytes 122888 | tf_op jit(solution)/shard_map/ppermute | solution.py:42
  257.2 6.4 %collective-permute-start.38 = (f32[2,8,640]{2,1,0:T(8,128)S(1)}, f32[2,8,640]{2,1,0:T(8,128)S(1)}, u32[]{:S(2)}, u32[]{:S(2)}) collective-permute-start(f32[2,8,640]{2,1,0:T(8,128)S(1)} %pad_maximum_fusion.10.refs_0_), channel_id=1, source_target_pairs={{0,4},{1,5},{2,6},{3,7},{4,0},{5,1},{6,2},{7,3},{8,12},{9,13},{10,... | collective-permute-start | bytes 122888 | tf_op jit(solution)/shard_map/ppermute | solution.py:42
  258.5 6.5 %collective-permute-start.37 = (f32[2,8,640]{2,1,0:T(8,128)S(1)}, f32[2,8,640]{2,1,0:T(8,128)S(1)}, u32[]{:S(2)}, u32[]{:S(2)}) collective-permute-start(f32[2,8,640]{2,1,0:T(8,128)S(1)} %pad_maximum_fusion.10.refs_0_), channel_id=1, source_target_pairs={{0,6},{1,7},{2,0},{3,1},{4,2},{5,3},{6,4},{7,5},{8,14},{9,15},{10,... | collective-permute-start | bytes 122888 | tf_op jit(solution)/shard_map/ppermute | solution.py:42
  265.5 4.6 %collective-permute-start.42 = (f32[8,640]{1,0:T(8,128)S(1)}, f32[8,640]{1,0:T(8,128)S(1)}, u32[]{:S(2)}, u32[]{:S(2)}) collective-permute-start(f32[8,640]{1,0:T(8,128)S(1)} %get-tuple-element.73.piece0), channel_id=1, source_target_pairs={{0,8},{1,9},{2,10},{3,11},{4,12},{5,13},{6,14},{7,15},{8,16},{9,17... | collective-permute-start | bytes 61448 | tf_op jit(solution)/shard_map/ppermute | solution.py:42
  266.8 5.9 %collective-permute-start.41 = (f32[8,640]{1,0:T(8,128)S(1)}, f32[8,640]{1,0:T(8,128)S(1)}, u32[]{:S(2)}, u32[]{:S(2)}) collective-permute-start(f32[8,640]{1,0:T(8,128)S(1)} %get-tuple-element.73.piece0), channel_id=1, source_target_pairs={{0,16},{1,17},{2,18},{3,19},{4,20},{5,21},{6,22},{7,23},{8,24},{9,... | collective-permute-start | bytes 61448 | tf_op jit(solution)/shard_map/ppermute | solution.py:42
  267.6 5.2 %collective-permute-start.40 = (f32[8,640]{1,0:T(8,128)S(1)}, f32[8,640]{1,0:T(8,128)S(1)}, u32[]{:S(2)}, u32[]{:S(2)}) collective-permute-start(f32[8,640]{1,0:T(8,128)S(1)} %get-tuple-element.73.piece0), channel_id=1, source_target_pairs={{0,24},{1,25},{2,26},{3,27},{4,28},{5,29},{6,30},{7,31},{8,0},{9,1... | collective-permute-start | bytes 61448 | tf_op jit(solution)/shard_map/ppermute | solution.py:42
  282.8 3.0 collective-permute-start.43
  292.2 7.9 %collective-permute-start.44 = (bf16[16,208,640]{2,1,0:T(8,128)(2,1)S(1)}, bf16[16,208,640]{2,1,0:T(8,128)(2,1)S(1)}, u32[]{:S(2)}, u32[]{:S(2)}) collective-permute-start(bf16[16,208,640]{2,1,0:T(8,128)(2,1)S(1)} %get-tuple-element.84), channel_id=1, source_target_pairs={{0,1},{1,0},{2,3},{3,2},{4,5},{5,4},{6,7},{7,6},{8,9},{9,8},{10,11... | collective-permute-start | bytes 12779528 | tf_op jit(solution)/shard_map/ppermute | solution.py:42
  304.4 12.7 %collective-permute-start.46 = (bf16[128,2048]{1,0:T(8,128)(2,1)}, bf16[128,2048]{1,0:T(8,128)(2,1)S(1)}, u32[]{:S(2)}, u32[]{:S(2)}) collective-permute-start(bf16[128,2048]{1,0:T(8,128)(2,1)} %get-tuple-element.119), channel_id=1, source_target_pairs={{0,32},{1,97},{2,34},{3,99},{4,36},{5,101},{6,38},{7,103},{8,40},{... | collective-permute-start | bytes 1572872 | tf_op jit(solution)/shard_map/ppermute | solution.py:60
  304.4 75.3 %all-to-all-start = ((bf16[16,208,640]{2,1,0:T(8,128)(2,1)}), bf16[16,208,640]{2,1,0:T(8,128)(2,1)}, u32[]{:S(2)}, u32[]{:S(2)}) async-start(bf16[16,208,640]{2,1,0:T(8,128)(2,1)} %add_convert_fusion), calls=%async_computation | async-start | bytes 8519680 | tf_op jit(solution)/shard_map/all_to_all | solution.py:137
  313.9 15.6 %collective-permute-start.45 = (bf16[128,2048]{1,0:T(8,128)(2,1)}, bf16[128,2048]{1,0:T(8,128)(2,1)S(1)}, u32[]{:S(2)}, u32[]{:S(2)}) collective-permute-start(bf16[128,2048]{1,0:T(8,128)(2,1)} %get-tuple-element.118), channel_id=1, source_target_pairs={{0,96},{1,33},{2,98},{3,35},{4,100},{5,37},{6,102},{7,39},{8,104},... | collective-permute-start | bytes 1572872 | tf_op jit(solution)/shard_map/ppermute | solution.py:60
  317.3 12.7 %collective-permute-start.47 = (bf16[128,2048]{1,0:T(8,128)(2,1)S(1)}, bf16[128,2048]{1,0:T(8,128)(2,1)S(1)}, u32[]{:S(2)}, u32[]{:S(2)}) collective-permute-start(bf16[128,2048]{1,0:T(8,128)(2,1)S(1)} %add_convert_fusion.4), channel_id=1, source_target_pairs={{0,32},{1,97},{2,34},{3,99},{4,36},{5,101},{6,38},{7,103},{8,40},{... | collective-permute-start | bytes 1572872 | tf_op jit(solution)/shard_map/ppermute | solution.py:60
  330.7 14.1 %collective-permute-start.49 = (bf16[128,2048]{1,0:T(8,128)(2,1)S(1)}, bf16[128,2048]{1,0:T(8,128)(2,1)S(1)}, u32[]{:S(2)}, u32[]{:S(2)}) collective-permute-start(bf16[128,2048]{1,0:T(8,128)(2,1)S(1)} %get-tuple-element.117), channel_id=1, source_target_pairs={{0,32},{1,97},{2,34},{3,99},{4,36},{5,101},{6,38},{7,103},{8,40},{... | collective-permute-start | bytes 1572872 | tf_op jit(solution)/shard_map/ppermute | solution.py:60
  330.8 15.7 %collective-permute-start.48 = (bf16[128,2048]{1,0:T(8,128)(2,1)S(1)}, bf16[128,2048]{1,0:T(8,128)(2,1)S(1)}, u32[]{:S(2)}, u32[]{:S(2)}) collective-permute-start(bf16[128,2048]{1,0:T(8,128)(2,1)S(1)} %get-tuple-element.116), channel_id=1, source_target_pairs={{0,96},{1,33},{2,98},{3,35},{4,100},{5,37},{6,102},{7,39},{8,104},... | collective-permute-start | bytes 1572872 | tf_op jit(solution)/shard_map/ppermute | solution.py:60
  345.1 10.5 %collective-permute-start.50 = (bf16[128,2048]{1,0:T(8,128)(2,1)S(1)}, bf16[128,2048]{1,0:T(8,128)(2,1)S(1)}, u32[]{:S(2)}, u32[]{:S(2)}) collective-permute-start(bf16[128,2048]{1,0:T(8,128)(2,1)S(1)} %add_convert_fusion.3), channel_id=1, source_target_pairs={{0,32},{1,97},{2,34},{3,99},{4,36},{5,101},{6,38},{7,103},{8,40},{... | collective-permute-start | bytes 1572872 | tf_op jit(solution)/shard_map/ppermute | solution.py:60
  356.6 25.9 %copy-start.32 = (bf16[64,640]{1,0:T(8,128)(2,1)S(1)}, bf16[64,640]{1,0:T(8,128)(2,1)}, u32[]{:S(2)}) copy-start(bf16[64,640]{1,0:T(8,128)(2,1)} %param.21) | copy-start | bytes 245764
  356.7 26.8 %copy-start.33 = (bf16[64]{0:T(256)(128)(2,1)S(1)}, bf16[64]{0:T(256)(128)(2,1)}, u32[]{:S(2)}) copy-start(bf16[64]{0:T(256)(128)(2,1)} %param.19) | copy-start | bytes 388
  356.7 29.6 %copy-start.34 = (bf16[20]{0:T(256)(128)(2,1)S(1)}, bf16[20]{0:T(256)(128)(2,1)}, u32[]{:S(2)}) copy-start(bf16[20]{0:T(256)(128)(2,1)} %param.28) | copy-start | bytes 124
  383.6 5.2 %collective-permute-start.53 = (f32[1,128]{1,0:T(1,128)S(1)}, f32[1,128]{1,0:T(1,128)S(1)}, u32[]{:S(2)}, u32[]{:S(2)}) collective-permute-start(f32[1,128]{1,0:T(1,128)S(1)} %maximum_bitcast_fusion), channel_id=1, source_target_pairs={{0,64},{32,96},{64,0},{96,32},{1,65},{33,97},{65,1},{97,33},{2,66}... | collective-permute-start | bytes 1544 | tf_op jit(solution)/shard_map/ppermute | solution.py:25
  383.6 5.1 %collective-permute-start.52 = (f32[1,128]{1,0:T(1,128)S(1)}, f32[1,128]{1,0:T(1,128)S(1)}, u32[]{:S(2)}, u32[]{:S(2)}) collective-permute-start(f32[1,128]{1,0:T(1,128)S(1)} %maximum_bitcast_fusion), channel_id=1, source_target_pairs={{0,96},{32,0},{64,32},{96,64},{1,97},{33,1},{65,33},{97,65},{2,98}... | collective-permute-start | bytes 1544 | tf_op jit(solution)/shard_map/ppermute | solution.py:25
  383.7 5.5 %collective-permute-start.51 = (f32[1,128]{1,0:T(1,128)S(1)}, f32[1,128]{1,0:T(1,128)S(1)}, u32[]{:S(2)}, u32[]{:S(2)}) collective-permute-start(f32[1,128]{1,0:T(1,128)S(1)} %maximum_bitcast_fusion), channel_id=1, source_target_pairs={{0,32},{32,64},{64,96},{96,0},{1,33},{33,65},{65,97},{97,1},{2,34}... | collective-permute-start | bytes 1544 | tf_op jit(solution)/shard_map/ppermute | solution.py:25
  (31 other events, 306.0 us)
Sparse Core Ops, SparseCore 0:
  10.8 53.8 all-gather.2
  67.0 77.8 all-gather.4
  180.8 122.3 reduce-scatter.1

commit v3 on v2

--- a/solution.py
+++ b/solution.py
@@ -179,11 +179,11 @@
     return 1.0 / (1.0 + jnp.exp(-values))
 
 
-def one_minus_exp(values):
+def one_minus_square(keeps, values):
     series = 1.0 + values * (1.0 / 6.0)
     for order in (5.0, 4.0, 3.0, 2.0):
         series = 1.0 + values * series * (1.0 / order)
-    return jnp.where(values > -0.1, -values * series, 1.0 - jnp.exp(values))
+    return jnp.where(values > -0.1, -values * series, 1.0 - keeps * keeps)
 
 
 def inverse_root(values):
@@ -271,8 +271,9 @@
             entries = 0.5 * jnp.tanh(0.5 * pre_ref[rows, channels:]) + 0.5
             log_keep = -soft_ref[...] * rates
             resets = place_ref[rows, :] == 0
-            coeff = jnp.where(resets, 0.0, jnp.exp(log_keep))
-            squared = one_minus_exp(2.0 * log_keep)
+            keeps = jnp.exp(log_keep)
+            coeff = jnp.where(resets, 0.0, keeps)
+            squared = one_minus_square(keeps, 2.0 * log_keep)
             scaling = jnp.where(resets, 1.0, squared * inverse_root(squared))
             value = entries * exact_ref[rows, :] * scaling
             for distance in (1, 2, 4):
@@ -385,7 +386,7 @@
         reach = row_ids < 8 - distance
         value = value + coeff * jnp.where(reach, pltpu.roll(value, 8 - distance, 0), 0.0)
         coeff = coeff * jnp.where(reach, pltpu.roll(coeff, 8 - distance, 0), 1.0)
-    return value + coeff * later, sgrad, coeff
+    return value + coeff * later, sgrad, coeff, keeps
 
 
 def local_backward_kernel(
@@ -411,7 +412,7 @@
             rows = rows_at(base + 8 * part, 8)
             gated, slope = gelu_parts(branch_ref[rows, :])
             slopes.append(slope * grad_ref[rows, :] * states[8 * part : 8 * part + 8])
-            held, _, coeff = reverse_scan(
+            held, _, coeff, _ = reverse_scan(
                 rows, later, gated, grad_ref, rate_ref, place_ref, soft_ref, row_ids
             )
             cum, later = coeff[0:1] * cum, held[0:1]
@@ -479,7 +480,7 @@
             first = base + 8 * part
             rows = rows_at(first, 8)
             gated, _ = gelu_parts(branch_ref[rows, :])
-            held, sgrad, _ = reverse_scan(
+            held, sgrad, _, keeps = reverse_scan(
                 rows, later, gated, grad_ref, rate_ref, place_ref, soft_ref, row_ids
             )
             adjoint = sgrad + jnp.where(row_ids == 7, later, pltpu.roll(held, 7, 0))
@@ -490,7 +491,7 @@
             rates, entries, conv = rate_ref[rows, :], all_entries[half], convs[half]
             resets = place_ref[rows, :] == 0
             log_keep = -soft_ref[...] * rates
-            squared = one_minus_exp(2.0 * log_keep)
+            squared = one_minus_square(keeps, 2.0 * log_keep)
             inverse = inverse_root(squared)
             scaling = jnp.where(resets, 1.0, squared * inverse)
             turn = jnp.where(resets, 0.0, (1.0 - squared) * inverse)
@@ -712,28 +713,27 @@
         theirs_ref[chip, at, :] = jnp.where(core == 0, high, low).astype(bf16)
 
 
-def outer_halves(spots, small, lhs, rhs):
+def outer_halves(spots, small, lhs, rhs, part):
     count = len(lhs)
-    features = lhs[0].shape[1]
     rows, columns = rhs[0].shape
     height = 1024
     chips = height // 128
     extra = SMALL if small is not None else 0
     total = 64 * count + extra
-    shape = jax.ShapeDtypeStruct((features // 128, total, columns), bf16)
-    out_spec = pl.BlockSpec((chips, total, columns), lambda i: (i, 0, 0))
+    shape = jax.ShapeDtypeStruct((chips, total, columns), bf16)
+    out_spec = pl.BlockSpec((chips, total, columns), lambda i: (0, 0, 0))
     return pl.pallas_call(
         functools.partial(halves_kernel, count, extra),
-        grid=(features // height,),
+        grid=(1,),
         in_specs=[pl.BlockSpec(memory_space=pltpu.SMEM)]
-        + [pl.BlockSpec((2 * chips, SMALL, columns), lambda i: (i, 0, 0))] * (extra > 0)
-        + [pl.BlockSpec((rows, height), lambda i: (0, i))] * count
+        + [pl.BlockSpec((2 * chips, SMALL, columns), lambda i: (part, 0, 0))] * (extra > 0)
+        + [pl.BlockSpec((rows, height), lambda i: (0, part))] * count
         + [pl.BlockSpec((rows, columns), lambda i: (0, 0))] * count,
         out_specs=[out_spec] * 2,
         out_shape=[shape] * 2,
         compiler_params=pltpu.CompilerParams(vmem_limit_bytes=28 * 1024 * 1024),
         cost_estimate=pl.CostEstimate(
-            flops=2 * count * rows * features * columns,
+            flops=2 * count * rows * height * columns,
             bytes_accessed=0,
             transcendentals=0,
         ),
@@ -866,7 +866,7 @@
         return [values[j * OWN : (j + 1) * OWN] for j in range(MEMBERS)]
 
     own_values = inputs.astype(f32)
-    middle = own_values + ring_scatter(rows_of(product_back(mixture, out_turned)), spot[2])
+    middle = own_values + ring_scatter(rows_of(product_back(mixture, out_turned, bf16)), spot[2])
 
     factor_two = norm_factor(middle)
     normed_two = (middle * factor_two * feed_gain).astype(bf16)
@@ -883,7 +883,7 @@
     feed_shares = feed_outer(wide_two, cotangent_all, (gate_grad, up_grad, hidden))
     feed_grads = lax.psum_scatter(feed_shares, "tok", scatter_dimension=0, tiled=True)
     gate_late, up_late = after((gate_grad, up_grad), feed_shares)
-    two_shares = product_back(jnp.concatenate([gate_late, up_late], axis=1), gate_up_all)
+    two_shares = product_back(jnp.concatenate([gate_late, up_late], axis=1), gate_up_all, bf16)
     two_parts = rows_of(two_shares)
     two_far, two_near = ring_open(two_parts, spot[2])
     two_grad = ring_close(two_parts, two_near, ring_pass(two_parts, two_far, spot[2]))
@@ -945,13 +945,19 @@
     )(conv, pregrads, sums, feed_rows)
 
     core = spot[2]
-    weight_mine, weight_theirs = outer_halves(
-        spots, small_rows, (middle_wide, wide_one, wide_one), (mixture, branch_grad, input_low)
-    )
-    weight_other = hop(weight_theirs, "core", 1)
-    late = after(input_low, weight_theirs)
+    chips_one, chips_two = [
+        outer_halves(
+            spots, small_rows, (middle_wide, wide_one, wide_one), (mixture, branch_grad, low), part
+        )
+        for part, low in enumerate((input_low, input_low))
+    ]
+    other_one = hop(chips_one[1], "core", 1)
+    other_two = hop(chips_two[1], "core", 1)
+    late = after(input_low, chips_two[1])
     one_shares = product_back(jnp.concatenate([late, branch_grad], axis=1), project_all, bf16)
-    weight_chip = narrow_sum(weight_mine, weight_other)
+    weight_chip = jnp.concatenate(
+        [narrow_sum(chips_one[0], other_one), narrow_sum(chips_two[0], other_two)], axis=0
+    )
     one_shares = after(one_shares, weight_chip)
     one_parts = rows_of(one_shares)
     one_grad = ring_scatter(one_parts, core)

time: 407 us -> 405 us (level)
  waiting for transfers between devices: 159 us -> 154 us
    unnamed x80 -> x100, local copies, waits for them, and re-layouts: 5.34 us -> 9.88 us
    ppermute x22 -> x23, waiting for transfers between devices: 27.9 us -> 30.3 us  [hop_tok(): return lax.ppermute(values, 'tok', route)]
    ppermute x22 -> x23, starting transfers between devices: 23.9 us -> 22.4 us  [hop_tok(): return lax.ppermute(values, 'tok', route)]
  transfers between devices with their start and end apart: 58 -> 59, of which waited for: 37 -> 34; matrix products, arithmetic and copies ran while one was open for 22% -> 21% of each run, Pallas kernels for 8% -> 8%
where the time goes in v3:
time: 405 us; the launch traced here: 397 us
  waiting for transfers between devices  154 us (38%)
  starting transfers between devices  68.8 us (17%)
  matrix products  48.8 us (12%)
  Pallas kernels  47.2 us (12%)
  other arithmetic  45.8 us (11%)
  local copies, waits for them, and re-layouts  17 us (4%)
  between operations  15.5 us (4%)
    ppermute x24, waiting for transfers between devices, hop_apart(): return lax.ppermute(values, ('blk', 'tok'), route)  101 us
    ppermute x23, waiting for transfers between devices, hop_tok(): return lax.ppermute(values, 'tok', route)  30.3 us
    ppermute x24, starting transfers between devices, hop_apart(): return lax.ppermute(values, ('blk', 'tok'), route)  29.4 us
    dot_general x5, matrix products, product(): return jnp.dot(operand, weight, preferred_element_type=f32).astype(out)  25.6 us
    pallas_call x4, Pallas kernels, by_slot(): pl.pallas_call(kernel, grid=(MEMBERS,), in_specs=[pl.BlockSpec(memory_spa...  23.7 us
    dot_general x4, matrix products, product_back(): lax.dot_general(operand, weight, (((1,), (1,)), ((), ())), preferred_elem...  23.3 us
    ppermute x23, starting transfers between devices, hop_tok(): return lax.ppermute(values, 'tok', route)  22.4 us
    all_to_all x1, waiting for transfers between devices, chips_sum(): lax.all_to_all(values, 'tok', 0, 0, axis_index_groups=cores, tiled=True)  20.6 us
  transfers between devices with their start and end apart: 59, of which 34 were waited for; matrix products, arithmetic and copies ran while one was open for 21% of the time, Pallas kernels for 8%

profile of v3, /device:TPU:80, one launch (start us, length us, event | category | flops | bytes accessed | tf_op | source)
XLA Modules:
  0.0 397.0 jit_solution(13331690073913690780)
XLA Ops:
  7.2 1.7 pad_maximum_fusion.7
  10.6 1.7 collective-permute-start.4
  15.7 2.0 pad_maximum_fusion.5
  18.3 3.1 collective-permute-start.1
  21.6 2.4 collective-permute-done.5
  29.9 2.2 collective-permute-start.14
  33.9 2.0 collective-permute-done.9
  40.0 3.2 collective-permute-done.8
  43.2 4.7 %collective-permute-done.7 = bf16[4,2,16,640]{3,2,1,0:T(8,128)(2,1)S(1)} collective-permute-done((bf16[4,2,16,640]{3,2,1,0:T(8,128)(2,1)S(1)}, bf16[4,2,16,640]{3,2,1,0:T(8,128)(2,1)S(1)}, u32[]{:S(2)}, u32[]{:S(2)}) %collective-permute-start.7) | collective-permute-done | bytes 163872 | tf_op jit(solution)/shard_map/ppermute | solution.py:42
  47.9 4.0 %collective-permute-done.6 = bf16[4,2,16,640]{3,2,1,0:T(8,128)(2,1)S(1)} collective-permute-done((bf16[4,2,16,640]{3,2,1,0:T(8,128)(2,1)S(1)}, bf16[4,2,16,640]{3,2,1,0:T(8,128)(2,1)S(1)}, u32[]{:S(2)}, u32[]{:S(2)}) %collective-permute-start.6) | collective-permute-done | bytes 163872 | tf_op jit(solution)/shard_map/ppermute | solution.py:42
  54.4 2.5 fusion.12.refs_2_.refs_3_
  56.9 7.9 %collective-permute-done.11 = bf16[128,2048]{1,0:T(8,128)(2,1)} collective-permute-done((bf16[128,2048]{1,0:T(8,128)(2,1)S(1)}, bf16[128,2048]{1,0:T(8,128)(2,1)}, u32[]{:S(2)}, u32[]{:S(2)}) %collective-permute-start.11) | collective-permute-done | bytes 524320 | tf_op jit(solution)/shard_map/ppermute | solution.py:60
  66.9 3.9 fusion.36.ci_ref.halo_ref
  70.8 7.4 %shard_map.305 = (bf16[512,640]{1,0:T(8,128)(2,1)}, f32[512,640]{1,0:T(8,128)}, bf16[512,640]{1,0:T(8,128)(2,1)}, f32[512,640]{1,0:T(8,128)S(1)}, f32[512,640]{1...) custom-call(f32[4,640]{1,0:T(4,128)S(1)} %slice.206.taps_ref, f32[1,640]{1,0:T(1,128)S(1)} %slice.208.shift_ref, ...), custom_call_target="tpu_custom_call" | custom-call | bytes 30000000 | tf_op jit(solution)/shard_map/pallas_call | solution.py:578
  79.5 1.7 collective-permute-start.18
  81.6 3.8 collective-permute-done.19.refs_3_
  85.4 2.6 collective-permute-done.17.refs_1_
  91.3 1.8 fusion.28.branch_ref
  93.1 1.9 collective-permute-done.21.piece2
  98.4 1.8 convolution_convert_fusion
  101.2 3.2 collective-permute-start.23
  104.4 10.7 %collective-permute-done.24 = bf16[128,2048]{1,0:T(8,128)(2,1)S(1)} collective-permute-done((bf16[128,2048]{1,0:T(8,128)(2,1)S(1)}, bf16[128,2048]{1,0:T(8,128)(2,1)S(1)}, u32[]{:S(2)}, u32[]{:S(2)}) %collective-permute-start.24) | collective-permute-done | bytes 524320 | tf_op jit(solution)/shard_map/ppermute | solution.py:60
  116.2 3.2 collective-permute-start.29
  119.5 7.4 %collective-permute-done.25 = bf16[128,2048]{1,0:T(8,128)(2,1)} collective-permute-done((bf16[128,2048]{1,0:T(8,128)(2,1)}, bf16[128,2048]{1,0:T(8,128)(2,1)}, u32[]{:S(2)}, u32[]{:S(2)}) %collective-permute-start.25) | collective-permute-done | bytes 524320 | tf_op jit(solution)/shard_map/ppermute | solution.py:60
  126.9 2.2 multiply_reduce_fusion.2
  130.5 3.0 collective-permute-start.26
  134.8 2.8 pad_maximum_fusion.1.lhs_two
  137.6 3.2 collective-permute-done.27
  141.3 2.9 collective-permute-done.26
  144.1 2.1 broadcast_select_fusion.8
  146.2 6.3 %fusion.6 = f32[512,1536]{1,0:T(8,128)S(1)} fusion(bf16[512,2048]{1,0:T(8,128)(2,1)} %pad_maximum_fusion.1.lhs_two, bf16[2048,4608]{1,0:T(8,128)(2,1)} %all-gather.5.cloned.1.call-done), kind=kOutput, calls=%fused_computation.9 | convolution fusion | flops 3221225472 | bytes 11534336 | tf_op jit(solution)/shard_map/dot_general | solution.py:152
  153.9 9.8 %fusion.2 = f32[512,3072]{1,0:T(8,128)S(1)} fusion(bf16[2048,4608]{1,0:T(8,128)(2,1)} %all-gather.5.cloned.1.call-done, bf16[128,2048]{1,0:T(8,128)(2,1)S(1)} %copy-done.30, bf16[128,2048]{1,0:T(8,128)(2,1)} %collective-permute-done.28, bf16[128,2048]{1,0:T(8,128)(2,1)S(1)} %copy-done.29, bf16[128,2048]{1,0:T(8,128)(2,1)S(1)} %copy-done.32), kind=kOutput, calls=%fused_computation.2 | convolution fusion | flops 6450839552 | bytes 20971520 | tf_op jit(solution)/shard_map/dot_general | solution.py:152
  163.7 2.6 multiply_convert_fusion
  166.3 13.6 %shard_map.308 = bf16[2048,4608]{1,0:T(8,128)(2,1)} custom-call(bf16[512,2048]{1,0:T(8,128)(2,1)S(1)} %pad_maximum_fusion.2.lhs_one, bf16[512,2048]{1,0:T(8,128)(2,1)S(1)} %copy-done.10, bf16[512,1536]{1,0:T(8,128)(2,1)S(1)} %get-tuple-element.68.rhs_one, bf16[512,1536]{1,0:T(8,128)(2,1)S(1)} %get-tuple-element.69.rhs_two, ...), custom_call_target="tpu_custom_call" | custom-call | flops 9663676416 | bytes 18874368 | tf_op jit(solution)/shard_map/pallas_call | solution.py:640
  183.4 10.7 %fusion.23 = bf16[512,2048]{1,0:T(8,128)(2,1)S(1)} fusion(bf16[2048,4608]{1,0:T(8,128)(2,1)} %all-gather.5.cloned.1.call-done, bf16[512,1536]{1,0:T(8,128)(2,1)} %copy-done.14, bf16[512,1536]{1,0:T(8,128)(2,1)} %copy-done.15), kind=kOutput, calls=%fused_computation.31 | convolution fusion | flops 6449790976 | bytes 17825792 | tf_op jit(solution)/shard_map/dot_general | solution.py:156
  194.8 3.4 collective-permute-start.31
  198.2 12.2 %collective-permute-done.30 = bf16[128,2048]{1,0:T(8,128)(2,1)S(1)} collective-permute-done((bf16[128,2048]{1,0:T(8,128)(2,1)S(1)}, bf16[128,2048]{1,0:T(8,128)(2,1)S(1)}, u32[]{:S(2)}, u32[]{:S(2)}) %collective-permute-start.30) | collective-permute-done | bytes 524320 | tf_op jit(solution)/shard_map/ppermute | solution.py:60
  210.8 10.4 %collective-permute-done.32 = bf16[128,2048]{1,0:T(8,128)(2,1)S(1)} collective-permute-done((bf16[128,2048]{1,0:T(8,128)(2,1)S(1)}, bf16[128,2048]{1,0:T(8,128)(2,1)S(1)}, u32[]{:S(2)}, u32[]{:S(2)}) %collective-permute-start.32) | collective-permute-done | bytes 524320 | tf_op jit(solution)/shard_map/ppermute | solution.py:60
  221.6 2.7 fusion.72
  224.3 3.2 collective-permute-start.33
  227.6 7.2 %collective-permute-done.34 = bf16[128,2048]{1,0:T(8,128)(2,1)S(1)} collective-permute-done((bf16[128,2048]{1,0:T(8,128)(2,1)S(1)}, bf16[128,2048]{1,0:T(8,128)(2,1)S(1)}, u32[]{:S(2)}, u32[]{:S(2)}) %collective-permute-start.34) | collective-permute-done | bytes 524320 | tf_op jit(solution)/shard_map/ppermute | solution.py:60
  234.7 7.6 %fusion.20 = bf16[512,2048]{1,0:T(8,128)(2,1)} fusion(bf16[512,1536]{1,0:T(8,128)(2,1)S(1)} %copy-done.13, bf16[2048,4608]{1,0:T(8,128)(2,1)} %all-gather.5.cloned.1.call-done), kind=kOutput, calls=%fused_computation.29 | convolution fusion | flops 3222274048 | bytes 9961472 | tf_op jit(solution)/shard_map/dot_general | solution.py:156
  242.4 2.7 collective-permute-done.35
  245.1 3.8 fusion.32.grad_ref
  249.0 4.6 %shard_map.309 = (bf16[512,640]{1,0:T(8,128)(2,1)S(1)}, f32[8,640]{1,0:T(8,128)S(1)}) custom-call(f32[1,640]{1,0:T(1,128)S(1)} %fusion.60.soft_ref, f32[512,640]{1,0:T(8,128)S(1)} %fusion.32.grad_ref, f32[512,640]{1,0:T(8,128)} %copy-done, bf16[512,640]{1,0:T(8,128)(2,1)S(1)} %copy-done.8, f32[512,640]{1,0:T(8,128)} %get-tuple-element.73.rate_ref, ...), custom_call_target="tpu_custom_call" | custom-call | bytes 9500000 | tf_op jit(solution)/shard_map/pallas_call | solution.py:578
  258.9 2.5 collective-permute-start.37
  261.4 2.4 collective-permute-done.38.refs_2_
  267.7 1.8 collective-permute-start.40
  270.1 2.1 collective-permute-done.41.piece2
  275.0 10.2 %shard_map.311 = (bf16[512,1280]{1,0:T(8,128)(2,1)S(1)}, f32[512,640]{1,0:T(8,128)S(1)}, f32[64,640]{1,0:T(8,128)S(1)}, f32[8,640]{1,0:T(8,128)S(1)}) custom-call(s32[4]{0:T(128)S(1)} %pad_add_fusion.spot_ref, f32[8,640]{1,0:T(8,128)S(1)} %get-tuple-element.75.piece0, f32[8,640]{1,0:T(8,128)S(1)} %collective-permute-done.40.piece1, ...), custom_call_target="tpu_custom_call" | custom-call | bytes 40000000 | tf_op jit(solution)/shard_map/pallas_call | solution.py:578
  285.9 2.3 shard_map.312.refs_0_
  288.4 3.2 shard_map.314
  292.7 3.2 shard_map.313
  296.1 3.1 fusion.17
  300.9 2.5 pad_maximum_fusion
  304.2 9.8 %all-to-all-start = ((bf16[16,208,640]{2,1,0:T(8,128)(2,1)}), bf16[16,208,640]{2,1,0:T(8,128)(2,1)}, u32[]{:S(2)}, u32[]{:S(2)}) async-start(bf16[16,208,640]{2,1,0:T(8,128)(2,1)} %pad_maximum_fusion), calls=%async_computation | async-start | bytes 8519680 | tf_op jit(solution)/shard_map/all_to_all | solution.py:137
  314.0 3.3 collective-permute-start.46
  317.7 11.2 %collective-permute-done.46 = bf16[128,2048]{1,0:T(8,128)(2,1)S(1)} collective-permute-done((bf16[128,2048]{1,0:T(8,128)(2,1)S(1)}, bf16[128,2048]{1,0:T(8,128)(2,1)S(1)}, u32[]{:S(2)}, u32[]{:S(2)}) %collective-permute-start.46) | collective-permute-done | bytes 524320 | tf_op jit(solution)/shard_map/ppermute | solution.py:60
  330.2 3.4 collective-permute-start.49
  333.6 11.1 %collective-permute-done.50 = bf16[128,2048]{1,0:T(8,128)(2,1)S(1)} collective-permute-done((bf16[128,2048]{1,0:T(8,128)(2,1)S(1)}, bf16[128,2048]{1,0:T(8,128)(2,1)S(1)}, u32[]{:S(2)}, u32[]{:S(2)}) %collective-permute-start.50) | collective-permute-done | bytes 524320 | tf_op jit(solution)/shard_map/ppermute | solution.py:60
  346.4 9.1 %collective-permute-done.51 = bf16[128,2048]{1,0:T(8,128)(2,1)S(1)} collective-permute-done((bf16[128,2048]{1,0:T(8,128)(2,1)S(1)}, bf16[128,2048]{1,0:T(8,128)(2,1)S(1)}, u32[]{:S(2)}, u32[]{:S(2)}) %collective-permute-start.51) | collective-permute-done | bytes 524320 | tf_op jit(solution)/shard_map/ppermute | solution.py:60
  356.6 20.6 %all-to-all-done = bf16[16,208,640]{2,1,0:T(8,128)(2,1)} async-done(((bf16[16,208,640]{2,1,0:T(8,128)(2,1)}), bf16[16,208,640]{2,1,0:T(8,128)(2,1)}, u32[]{:S(2)}, u32[]{:S(2)}) %all-to-all-start) | async-done | bytes 4259872 | tf_op jit(solution)/shard_map/all_to_all | solution.py:137
  377.2 2.9 convert_reduce_fusion
  387.9 2.1 convert_bitcast_fusion
  (282 shorter events, 70.8 us)
Async XLA Ops:
  7.2 59.6 %all-gather.3.cloned.1.call-start = ((), (), s32[]{:S(2)}) async-start(), calls=%async_computation.2 | async-start | bytes 8110080 | tf_op jit(solution)/shard_map/all_gather | solution.py:786
  9.0 137.2 %all-gather.5.cloned.1.call-start = ((), (), s32[]{:S(2)}) async-start(), calls=%async_computation.3 | async-start | bytes 19464192 | tf_op jit(solution)/shard_map/all_gather | solution.py:811
  9.0 14.9 %collective-permute-start.5 = (bf16[128,2048]{1,0:T(8,128)(2,1)}, bf16[128,2048]{1,0:T(8,128)(2,1)S(1)}, u32[]{:S(2)}, u32[]{:S(2)}) collective-permute-start(bf16[128,2048]{1,0:T(8,128)(2,1)} %param.18), channel_id=1, source_target_pairs={{0,32},{1,97},{2,34},{3,99},{4,36},{5,101},{6,38},{7,103},{8,40},{... | collective-permute-start | bytes 1572872 | tf_op jit(solution)/shard_map/ppermute | solution.py:60
  10.6 22.2 %collective-permute-start.4 = (bf16[128,2048]{1,0:T(8,128)(2,1)}, bf16[128,2048]{1,0:T(8,128)(2,1)}, u32[]{:S(2)}, u32[]{:S(2)}) collective-permute-start(bf16[128,2048]{1,0:T(8,128)(2,1)} %param.18), channel_id=1, source_target_pairs={{0,96},{1,33},{2,98},{3,35},{4,100},{5,37},{6,102},{7,39},{8,104},... | collective-permute-start | bytes 1572872 | tf_op jit(solution)/shard_map/ppermute | solution.py:60
  15.6 2.1 collective-permute-start
  18.3 5.8 %collective-permute-start.2 = (bf16[2,16,640]{2,1,0:T(8,128)(2,1)}, bf16[2,16,640]{2,1,0:T(8,128)(2,1)S(1)}, u32[]{:S(2)}, u32[]{:S(2)}) collective-permute-start(bf16[2,16,640]{2,1,0:T(8,128)(2,1)} %get-tuple-element.142), channel_id=1, source_target_pairs={{0,4},{1,5},{2,6},{3,7},{4,0},{5,1},{6,2},{7,3},{8,12},{9,13},{10,... | collective-permute-start | bytes 122888 | tf_op jit(solution)/shard_map/ppermute | solution.py:42
  18.3 7.2 %collective-permute-start.1 = (bf16[2,16,640]{2,1,0:T(8,128)(2,1)}, bf16[2,16,640]{2,1,0:T(8,128)(2,1)}, u32[]{:S(2)}, u32[]{:S(2)}) collective-permute-start(bf16[2,16,640]{2,1,0:T(8,128)(2,1)} %get-tuple-element.142), channel_id=1, source_target_pairs={{0,6},{1,7},{2,0},{3,1},{4,2},{5,3},{6,4},{7,5},{8,14},{9,15},{10,... | collective-permute-start | bytes 122888 | tf_op jit(solution)/shard_map/ppermute | solution.py:42
  21.4 5.0 %collective-permute-start.3 = (bf16[2,16,640]{2,1,0:T(8,128)(2,1)}, bf16[2,16,640]{2,1,0:T(8,128)(2,1)}, u32[]{:S(2)}, u32[]{:S(2)}) collective-permute-start(bf16[2,16,640]{2,1,0:T(8,128)(2,1)} %get-tuple-element.142), channel_id=1, source_target_pairs={{0,2},{1,3},{2,4},{3,5},{4,6},{5,7},{6,0},{7,1},{8,10},{9,11},{10,... | collective-permute-start | bytes 122888 | tf_op jit(solution)/shard_map/ppermute | solution.py:42
  24.0 4.4 %collective-permute-start.12 = (bf16[16,2048]{1,0:T(8,128)(2,1)S(1)}, bf16[16,2048]{1,0:T(8,128)(2,1)S(1)}, u32[]{:S(2)}, u32[]{:S(2)}) collective-permute-start(bf16[16,2048]{1,0:T(8,128)(2,1)S(1)} %slice.216), channel_id=1, source_target_pairs={{0,1},{1,2},{2,3},{3,4},{4,5},{5,6},{6,7},{7,8},{8,9},{9,10},{10,1... | collective-permute-start | bytes 196616 | tf_op jit(solution)/shard_map/ppermute | solution.py:790
  24.1 11.8 %collective-permute-start.9 = (bf16[128,2048]{1,0:T(8,128)(2,1)S(1)}, bf16[128,2048]{1,0:T(8,128)(2,1)S(1)}, u32[]{:S(2)}, u32[]{:S(2)}) collective-permute-start(bf16[128,2048]{1,0:T(8,128)(2,1)S(1)} %collective-permute-done.5), channel_id=1, source_target_pairs={{0,32},{1,97},{2,34},{3,99},{4,36},{5,101},{6,38},{7,103},{8,40},{... | collective-permute-start | bytes 1572872 | tf_op jit(solution)/shard_map/ppermute | solution.py:60
  28.3 11.1 %collective-permute-start.15 = (bf16[16,2048]{1,0:T(8,128)(2,1)S(1)}, bf16[16,2048]{1,0:T(8,128)(2,1)S(1)}, u32[]{:S(2)}, u32[]{:S(2)}) collective-permute-start(bf16[16,2048]{1,0:T(8,128)(2,1)S(1)} %collective-permute-done.12), channel_id=1, source_target_pairs={{0,32},{32,64},{64,96},{96,0},{1,33},{33,65},{65,97},{97,1},{2,34}... | collective-permute-start | bytes 196616 | tf_op jit(solution)/shard_map/ppermute | solution.py:25
  29.9 9.4 %collective-permute-start.14 = (bf16[16,2048]{1,0:T(8,128)(2,1)S(1)}, bf16[16,2048]{1,0:T(8,128)(2,1)S(1)}, u32[]{:S(2)}, u32[]{:S(2)}) collective-permute-start(bf16[16,2048]{1,0:T(8,128)(2,1)S(1)} %collective-permute-done.12), channel_id=1, source_target_pairs={{0,64},{32,96},{64,0},{96,32},{1,65},{33,97},{65,1},{97,33},{2,66}... | collective-permute-start | bytes 196616 | tf_op jit(solution)/shard_map/ppermute | solution.py:25
  32.1 5.9 %collective-permute-start.13 = (bf16[16,2048]{1,0:T(8,128)(2,1)S(1)}, bf16[16,2048]{1,0:T(8,128)(2,1)S(1)}, u32[]{:S(2)}, u32[]{:S(2)}) collective-permute-start(bf16[16,2048]{1,0:T(8,128)(2,1)S(1)} %collective-permute-done.12), channel_id=1, source_target_pairs={{0,96},{32,0},{64,32},{96,64},{1,97},{33,1},{65,33},{97,65},{2,98}... | collective-permute-start | bytes 196616 | tf_op jit(solution)/shard_map/ppermute | solution.py:25
  36.1 7.1 %collective-permute-start.8 = (bf16[4,2,16,640]{3,2,1,0:T(8,128)(2,1)S(1)}, bf16[4,2,16,640]{3,2,1,0:T(8,128)(2,1)S(1)}, u32[]{:S(2)}, u32[]{:S(2)}) collective-permute-start(bf16[4,2,16,640]{3,2,1,0:T(8,128)(2,1)S(1)} %pad_maximum_fusion.8), channel_id=1, source_target_pairs={{0,8},{1,9},{2,10},{3,11},{4,12},{5,13},{6,14},{7,15},{8,16},{9,17... | collective-permute-start | bytes 491528 | tf_op jit(solution)/shard_map/ppermute | solution.py:42
  37.5 10.4 %collective-permute-start.7 = (bf16[4,2,16,640]{3,2,1,0:T(8,128)(2,1)S(1)}, bf16[4,2,16,640]{3,2,1,0:T(8,128)(2,1)S(1)}, u32[]{:S(2)}, u32[]{:S(2)}) collective-permute-start(bf16[4,2,16,640]{3,2,1,0:T(8,128)(2,1)S(1)} %pad_maximum_fusion.8), channel_id=1, source_target_pairs={{0,16},{1,17},{2,18},{3,19},{4,20},{5,21},{6,22},{7,23},{8,24},{9,... | collective-permute-start | bytes 491528 | tf_op jit(solution)/shard_map/ppermute | solution.py:42
  38.0 13.9 %collective-permute-start.6 = (bf16[4,2,16,640]{3,2,1,0:T(8,128)(2,1)S(1)}, bf16[4,2,16,640]{3,2,1,0:T(8,128)(2,1)S(1)}, u32[]{:S(2)}, u32[]{:S(2)}) collective-permute-start(bf16[4,2,16,640]{3,2,1,0:T(8,128)(2,1)S(1)} %pad_maximum_fusion.8), channel_id=1, source_target_pairs={{0,24},{1,25},{2,26},{3,27},{4,28},{5,29},{6,30},{7,31},{8,0},{9,1... | collective-permute-start | bytes 491528 | tf_op jit(solution)/shard_map/ppermute | solution.py:42
  39.3 15.0 %collective-permute-start.10 = (bf16[128,2048]{1,0:T(8,128)(2,1)}, bf16[128,2048]{1,0:T(8,128)(2,1)S(1)}, u32[]{:S(2)}, u32[]{:S(2)}) collective-permute-start(bf16[128,2048]{1,0:T(8,128)(2,1)} %param.35), channel_id=1, source_target_pairs={{0,32},{1,97},{2,34},{3,99},{4,36},{5,101},{6,38},{7,103},{8,40},{... | collective-permute-start | bytes 1572872 | tf_op jit(solution)/shard_map/ppermute | solution.py:60
  54.4 10.5 %collective-permute-start.11 = (bf16[128,2048]{1,0:T(8,128)(2,1)S(1)}, bf16[128,2048]{1,0:T(8,128)(2,1)}, u32[]{:S(2)}, u32[]{:S(2)}) collective-permute-start(bf16[128,2048]{1,0:T(8,128)(2,1)S(1)} %collective-permute-done.10), channel_id=1, source_target_pairs={{0,32},{1,97},{2,34},{3,99},{4,36},{5,101},{6,38},{7,103},{8,40},{... | collective-permute-start | bytes 1572872 | tf_op jit(solution)/shard_map/ppermute | solution.py:60
  64.9 323.0 %reduce-scatter.2.cloned.1.call-start = ((), (), s32[]{:S(2)}) async-start(), calls=%async_computation.4 | async-start | bytes 19464192 | tf_op jit(solution)/shard_map/reduce_scatter | solution.py:884
  66.8 24.4 %copy-start.43 = (bf16[2048,1920]{1,0:T(8,128)(2,1)S(1)}, bf16[2048,1920]{1,0:T(8,128)(2,1)}, u32[]{:S(2)}) copy-start(bf16[2048,1920]{1,0:T(8,128)(2,1)} %all-gather.3.cloned.1.call-done) | copy-start | bytes 23592964
  78.2 1.3 collective-permute-start.16
  79.5 5.9 %collective-permute-start.19 = (f32[2,8,640]{2,1,0:T(8,128)S(1)}, f32[2,8,640]{2,1,0:T(8,128)S(1)}, u32[]{:S(2)}, u32[]{:S(2)}) collective-permute-start(f32[2,8,640]{2,1,0:T(8,128)S(1)} %pad_maximum_fusion.10.refs_0_), channel_id=1, source_target_pairs={{0,2},{1,3},{2,4},{3,5},{4,6},{5,7},{6,0},{7,1},{8,10},{9,11},{10,... | collective-permute-start | bytes 122888 | tf_op jit(solution)/shard_map/ppermute | solution.py:42
  79.5 5.9 %collective-permute-start.18 = (f32[2,8,640]{2,1,0:T(8,128)S(1)}, f32[2,8,640]{2,1,0:T(8,128)S(1)}, u32[]{:S(2)}, u32[]{:S(2)}) collective-permute-start(f32[2,8,640]{2,1,0:T(8,128)S(1)} %pad_maximum_fusion.10.refs_0_), channel_id=1, source_target_pairs={{0,4},{1,5},{2,6},{3,7},{4,0},{5,1},{6,2},{7,3},{8,12},{9,13},{10,... | collective-permute-start | bytes 122888 | tf_op jit(solution)/shard_map/ppermute | solution.py:42
  81.2 6.7 %collective-permute-start.17 = (f32[2,8,640]{2,1,0:T(8,128)S(1)}, f32[2,8,640]{2,1,0:T(8,128)S(1)}, u32[]{:S(2)}, u32[]{:S(2)}) collective-permute-start(f32[2,8,640]{2,1,0:T(8,128)S(1)} %pad_maximum_fusion.10.refs_0_), channel_id=1, source_target_pairs={{0,6},{1,7},{2,0},{3,1},{4,2},{5,3},{6,4},{7,5},{8,14},{9,15},{10,... | collective-permute-start | bytes 122888 | tf_op jit(solution)/shard_map/ppermute | solution.py:42
  88.5 4.6 %collective-permute-start.22 = (f32[8,640]{1,0:T(8,128)S(1)}, f32[8,640]{1,0:T(8,128)S(1)}, u32[]{:S(2)}, u32[]{:S(2)}) collective-permute-start(f32[8,640]{1,0:T(8,128)S(1)} %get-tuple-element.60.piece0), channel_id=1, source_target_pairs={{0,8},{1,9},{2,10},{3,11},{4,12},{5,13},{6,14},{7,15},{8,16},{9,17... | collective-permute-start | bytes 61448 | tf_op jit(solution)/shard_map/ppermute | solution.py:42
  89.7 5.3 %collective-permute-start.21 = (f32[8,640]{1,0:T(8,128)S(1)}, f32[8,640]{1,0:T(8,128)S(1)}, u32[]{:S(2)}, u32[]{:S(2)}) collective-permute-start(f32[8,640]{1,0:T(8,128)S(1)} %get-tuple-element.60.piece0), channel_id=1, source_target_pairs={{0,16},{1,17},{2,18},{3,19},{4,20},{5,21},{6,22},{7,23},{8,24},{9,... | collective-permute-start | bytes 61448 | tf_op jit(solution)/shard_map/ppermute | solution.py:42
  90.6 4.4 %collective-permute-start.20 = (f32[8,640]{1,0:T(8,128)S(1)}, f32[8,640]{1,0:T(8,128)S(1)}, u32[]{:S(2)}, u32[]{:S(2)}) collective-permute-start(f32[8,640]{1,0:T(8,128)S(1)} %get-tuple-element.60.piece0), channel_id=1, source_target_pairs={{0,24},{1,25},{2,26},{3,27},{4,28},{5,29},{6,30},{7,31},{8,0},{9,1... | collective-permute-start | bytes 61448 | tf_op jit(solution)/shard_map/ppermute | solution.py:42
  101.2 13.9 %collective-permute-start.24 = (bf16[128,2048]{1,0:T(8,128)(2,1)S(1)}, bf16[128,2048]{1,0:T(8,128)(2,1)S(1)}, u32[]{:S(2)}, u32[]{:S(2)}) collective-permute-start(bf16[128,2048]{1,0:T(8,128)(2,1)S(1)} %get-tuple-element.123), channel_id=1, source_target_pairs={{0,32},{1,97},{2,34},{3,99},{4,36},{5,101},{6,38},{7,103},{8,40},{... | collective-permute-start | bytes 1572872 | tf_op jit(solution)/shard_map/ppermute | solution.py:60
  101.2 18.3 %collective-permute-start.23 = (bf16[128,2048]{1,0:T(8,128)(2,1)}, bf16[128,2048]{1,0:T(8,128)(2,1)}, u32[]{:S(2)}, u32[]{:S(2)}) collective-permute-start(bf16[128,2048]{1,0:T(8,128)(2,1)} %get-tuple-element.122), channel_id=1, source_target_pairs={{0,96},{1,33},{2,98},{3,35},{4,100},{5,37},{6,102},{7,39},{8,104},... | collective-permute-start | bytes 1572872 | tf_op jit(solution)/shard_map/ppermute | solution.py:60
  116.2 10.7 %collective-permute-start.25 = (bf16[128,2048]{1,0:T(8,128)(2,1)}, bf16[128,2048]{1,0:T(8,128)(2,1)}, u32[]{:S(2)}, u32[]{:S(2)}) collective-permute-start(bf16[128,2048]{1,0:T(8,128)(2,1)} %add_convert_fusion.7), channel_id=1, source_target_pairs={{0,32},{1,97},{2,34},{3,99},{4,36},{5,101},{6,38},{7,103},{8,40},{... | collective-permute-start | bytes 1572872 | tf_op jit(solution)/shard_map/ppermute | solution.py:60
  116.2 17.3 %collective-permute-start.29 = (bf16[128,2048]{1,0:T(8,128)(2,1)}, bf16[128,2048]{1,0:T(8,128)(2,1)}, u32[]{:S(2)}, u32[]{:S(2)}) collective-permute-start(bf16[128,2048]{1,0:T(8,128)(2,1)} %param.35), channel_id=1, source_target_pairs={{0,96},{1,33},{2,98},{3,35},{4,100},{5,37},{6,102},{7,39},{8,104},... | collective-permute-start | bytes 1572872 | tf_op jit(solution)/shard_map/ppermute | solution.py:60
  130.3 10.6 %collective-permute-start.27 = (bf16[128,2048]{1,0:T(8,128)(2,1)S(1)}, bf16[128,2048]{1,0:T(8,128)(2,1)}, u32[]{:S(2)}, u32[]{:S(2)}) collective-permute-start(bf16[128,2048]{1,0:T(8,128)(2,1)S(1)} %multiply_convert_fusion.3), channel_id=1, source_target_pairs={{0,32},{1,97},{2,34},{3,99},{4,36},{5,101},{6,38},{7,103},{8,40},{... | collective-permute-start | bytes 1572872 | tf_op jit(solution)/shard_map/ppermute | solution.py:60
  130.5 13.6 %collective-permute-start.26 = (bf16[128,2048]{1,0:T(8,128)(2,1)S(1)}, bf16[128,2048]{1,0:T(8,128)(2,1)S(1)}, u32[]{:S(2)}, u32[]{:S(2)}) collective-permute-start(bf16[128,2048]{1,0:T(8,128)(2,1)S(1)} %multiply_convert_fusion.3), channel_id=1, source_target_pairs={{0,96},{1,33},{2,98},{3,35},{4,100},{5,37},{6,102},{7,39},{8,104},... | collective-permute-start | bytes 1572872 | tf_op jit(solution)/shard_map/ppermute | solution.py:60
  140.8 11.7 %collective-permute-start.28 = (bf16[128,2048]{1,0:T(8,128)(2,1)}, bf16[128,2048]{1,0:T(8,128)(2,1)}, u32[]{:S(2)}, u32[]{:S(2)}) collective-permute-start(bf16[128,2048]{1,0:T(8,128)(2,1)} %collective-permute-done.27), channel_id=1, source_target_pairs={{0,32},{1,97},{2,34},{3,99},{4,36},{5,101},{6,38},{7,103},{8,40},{... | collective-permute-start | bytes 1572872 | tf_op jit(solution)/shard_map/ppermute | solution.py:60
  194.1 27.0 %copy-start.17 = (f32[128,2048]{1,0:T(8,128)S(1)}, f32[128,2048]{1,0:T(8,128)}, u32[]{:S(2)}) copy-start(f32[128,2048]{1,0:T(8,128)} %copy-done.16) | copy-start | bytes 3145732
  194.2 16.2 %collective-permute-start.30 = (bf16[128,2048]{1,0:T(8,128)(2,1)S(1)}, bf16[128,2048]{1,0:T(8,128)(2,1)S(1)}, u32[]{:S(2)}, u32[]{:S(2)}) collective-permute-start(bf16[128,2048]{1,0:T(8,128)(2,1)S(1)} %get-tuple-element.121), channel_id=1, source_target_pairs={{0,32},{1,97},{2,34},{3,99},{4,36},{5,101},{6,38},{7,103},{8,40},{... | collective-permute-start | bytes 1572872 | tf_op jit(solution)/shard_map/ppermute | solution.py:60
  194.8 15.9 %collective-permute-start.31 = (bf16[128,2048]{1,0:T(8,128)(2,1)S(1)}, bf16[128,2048]{1,0:T(8,128)(2,1)S(1)}, u32[]{:S(2)}, u32[]{:S(2)}) collective-permute-start(bf16[128,2048]{1,0:T(8,128)(2,1)S(1)} %get-tuple-element.120), channel_id=1, source_target_pairs={{0,96},{1,33},{2,98},{3,35},{4,100},{5,37},{6,102},{7,39},{8,104},... | collective-permute-start | bytes 1572872 | tf_op jit(solution)/shard_map/ppermute | solution.py:60
  210.7 10.5 %collective-permute-start.32 = (bf16[128,2048]{1,0:T(8,128)(2,1)S(1)}, bf16[128,2048]{1,0:T(8,128)(2,1)S(1)}, u32[]{:S(2)}, u32[]{:S(2)}) collective-permute-start(bf16[128,2048]{1,0:T(8,128)(2,1)S(1)} %add_convert_fusion.6), channel_id=1, source_target_pairs={{0,32},{1,97},{2,34},{3,99},{4,36},{5,101},{6,38},{7,103},{8,40},{... | collective-permute-start | bytes 1572872 | tf_op jit(solution)/shard_map/ppermute | solution.py:60
  224.3 10.4 %collective-permute-start.34 = (bf16[128,2048]{1,0:T(8,128)(2,1)S(1)}, bf16[128,2048]{1,0:T(8,128)(2,1)S(1)}, u32[]{:S(2)}, u32[]{:S(2)}) collective-permute-start(bf16[128,2048]{1,0:T(8,128)(2,1)S(1)} %get-tuple-element.105), channel_id=1, source_target_pairs={{0,32},{1,97},{2,34},{3,99},{4,36},{5,101},{6,38},{7,103},{8,40},{... | collective-permute-start | bytes 1572872 | tf_op jit(solution)/shard_map/ppermute | solution.py:60
  224.3 18.0 %collective-permute-start.33 = (bf16[128,2048]{1,0:T(8,128)(2,1)S(1)}, bf16[128,2048]{1,0:T(8,128)(2,1)S(1)}, u32[]{:S(2)}, u32[]{:S(2)}) collective-permute-start(bf16[128,2048]{1,0:T(8,128)(2,1)S(1)} %get-tuple-element.105), channel_id=1, source_target_pairs={{0,96},{1,33},{2,98},{3,35},{4,100},{5,37},{6,102},{7,39},{8,104},... | collective-permute-start | bytes 1572872 | tf_op jit(solution)/shard_map/ppermute | solution.py:60
  234.7 10.4 %collective-permute-start.35 = (bf16[128,2048]{1,0:T(8,128)(2,1)S(1)}, bf16[128,2048]{1,0:T(8,128)(2,1)S(1)}, u32[]{:S(2)}, u32[]{:S(2)}) collective-permute-start(bf16[128,2048]{1,0:T(8,128)(2,1)S(1)} %collective-permute-done.34), channel_id=1, source_target_pairs={{0,32},{1,97},{2,34},{3,99},{4,36},{5,101},{6,38},{7,103},{8,40},{... | collective-permute-start | bytes 1572872 | tf_op jit(solution)/shard_map/ppermute | solution.py:60
  254.4 1.2 collective-permute-start.36
  255.6 5.8 %collective-permute-start.39 = (f32[2,8,640]{2,1,0:T(8,128)S(1)}, f32[2,8,640]{2,1,0:T(8,128)S(1)}, u32[]{:S(2)}, u32[]{:S(2)}) collective-permute-start(f32[2,8,640]{2,1,0:T(8,128)S(1)} %pad_maximum_fusion.11.refs_0_), channel_id=1, source_target_pairs={{0,2},{1,3},{2,4},{3,5},{4,6},{5,7},{6,0},{7,1},{8,10},{9,11},{10,... | collective-permute-start | bytes 122888 | tf_op jit(solution)/shard_map/ppermute | solution.py:42
  257.3 6.6 %collective-permute-start.38 = (f32[2,8,640]{2,1,0:T(8,128)S(1)}, f32[2,8,640]{2,1,0:T(8,128)S(1)}, u32[]{:S(2)}, u32[]{:S(2)}) collective-permute-start(f32[2,8,640]{2,1,0:T(8,128)S(1)} %pad_maximum_fusion.11.refs_0_), channel_id=1, source_target_pairs={{0,4},{1,5},{2,6},{3,7},{4,0},{5,1},{6,2},{7,3},{8,12},{9,13},{10,... | collective-permute-start | bytes 122888 | tf_op jit(solution)/shard_map/ppermute | solution.py:42
  258.9 5.9 %collective-permute-start.37 = (f32[2,8,640]{2,1,0:T(8,128)S(1)}, f32[2,8,640]{2,1,0:T(8,128)S(1)}, u32[]{:S(2)}, u32[]{:S(2)}) collective-permute-start(f32[2,8,640]{2,1,0:T(8,128)S(1)} %pad_maximum_fusion.11.refs_0_), channel_id=1, source_target_pairs={{0,6},{1,7},{2,0},{3,1},{4,2},{5,3},{6,4},{7,5},{8,14},{9,15},{10,... | collective-permute-start | bytes 122888 | tf_op jit(solution)/shard_map/ppermute | solution.py:42
  265.4 4.7 %collective-permute-start.42 = (f32[8,640]{1,0:T(8,128)S(1)}, f32[8,640]{1,0:T(8,128)S(1)}, u32[]{:S(2)}, u32[]{:S(2)}) collective-permute-start(f32[8,640]{1,0:T(8,128)S(1)} %get-tuple-element.75.piece0), channel_id=1, source_target_pairs={{0,8},{1,9},{2,10},{3,11},{4,12},{5,13},{6,14},{7,15},{8,16},{9,17... | collective-permute-start | bytes 61448 | tf_op jit(solution)/shard_map/ppermute | solution.py:42
  266.3 5.9 %collective-permute-start.41 = (f32[8,640]{1,0:T(8,128)S(1)}, f32[8,640]{1,0:T(8,128)S(1)}, u32[]{:S(2)}, u32[]{:S(2)}) collective-permute-start(f32[8,640]{1,0:T(8,128)S(1)} %get-tuple-element.75.piece0), channel_id=1, source_target_pairs={{0,16},{1,17},{2,18},{3,19},{4,20},{5,21},{6,22},{7,23},{8,24},{9,... | collective-permute-start | bytes 61448 | tf_op jit(solution)/shard_map/ppermute | solution.py:42
  267.7 4.9 %collective-permute-start.40 = (f32[8,640]{1,0:T(8,128)S(1)}, f32[8,640]{1,0:T(8,128)S(1)}, u32[]{:S(2)}, u32[]{:S(2)}) collective-permute-start(f32[8,640]{1,0:T(8,128)S(1)} %get-tuple-element.75.piece0), channel_id=1, source_target_pairs={{0,24},{1,25},{2,26},{3,27},{4,28},{5,29},{6,30},{7,31},{8,0},{9,1... | collective-permute-start | bytes 61448 | tf_op jit(solution)/shard_map/ppermute | solution.py:42
  285.3 2.9 collective-permute-start.43
  291.6 7.7 %collective-permute-start.44 = (bf16[8,208,640]{2,1,0:T(8,128)(2,1)S(1)}, bf16[8,208,640]{2,1,0:T(8,128)(2,1)S(1)}, u32[]{:S(2)}, u32[]{:S(2)}) collective-permute-start(bf16[8,208,640]{2,1,0:T(8,128)(2,1)S(1)} %get-tuple-element.89), channel_id=1, source_target_pairs={{0,1},{1,0},{2,3},{3,2},{4,5},{5,4},{6,7},{7,6},{8,9},{9,8},{10,11... | collective-permute-start | bytes 6389768 | tf_op jit(solution)/shard_map/ppermute | solution.py:42
  296.0 4.3 %collective-permute-start.45 = (bf16[8,208,640]{2,1,0:T(8,128)(2,1)S(1)}, bf16[8,208,640]{2,1,0:T(8,128)(2,1)S(1)}, u32[]{:S(2)}, u32[]{:S(2)}) collective-permute-start(bf16[8,208,640]{2,1,0:T(8,128)(2,1)S(1)} %get-tuple-element.86), channel_id=1, source_target_pairs={{0,1},{1,0},{2,3},{3,2},{4,5},{5,4},{6,7},{7,6},{8,9},{9,8},{10,11... | collective-permute-start | bytes 6389768 | tf_op jit(solution)/shard_map/ppermute | solution.py:42
  304.2 13.1 %collective-permute-start.47 = (bf16[128,2048]{1,0:T(8,128)(2,1)}, bf16[128,2048]{1,0:T(8,128)(2,1)S(1)}, u32[]{:S(2)}, u32[]{:S(2)}) collective-permute-start(bf16[128,2048]{1,0:T(8,128)(2,1)} %get-tuple-element.119), channel_id=1, source_target_pairs={{0,32},{1,97},{2,34},{3,99},{4,36},{5,101},{6,38},{7,103},{8,40},{... | collective-permute-start | bytes 1572872 | tf_op jit(solution)/shard_map/ppermute | solution.py:60
  304.2 73.0 %all-to-all-start = ((bf16[16,208,640]{2,1,0:T(8,128)(2,1)}), bf16[16,208,640]{2,1,0:T(8,128)(2,1)}, u32[]{:S(2)}, u32[]{:S(2)}) async-start(bf16[16,208,640]{2,1,0:T(8,128)(2,1)} %pad_maximum_fusion), calls=%async_computation | async-start | bytes 8519680 | tf_op jit(solution)/shard_map/all_to_all | solution.py:137
  314.0 14.9 %collective-permute-start.46 = (bf16[128,2048]{1,0:T(8,128)(2,1)S(1)}, bf16[128,2048]{1,0:T(8,128)(2,1)S(1)}, u32[]{:S(2)}, u32[]{:S(2)}) collective-permute-start(bf16[128,2048]{1,0:T(8,128)(2,1)S(1)} %get-tuple-element.118), channel_id=1, source_target_pairs={{0,96},{1,33},{2,98},{3,35},{4,100},{5,37},{6,102},{7,39},{8,104},... | collective-permute-start | bytes 1572872 | tf_op jit(solution)/shard_map/ppermute | solution.py:60
  317.6 11.7 %collective-permute-start.48 = (bf16[128,2048]{1,0:T(8,128)(2,1)S(1)}, bf16[128,2048]{1,0:T(8,128)(2,1)S(1)}, u32[]{:S(2)}, u32[]{:S(2)}) collective-permute-start(bf16[128,2048]{1,0:T(8,128)(2,1)S(1)} %add_convert_fusion.5), channel_id=1, source_target_pairs={{0,32},{1,97},{2,34},{3,99},{4,36},{5,101},{6,38},{7,103},{8,40},{... | collective-permute-start | bytes 1572872 | tf_op jit(solution)/shard_map/ppermute | solution.py:60
  329.9 14.8 %collective-permute-start.50 = (bf16[128,2048]{1,0:T(8,128)(2,1)S(1)}, bf16[128,2048]{1,0:T(8,128)(2,1)S(1)}, u32[]{:S(2)}, u32[]{:S(2)}) collective-permute-start(bf16[128,2048]{1,0:T(8,128)(2,1)S(1)} %get-tuple-element.117), channel_id=1, source_target_pairs={{0,32},{1,97},{2,34},{3,99},{4,36},{5,101},{6,38},{7,103},{8,40},{... | collective-permute-start | bytes 1572872 | tf_op jit(solution)/shard_map/ppermute | solution.py:60
  330.2 16.2 %collective-permute-start.49 = (bf16[128,2048]{1,0:T(8,128)(2,1)S(1)}, bf16[128,2048]{1,0:T(8,128)(2,1)S(1)}, u32[]{:S(2)}, u32[]{:S(2)}) collective-permute-start(bf16[128,2048]{1,0:T(8,128)(2,1)S(1)} %get-tuple-element.116), channel_id=1, source_target_pairs={{0,96},{1,33},{2,98},{3,35},{4,100},{5,37},{6,102},{7,39},{8,104},... | collective-permute-start | bytes 1572872 | tf_op jit(solution)/shard_map/ppermute | solution.py:60
  345.0 10.5 %collective-permute-start.51 = (bf16[128,2048]{1,0:T(8,128)(2,1)S(1)}, bf16[128,2048]{1,0:T(8,128)(2,1)S(1)}, u32[]{:S(2)}, u32[]{:S(2)}) collective-permute-start(bf16[128,2048]{1,0:T(8,128)(2,1)S(1)} %add_convert_fusion.4), channel_id=1, source_target_pairs={{0,32},{1,97},{2,34},{3,99},{4,36},{5,101},{6,38},{7,103},{8,40},{... | collective-permute-start | bytes 1572872 | tf_op jit(solution)/shard_map/ppermute | solution.py:60
  356.6 23.6 %copy-start.40 = (bf16[64,640]{1,0:T(8,128)(2,1)S(1)}, bf16[64,640]{1,0:T(8,128)(2,1)}, u32[]{:S(2)}) copy-start(bf16[64,640]{1,0:T(8,128)(2,1)} %param.21) | copy-start | bytes 245764
  356.6 24.5 %copy-start.41 = (bf16[64]{0:T(256)(128)(2,1)S(1)}, bf16[64]{0:T(256)(128)(2,1)}, u32[]{:S(2)}) copy-start(bf16[64]{0:T(256)(128)(2,1)} %param.19) | copy-start | bytes 388
  356.6 27.2 %copy-start.42 = (bf16[20]{0:T(256)(128)(2,1)S(1)}, bf16[20]{0:T(256)(128)(2,1)}, u32[]{:S(2)}) copy-start(bf16[20]{0:T(256)(128)(2,1)} %param.28) | copy-start | bytes 124
  381.2 5.2 %collective-permute-start.54 = (f32[1,128]{1,0:T(1,128)S(1)}, f32[1,128]{1,0:T(1,128)S(1)}, u32[]{:S(2)}, u32[]{:S(2)}) collective-permute-start(f32[1,128]{1,0:T(1,128)S(1)} %maximum_bitcast_fusion), channel_id=1, source_target_pairs={{0,64},{32,96},{64,0},{96,32},{1,65},{33,97},{65,1},{97,33},{2,66}... | collective-permute-start | bytes 1544 | tf_op jit(solution)/shard_map/ppermute | solution.py:25
  381.2 5.1 %collective-permute-start.53 = (f32[1,128]{1,0:T(1,128)S(1)}, f32[1,128]{1,0:T(1,128)S(1)}, u32[]{:S(2)}, u32[]{:S(2)}) collective-permute-start(f32[1,128]{1,0:T(1,128)S(1)} %maximum_bitcast_fusion), channel_id=1, source_target_pairs={{0,96},{32,0},{64,32},{96,64},{1,97},{33,1},{65,33},{97,65},{2,98}... | collective-permute-start | bytes 1544 | tf_op jit(solution)/shard_map/ppermute | solution.py:25
  382.5 4.8 %collective-permute-start.52 = (f32[1,128]{1,0:T(1,128)S(1)}, f32[1,128]{1,0:T(1,128)S(1)}, u32[]{:S(2)}, u32[]{:S(2)}) collective-permute-start(f32[1,128]{1,0:T(1,128)S(1)} %maximum_bitcast_fusion), channel_id=1, source_target_pairs={{0,32},{32,64},{64,96},{96,0},{1,33},{33,65},{65,97},{97,1},{2,34}... | collective-permute-start | bytes 1544 | tf_op jit(solution)/shard_map/ppermute | solution.py:25
  (42 other events, 325.4 us)
Sparse Core Ops, SparseCore 0:
  10.9 55.2 all-gather.2
  68.4 76.0 all-gather.4
  183.5 123.2 reduce-scatter.1

commit v4 on v3

--- a/solution.py
+++ b/solution.py
@@ -633,7 +633,7 @@
 def feed_outer(lhs_one, lhs_two, rhs):
     rows, features = lhs_one.shape
     columns = rhs[0].shape[1]
-    height = 1024
+    height = 2048
     whole = pl.BlockSpec(
         (rows, columns), lambda j, i: (0, 0), pipeline_mode=pl.Buffered(buffer_count=1)
     )
@@ -649,7 +649,7 @@
         ],
         out_specs=pl.BlockSpec((height, columns), lambda j, i: (i, j)),
         out_shape=pltpu.HBM((features, 3 * columns), bf16),
-        compiler_params=pltpu.CompilerParams(vmem_limit_bytes=26 * 1024 * 1024),
+        compiler_params=pltpu.CompilerParams(vmem_limit_bytes=44 * 1024 * 1024),
         cost_estimate=pl.CostEstimate(
             flops=6 * rows * features * columns,
             bytes_accessed=6 * features * columns,

time: 405 us -> 406 us (level)
  transfers between devices with their start and end apart: 59 -> 59, of which waited for: 34 -> 33; matrix products, arithmetic and copies ran while one was open for 21% -> 21% of each run, Pallas kernels for 8% -> 8%
where the time goes in v4:
time: 406 us; the launch traced here: 398 us
  waiting for transfers between devices  156 us (38%)
  starting transfers between devices  68.5 us (17%)
  matrix products  48.8 us (12%)
  Pallas kernels  47.1 us (12%)
  other arithmetic  45.7 us (11%)
  local copies, waits for them, and re-layouts  17.1 us (4%)
  between operations  15.2 us (4%)
    ppermute x24, waiting for transfers between devices, hop_apart(): return lax.ppermute(values, ('blk', 'tok'), route)  101 us
    ppermute x23, waiting for transfers between devices, hop_tok(): return lax.ppermute(values, 'tok', route)  30.2 us
    ppermute x24, starting transfers between devices, hop_apart(): return lax.ppermute(values, ('blk', 'tok'), route)  28.9 us
    dot_general x5, matrix products, product(): return jnp.dot(operand, weight, preferred_element_type=f32).astype(out)  25.6 us
    pallas_call x4, Pallas kernels, by_slot(): pl.pallas_call(kernel, grid=(MEMBERS,), in_specs=[pl.BlockSpec(memory_spa...  23.7 us
    dot_general x4, matrix products, product_back(): lax.dot_general(operand, weight, (((1,), (1,)), ((), ())), preferred_elem...  23.2 us
    all_to_all x1, waiting for transfers between devices, chips_sum(): lax.all_to_all(values, 'tok', 0, 0, axis_index_groups=cores, tiled=True)  22.3 us
    ppermute x23, starting transfers between devices, hop_tok(): return lax.ppermute(values, 'tok', route)  22.2 us
  transfers between devices with their start and end apart: 59, of which 33 were waited for; matrix products, arithmetic and copies ran while one was open for 21% of the time, Pallas kernels for 8%

profile of v4, /device:TPU:80, one launch (start us, length us, event | category | flops | bytes accessed | tf_op | source)
XLA Modules:
  0.0 398.1 jit_solution(9775390007053692934)
XLA Ops:
  7.2 1.7 pad_maximum_fusion.7
  10.6 1.7 collective-permute-start.4
  15.7 2.0 pad_maximum_fusion.5
  18.3 3.1 collective-permute-start.1
  21.6 2.4 collective-permute-done.5
  29.9 2.2 collective-permute-start.14
  33.9 2.0 collective-permute-done.9
  40.0 3.2 collective-permute-done.8
  43.2 4.7 %collective-permute-done.7 = bf16[4,2,16,640]{3,2,1,0:T(8,128)(2,1)S(1)} collective-permute-done((bf16[4,2,16,640]{3,2,1,0:T(8,128)(2,1)S(1)}, bf16[4,2,16,640]{3,2,1,0:T(8,128)(2,1)S(1)}, u32[]{:S(2)}, u32[]{:S(2)}) %collective-permute-start.7) | collective-permute-done | bytes 163872 | tf_op jit(solution)/shard_map/ppermute | solution.py:42
  47.9 4.0 %collective-permute-done.6 = bf16[4,2,16,640]{3,2,1,0:T(8,128)(2,1)S(1)} collective-permute-done((bf16[4,2,16,640]{3,2,1,0:T(8,128)(2,1)S(1)}, bf16[4,2,16,640]{3,2,1,0:T(8,128)(2,1)S(1)}, u32[]{:S(2)}, u32[]{:S(2)}) %collective-permute-start.6) | collective-permute-done | bytes 163872 | tf_op jit(solution)/shard_map/ppermute | solution.py:42
  54.4 2.5 fusion.12.refs_2_.refs_3_
  56.9 7.9 %collective-permute-done.11 = bf16[128,2048]{1,0:T(8,128)(2,1)} collective-permute-done((bf16[128,2048]{1,0:T(8,128)(2,1)S(1)}, bf16[128,2048]{1,0:T(8,128)(2,1)}, u32[]{:S(2)}, u32[]{:S(2)}) %collective-permute-start.11) | collective-permute-done | bytes 524320 | tf_op jit(solution)/shard_map/ppermute | solution.py:60
  67.1 3.9 fusion.36.ci_ref.halo_ref
  71.0 7.4 %shard_map.305 = (bf16[512,640]{1,0:T(8,128)(2,1)}, f32[512,640]{1,0:T(8,128)}, bf16[512,640]{1,0:T(8,128)(2,1)}, f32[512,640]{1,0:T(8,128)S(1)}, f32[512,640]{1...) custom-call(f32[4,640]{1,0:T(4,128)S(1)} %slice.206.taps_ref, f32[1,640]{1,0:T(1,128)S(1)} %slice.208.shift_ref, ...), custom_call_target="tpu_custom_call" | custom-call | bytes 30000000 | tf_op jit(solution)/shard_map/pallas_call | solution.py:578
  81.8 3.8 collective-permute-done.19.refs_3_
  85.6 2.5 collective-permute-done.17.refs_1_
  91.7 1.8 fusion.28.branch_ref
  93.5 1.9 collective-permute-done.21.piece2
  98.8 1.8 convolution_convert_fusion
  101.6 3.2 collective-permute-start.23
  104.8 10.5 %collective-permute-done.24 = bf16[128,2048]{1,0:T(8,128)(2,1)S(1)} collective-permute-done((bf16[128,2048]{1,0:T(8,128)(2,1)S(1)}, bf16[128,2048]{1,0:T(8,128)(2,1)S(1)}, u32[]{:S(2)}, u32[]{:S(2)}) %collective-permute-start.24) | collective-permute-done | bytes 524320 | tf_op jit(solution)/shard_map/ppermute | solution.py:60
  116.4 3.1 collective-permute-start.29
  119.6 7.4 %collective-permute-done.25 = bf16[128,2048]{1,0:T(8,128)(2,1)} collective-permute-done((bf16[128,2048]{1,0:T(8,128)(2,1)}, bf16[128,2048]{1,0:T(8,128)(2,1)}, u32[]{:S(2)}, u32[]{:S(2)}) %collective-permute-start.25) | collective-permute-done | bytes 524320 | tf_op jit(solution)/shard_map/ppermute | solution.py:60
  127.0 2.2 multiply_reduce_fusion.2
  130.6 3.1 collective-permute-start.26
  134.8 2.8 pad_maximum_fusion.1.lhs_two
  137.6 3.3 collective-permute-done.27
  141.0 3.8 collective-permute-done.26
  144.8 2.1 broadcast_select_fusion.8
  146.9 6.3 %fusion.6 = f32[512,1536]{1,0:T(8,128)S(1)} fusion(bf16[512,2048]{1,0:T(8,128)(2,1)} %pad_maximum_fusion.1.lhs_two, bf16[2048,4608]{1,0:T(8,128)(2,1)} %all-gather.5.cloned.1.call-done), kind=kOutput, calls=%fused_computation.9 | convolution fusion | flops 3221225472 | bytes 11534336 | tf_op jit(solution)/shard_map/dot_general | solution.py:152
  154.5 9.7 %fusion.2 = f32[512,3072]{1,0:T(8,128)S(1)} fusion(bf16[2048,4608]{1,0:T(8,128)(2,1)} %all-gather.5.cloned.1.call-done, bf16[128,2048]{1,0:T(8,128)(2,1)S(1)} %copy-done.30, bf16[128,2048]{1,0:T(8,128)(2,1)} %collective-permute-done.28, bf16[128,2048]{1,0:T(8,128)(2,1)S(1)} %copy-done.29, bf16[128,2048]{1,0:T(8,128)(2,1)S(1)} %copy-done.32), kind=kOutput, calls=%fused_computation.2 | convolution fusion | flops 6450839552 | bytes 20971520 | tf_op jit(solution)/shard_map/dot_general | solution.py:152
  164.3 2.5 multiply_convert_fusion
  166.8 13.4 %shard_map.308 = bf16[2048,4608]{1,0:T(8,128)(2,1)} custom-call(bf16[512,2048]{1,0:T(8,128)(2,1)S(1)} %pad_maximum_fusion.2.lhs_one, bf16[512,2048]{1,0:T(8,128)(2,1)S(1)} %copy-done.10, bf16[512,1536]{1,0:T(8,128)(2,1)S(1)} %get-tuple-element.68.rhs_one, bf16[512,1536]{1,0:T(8,128)(2,1)S(1)} %get-tuple-element.69.rhs_two, ...), custom_call_target="tpu_custom_call" | custom-call | flops 9663676416 | bytes 18874368 | tf_op jit(solution)/shard_map/pallas_call | solution.py:640
  183.8 10.7 %fusion.23 = bf16[512,2048]{1,0:T(8,128)(2,1)S(1)} fusion(bf16[2048,4608]{1,0:T(8,128)(2,1)} %all-gather.5.cloned.1.call-done, bf16[512,1536]{1,0:T(8,128)(2,1)} %copy-done.14, bf16[512,1536]{1,0:T(8,128)(2,1)} %copy-done.15), kind=kOutput, calls=%fused_computation.31 | convolution fusion | flops 6449790976 | bytes 17825792 | tf_op jit(solution)/shard_map/dot_general | solution.py:156
  194.9 3.8 collective-permute-start.31
  198.7 11.5 %collective-permute-done.30 = bf16[128,2048]{1,0:T(8,128)(2,1)S(1)} collective-permute-done((bf16[128,2048]{1,0:T(8,128)(2,1)S(1)}, bf16[128,2048]{1,0:T(8,128)(2,1)S(1)}, u32[]{:S(2)}, u32[]{:S(2)}) %collective-permute-start.30) | collective-permute-done | bytes 524320 | tf_op jit(solution)/shard_map/ppermute | solution.py:60
  210.6 10.4 %collective-permute-done.32 = bf16[128,2048]{1,0:T(8,128)(2,1)S(1)} collective-permute-done((bf16[128,2048]{1,0:T(8,128)(2,1)S(1)}, bf16[128,2048]{1,0:T(8,128)(2,1)S(1)}, u32[]{:S(2)}, u32[]{:S(2)}) %collective-permute-start.32) | collective-permute-done | bytes 524320 | tf_op jit(solution)/shard_map/ppermute | solution.py:60
  221.5 2.7 fusion.72
  224.2 3.2 collective-permute-start.33
  227.4 7.2 %collective-permute-done.34 = bf16[128,2048]{1,0:T(8,128)(2,1)S(1)} collective-permute-done((bf16[128,2048]{1,0:T(8,128)(2,1)S(1)}, bf16[128,2048]{1,0:T(8,128)(2,1)S(1)}, u32[]{:S(2)}, u32[]{:S(2)}) %collective-permute-start.34) | collective-permute-done | bytes 524320 | tf_op jit(solution)/shard_map/ppermute | solution.py:60
  234.6 7.6 %fusion.20 = bf16[512,2048]{1,0:T(8,128)(2,1)} fusion(bf16[512,1536]{1,0:T(8,128)(2,1)S(1)} %copy-done.13, bf16[2048,4608]{1,0:T(8,128)(2,1)} %all-gather.5.cloned.1.call-done), kind=kOutput, calls=%fused_computation.29 | convolution fusion | flops 3222274048 | bytes 9961472 | tf_op jit(solution)/shard_map/dot_general | solution.py:156
  242.2 2.7 collective-permute-done.35
  245.0 3.9 fusion.32.grad_ref
  248.9 4.6 %shard_map.309 = (bf16[512,640]{1,0:T(8,128)(2,1)S(1)}, f32[8,640]{1,0:T(8,128)S(1)}) custom-call(f32[1,640]{1,0:T(1,128)S(1)} %fusion.60.soft_ref, f32[512,640]{1,0:T(8,128)S(1)} %fusion.32.grad_ref, f32[512,640]{1,0:T(8,128)} %copy-done, bf16[512,640]{1,0:T(8,128)(2,1)S(1)} %copy-done.8, f32[512,640]{1,0:T(8,128)} %get-tuple-element.73.rate_ref, ...), custom_call_target="tpu_custom_call" | custom-call | bytes 9500000 | tf_op jit(solution)/shard_map/pallas_call | solution.py:578
  256.5 1.8 collective-permute-start.38
  258.4 2.6 collective-permute-start.37
  260.9 2.2 collective-permute-done.38.refs_2_
  267.2 2.1 collective-permute-start.40
  269.5 2.7 collective-permute-done.41.piece2
  274.7 10.2 %shard_map.311 = (bf16[512,1280]{1,0:T(8,128)(2,1)S(1)}, f32[512,640]{1,0:T(8,128)S(1)}, f32[64,640]{1,0:T(8,128)S(1)}, f32[8,640]{1,0:T(8,128)S(1)}) custom-call(s32[4]{0:T(128)S(1)} %pad_add_fusion.spot_ref, f32[8,640]{1,0:T(8,128)S(1)} %get-tuple-element.75.piece0, f32[8,640]{1,0:T(8,128)S(1)} %collective-permute-done.40.piece1, ...), custom_call_target="tpu_custom_call" | custom-call | bytes 40000000 | tf_op jit(solution)/shard_map/pallas_call | solution.py:578
  285.7 2.3 shard_map.312.refs_0_
  288.2 3.2 shard_map.314
  292.4 3.2 shard_map.313
  295.7 3.1 fusion.17
  300.5 2.5 pad_maximum_fusion
  303.9 9.8 %all-to-all-start = ((bf16[16,208,640]{2,1,0:T(8,128)(2,1)}), bf16[16,208,640]{2,1,0:T(8,128)(2,1)}, u32[]{:S(2)}, u32[]{:S(2)}) async-start(bf16[16,208,640]{2,1,0:T(8,128)(2,1)} %pad_maximum_fusion), calls=%async_computation | async-start | bytes 8519680 | tf_op jit(solution)/shard_map/all_to_all | solution.py:137
  313.7 3.3 collective-permute-start.46
  317.3 11.5 %collective-permute-done.46 = bf16[128,2048]{1,0:T(8,128)(2,1)S(1)} collective-permute-done((bf16[128,2048]{1,0:T(8,128)(2,1)S(1)}, bf16[128,2048]{1,0:T(8,128)(2,1)S(1)}, u32[]{:S(2)}, u32[]{:S(2)}) %collective-permute-start.46) | collective-permute-done | bytes 524320 | tf_op jit(solution)/shard_map/ppermute | solution.py:60
  330.1 3.4 collective-permute-start.49
  333.5 10.8 %collective-permute-done.50 = bf16[128,2048]{1,0:T(8,128)(2,1)S(1)} collective-permute-done((bf16[128,2048]{1,0:T(8,128)(2,1)S(1)}, bf16[128,2048]{1,0:T(8,128)(2,1)S(1)}, u32[]{:S(2)}, u32[]{:S(2)}) %collective-permute-start.50) | collective-permute-done | bytes 524320 | tf_op jit(solution)/shard_map/ppermute | solution.py:60
  345.9 9.1 %collective-permute-done.51 = bf16[128,2048]{1,0:T(8,128)(2,1)S(1)} collective-permute-done((bf16[128,2048]{1,0:T(8,128)(2,1)S(1)}, bf16[128,2048]{1,0:T(8,128)(2,1)S(1)}, u32[]{:S(2)}, u32[]{:S(2)}) %collective-permute-start.51) | collective-permute-done | bytes 524320 | tf_op jit(solution)/shard_map/ppermute | solution.py:60
  356.1 22.3 %all-to-all-done = bf16[16,208,640]{2,1,0:T(8,128)(2,1)} async-done(((bf16[16,208,640]{2,1,0:T(8,128)(2,1)}), bf16[16,208,640]{2,1,0:T(8,128)(2,1)}, u32[]{:S(2)}, u32[]{:S(2)}) %all-to-all-start) | async-done | bytes 4259872 | tf_op jit(solution)/shard_map/all_to_all | solution.py:137
  378.4 2.9 convert_reduce_fusion
  389.2 2.1 convert_bitcast_fusion
  (282 shorter events, 69.2 us)
Async XLA Ops:
  7.2 59.9 %all-gather.3.cloned.1.call-start = ((), (), s32[]{:S(2)}) async-start(), calls=%async_computation.2 | async-start | bytes 8110080 | tf_op jit(solution)/shard_map/all_gather | solution.py:786
  9.0 137.9 %all-gather.5.cloned.1.call-start = ((), (), s32[]{:S(2)}) async-start(), calls=%async_computation.3 | async-start | bytes 19464192 | tf_op jit(solution)/shard_map/all_gather | solution.py:811
  9.0 14.9 %collective-permute-start.5 = (bf16[128,2048]{1,0:T(8,128)(2,1)}, bf16[128,2048]{1,0:T(8,128)(2,1)S(1)}, u32[]{:S(2)}, u32[]{:S(2)}) collective-permute-start(bf16[128,2048]{1,0:T(8,128)(2,1)} %param.18), channel_id=1, source_target_pairs={{0,32},{1,97},{2,34},{3,99},{4,36},{5,101},{6,38},{7,103},{8,40},{... | collective-permute-start | bytes 1572872 | tf_op jit(solution)/shard_map/ppermute | solution.py:60
  10.6 22.2 %collective-permute-start.4 = (bf16[128,2048]{1,0:T(8,128)(2,1)}, bf16[128,2048]{1,0:T(8,128)(2,1)}, u32[]{:S(2)}, u32[]{:S(2)}) collective-permute-start(bf16[128,2048]{1,0:T(8,128)(2,1)} %param.18), channel_id=1, source_target_pairs={{0,96},{1,33},{2,98},{3,35},{4,100},{5,37},{6,102},{7,39},{8,104},... | collective-permute-start | bytes 1572872 | tf_op jit(solution)/shard_map/ppermute | solution.py:60
  15.6 2.1 collective-permute-start
  18.3 5.8 %collective-permute-start.2 = (bf16[2,16,640]{2,1,0:T(8,128)(2,1)}, bf16[2,16,640]{2,1,0:T(8,128)(2,1)S(1)}, u32[]{:S(2)}, u32[]{:S(2)}) collective-permute-start(bf16[2,16,640]{2,1,0:T(8,128)(2,1)} %get-tuple-element.142), channel_id=1, source_target_pairs={{0,4},{1,5},{2,6},{3,7},{4,0},{5,1},{6,2},{7,3},{8,12},{9,13},{10,... | collective-permute-start | bytes 122888 | tf_op jit(solution)/shard_map/ppermute | solution.py:42
  18.3 7.2 %collective-permute-start.1 = (bf16[2,16,640]{2,1,0:T(8,128)(2,1)}, bf16[2,16,640]{2,1,0:T(8,128)(2,1)}, u32[]{:S(2)}, u32[]{:S(2)}) collective-permute-start(bf16[2,16,640]{2,1,0:T(8,128)(2,1)} %get-tuple-element.142), channel_id=1, source_target_pairs={{0,6},{1,7},{2,0},{3,1},{4,2},{5,3},{6,4},{7,5},{8,14},{9,15},{10,... | collective-permute-start | bytes 122888 | tf_op jit(solution)/shard_map/ppermute | solution.py:42
  21.4 5.0 %collective-permute-start.3 = (bf16[2,16,640]{2,1,0:T(8,128)(2,1)}, bf16[2,16,640]{2,1,0:T(8,128)(2,1)}, u32[]{:S(2)}, u32[]{:S(2)}) collective-permute-start(bf16[2,16,640]{2,1,0:T(8,128)(2,1)} %get-tuple-element.142), channel_id=1, source_target_pairs={{0,2},{1,3},{2,4},{3,5},{4,6},{5,7},{6,0},{7,1},{8,10},{9,11},{10,... | collective-permute-start | bytes 122888 | tf_op jit(solution)/shard_map/ppermute | solution.py:42
  24.0 4.4 %collective-permute-start.12 = (bf16[16,2048]{1,0:T(8,128)(2,1)S(1)}, bf16[16,2048]{1,0:T(8,128)(2,1)S(1)}, u32[]{:S(2)}, u32[]{:S(2)}) collective-permute-start(bf16[16,2048]{1,0:T(8,128)(2,1)S(1)} %slice.216), channel_id=1, source_target_pairs={{0,1},{1,2},{2,3},{3,4},{4,5},{5,6},{6,7},{7,8},{8,9},{9,10},{10,1... | collective-permute-start | bytes 196616 | tf_op jit(solution)/shard_map/ppermute | solution.py:790
  24.1 11.8 %collective-permute-start.9 = (bf16[128,2048]{1,0:T(8,128)(2,1)S(1)}, bf16[128,2048]{1,0:T(8,128)(2,1)S(1)}, u32[]{:S(2)}, u32[]{:S(2)}) collective-permute-start(bf16[128,2048]{1,0:T(8,128)(2,1)S(1)} %collective-permute-done.5), channel_id=1, source_target_pairs={{0,32},{1,97},{2,34},{3,99},{4,36},{5,101},{6,38},{7,103},{8,40},{... | collective-permute-start | bytes 1572872 | tf_op jit(solution)/shard_map/ppermute | solution.py:60
  28.3 11.1 %collective-permute-start.15 = (bf16[16,2048]{1,0:T(8,128)(2,1)S(1)}, bf16[16,2048]{1,0:T(8,128)(2,1)S(1)}, u32[]{:S(2)}, u32[]{:S(2)}) collective-permute-start(bf16[16,2048]{1,0:T(8,128)(2,1)S(1)} %collective-permute-done.12), channel_id=1, source_target_pairs={{0,32},{32,64},{64,96},{96,0},{1,33},{33,65},{65,97},{97,1},{2,34}... | collective-permute-start | bytes 196616 | tf_op jit(solution)/shard_map/ppermute | solution.py:25
  29.9 9.4 %collective-permute-start.14 = (bf16[16,2048]{1,0:T(8,128)(2,1)S(1)}, bf16[16,2048]{1,0:T(8,128)(2,1)S(1)}, u32[]{:S(2)}, u32[]{:S(2)}) collective-permute-start(bf16[16,2048]{1,0:T(8,128)(2,1)S(1)} %collective-permute-done.12), channel_id=1, source_target_pairs={{0,64},{32,96},{64,0},{96,32},{1,65},{33,97},{65,1},{97,33},{2,66}... | collective-permute-start | bytes 196616 | tf_op jit(solution)/shard_map/ppermute | solution.py:25
  32.1 5.9 %collective-permute-start.13 = (bf16[16,2048]{1,0:T(8,128)(2,1)S(1)}, bf16[16,2048]{1,0:T(8,128)(2,1)S(1)}, u32[]{:S(2)}, u32[]{:S(2)}) collective-permute-start(bf16[16,2048]{1,0:T(8,128)(2,1)S(1)} %collective-permute-done.12), channel_id=1, source_target_pairs={{0,96},{32,0},{64,32},{96,64},{1,97},{33,1},{65,33},{97,65},{2,98}... | collective-permute-start | bytes 196616 | tf_op jit(solution)/shard_map/ppermute | solution.py:25
  36.1 7.1 %collective-permute-start.8 = (bf16[4,2,16,640]{3,2,1,0:T(8,128)(2,1)S(1)}, bf16[4,2,16,640]{3,2,1,0:T(8,128)(2,1)S(1)}, u32[]{:S(2)}, u32[]{:S(2)}) collective-permute-start(bf16[4,2,16,640]{3,2,1,0:T(8,128)(2,1)S(1)} %pad_maximum_fusion.8), channel_id=1, source_target_pairs={{0,8},{1,9},{2,10},{3,11},{4,12},{5,13},{6,14},{7,15},{8,16},{9,17... | collective-permute-start | bytes 491528 | tf_op jit(solution)/shard_map/ppermute | solution.py:42
  37.5 10.4 %collective-permute-start.7 = (bf16[4,2,16,640]{3,2,1,0:T(8,128)(2,1)S(1)}, bf16[4,2,16,640]{3,2,1,0:T(8,128)(2,1)S(1)}, u32[]{:S(2)}, u32[]{:S(2)}) collective-permute-start(bf16[4,2,16,640]{3,2,1,0:T(8,128)(2,1)S(1)} %pad_maximum_fusion.8), channel_id=1, source_target_pairs={{0,16},{1,17},{2,18},{3,19},{4,20},{5,21},{6,22},{7,23},{8,24},{9,... | collective-permute-start | bytes 491528 | tf_op jit(solution)/shard_map/ppermute | solution.py:42
  38.0 13.9 %collective-permute-start.6 = (bf16[4,2,16,640]{3,2,1,0:T(8,128)(2,1)S(1)}, bf16[4,2,16,640]{3,2,1,0:T(8,128)(2,1)S(1)}, u32[]{:S(2)}, u32[]{:S(2)}) collective-permute-start(bf16[4,2,16,640]{3,2,1,0:T(8,128)(2,1)S(1)} %pad_maximum_fusion.8), channel_id=1, source_target_pairs={{0,24},{1,25},{2,26},{3,27},{4,28},{5,29},{6,30},{7,31},{8,0},{9,1... | collective-permute-start | bytes 491528 | tf_op jit(solution)/shard_map/ppermute | solution.py:42
  39.3 15.0 %collective-permute-start.10 = (bf16[128,2048]{1,0:T(8,128)(2,1)}, bf16[128,2048]{1,0:T(8,128)(2,1)S(1)}, u32[]{:S(2)}, u32[]{:S(2)}) collective-permute-start(bf16[128,2048]{1,0:T(8,128)(2,1)} %param.35), channel_id=1, source_target_pairs={{0,32},{1,97},{2,34},{3,99},{4,36},{5,101},{6,38},{7,103},{8,40},{... | collective-permute-start | bytes 1572872 | tf_op jit(solution)/shard_map/ppermute | solution.py:60
  54.4 10.5 %collective-permute-start.11 = (bf16[128,2048]{1,0:T(8,128)(2,1)S(1)}, bf16[128,2048]{1,0:T(8,128)(2,1)}, u32[]{:S(2)}, u32[]{:S(2)}) collective-permute-start(bf16[128,2048]{1,0:T(8,128)(2,1)S(1)} %collective-permute-done.10), channel_id=1, source_target_pairs={{0,32},{1,97},{2,34},{3,99},{4,36},{5,101},{6,38},{7,103},{8,40},{... | collective-permute-start | bytes 1572872 | tf_op jit(solution)/shard_map/ppermute | solution.py:60
  64.9 324.4 %reduce-scatter.2.cloned.1.call-start = ((), (), s32[]{:S(2)}) async-start(), calls=%async_computation.4 | async-start | bytes 19464192 | tf_op jit(solution)/shard_map/reduce_scatter | solution.py:884
  78.4 1.3 collective-permute-start.16
  79.7 5.9 %collective-permute-start.19 = (f32[2,8,640]{2,1,0:T(8,128)S(1)}, f32[2,8,640]{2,1,0:T(8,128)S(1)}, u32[]{:S(2)}, u32[]{:S(2)}) collective-permute-start(f32[2,8,640]{2,1,0:T(8,128)S(1)} %pad_maximum_fusion.10.refs_0_), channel_id=1, source_target_pairs={{0,2},{1,3},{2,4},{3,5},{4,6},{5,7},{6,0},{7,1},{8,10},{9,11},{10,... | collective-permute-start | bytes 122888 | tf_op jit(solution)/shard_map/ppermute | solution.py:42
  79.7 5.9 %collective-permute-start.18 = (f32[2,8,640]{2,1,0:T(8,128)S(1)}, f32[2,8,640]{2,1,0:T(8,128)S(1)}, u32[]{:S(2)}, u32[]{:S(2)}) collective-permute-start(f32[2,8,640]{2,1,0:T(8,128)S(1)} %pad_maximum_fusion.10.refs_0_), channel_id=1, source_target_pairs={{0,4},{1,5},{2,6},{3,7},{4,0},{5,1},{6,2},{7,3},{8,12},{9,13},{10,... | collective-permute-start | bytes 122888 | tf_op jit(solution)/shard_map/ppermute | solution.py:42
  81.4 6.7 %collective-permute-start.17 = (f32[2,8,640]{2,1,0:T(8,128)S(1)}, f32[2,8,640]{2,1,0:T(8,128)S(1)}, u32[]{:S(2)}, u32[]{:S(2)}) collective-permute-start(f32[2,8,640]{2,1,0:T(8,128)S(1)} %pad_maximum_fusion.10.refs_0_), channel_id=1, source_target_pairs={{0,6},{1,7},{2,0},{3,1},{4,2},{5,3},{6,4},{7,5},{8,14},{9,15},{10,... | collective-permute-start | bytes 122888 | tf_op jit(solution)/shard_map/ppermute | solution.py:42
  88.7 4.8 %collective-permute-start.22 = (f32[8,640]{1,0:T(8,128)S(1)}, f32[8,640]{1,0:T(8,128)S(1)}, u32[]{:S(2)}, u32[]{:S(2)}) collective-permute-start(f32[8,640]{1,0:T(8,128)S(1)} %get-tuple-element.60.piece0), channel_id=1, source_target_pairs={{0,8},{1,9},{2,10},{3,11},{4,12},{5,13},{6,14},{7,15},{8,16},{9,17... | collective-permute-start | bytes 61448 | tf_op jit(solution)/shard_map/ppermute | solution.py:42
  90.1 5.3 %collective-permute-start.21 = (f32[8,640]{1,0:T(8,128)S(1)}, f32[8,640]{1,0:T(8,128)S(1)}, u32[]{:S(2)}, u32[]{:S(2)}) collective-permute-start(f32[8,640]{1,0:T(8,128)S(1)} %get-tuple-element.60.piece0), channel_id=1, source_target_pairs={{0,16},{1,17},{2,18},{3,19},{4,20},{5,21},{6,22},{7,23},{8,24},{9,... | collective-permute-start | bytes 61448 | tf_op jit(solution)/shard_map/ppermute | solution.py:42
  90.6 4.8 %collective-permute-start.20 = (f32[8,640]{1,0:T(8,128)S(1)}, f32[8,640]{1,0:T(8,128)S(1)}, u32[]{:S(2)}, u32[]{:S(2)}) collective-permute-start(f32[8,640]{1,0:T(8,128)S(1)} %get-tuple-element.60.piece0), channel_id=1, source_target_pairs={{0,24},{1,25},{2,26},{3,27},{4,28},{5,29},{6,30},{7,31},{8,0},{9,1... | collective-permute-start | bytes 61448 | tf_op jit(solution)/shard_map/ppermute | solution.py:42
  101.6 13.7 %collective-permute-start.24 = (bf16[128,2048]{1,0:T(8,128)(2,1)S(1)}, bf16[128,2048]{1,0:T(8,128)(2,1)S(1)}, u32[]{:S(2)}, u32[]{:S(2)}) collective-permute-start(bf16[128,2048]{1,0:T(8,128)(2,1)S(1)} %get-tuple-element.123), channel_id=1, source_target_pairs={{0,32},{1,97},{2,34},{3,99},{4,36},{5,101},{6,38},{7,103},{8,40},{... | collective-permute-start | bytes 1572872 | tf_op jit(solution)/shard_map/ppermute | solution.py:60
  101.6 18.1 %collective-permute-start.23 = (bf16[128,2048]{1,0:T(8,128)(2,1)}, bf16[128,2048]{1,0:T(8,128)(2,1)}, u32[]{:S(2)}, u32[]{:S(2)}) collective-permute-start(bf16[128,2048]{1,0:T(8,128)(2,1)} %get-tuple-element.122), channel_id=1, source_target_pairs={{0,96},{1,33},{2,98},{3,35},{4,100},{5,37},{6,102},{7,39},{8,104},... | collective-permute-start | bytes 1572872 | tf_op jit(solution)/shard_map/ppermute | solution.py:60
  116.3 10.7 %collective-permute-start.25 = (bf16[128,2048]{1,0:T(8,128)(2,1)}, bf16[128,2048]{1,0:T(8,128)(2,1)}, u32[]{:S(2)}, u32[]{:S(2)}) collective-permute-start(bf16[128,2048]{1,0:T(8,128)(2,1)} %add_convert_fusion.7), channel_id=1, source_target_pairs={{0,32},{1,97},{2,34},{3,99},{4,36},{5,101},{6,38},{7,103},{8,40},{... | collective-permute-start | bytes 1572872 | tf_op jit(solution)/shard_map/ppermute | solution.py:60
  116.4 17.3 %collective-permute-start.29 = (bf16[128,2048]{1,0:T(8,128)(2,1)}, bf16[128,2048]{1,0:T(8,128)(2,1)}, u32[]{:S(2)}, u32[]{:S(2)}) collective-permute-start(bf16[128,2048]{1,0:T(8,128)(2,1)} %param.35), channel_id=1, source_target_pairs={{0,96},{1,33},{2,98},{3,35},{4,100},{5,37},{6,102},{7,39},{8,104},... | collective-permute-start | bytes 1572872 | tf_op jit(solution)/shard_map/ppermute | solution.py:60
  130.4 10.6 %collective-permute-start.27 = (bf16[128,2048]{1,0:T(8,128)(2,1)S(1)}, bf16[128,2048]{1,0:T(8,128)(2,1)}, u32[]{:S(2)}, u32[]{:S(2)}) collective-permute-start(bf16[128,2048]{1,0:T(8,128)(2,1)S(1)} %multiply_convert_fusion.3), channel_id=1, source_target_pairs={{0,32},{1,97},{2,34},{3,99},{4,36},{5,101},{6,38},{7,103},{8,40},{... | collective-permute-start | bytes 1572872 | tf_op jit(solution)/shard_map/ppermute | solution.py:60
  130.6 14.2 %collective-permute-start.26 = (bf16[128,2048]{1,0:T(8,128)(2,1)S(1)}, bf16[128,2048]{1,0:T(8,128)(2,1)S(1)}, u32[]{:S(2)}, u32[]{:S(2)}) collective-permute-start(bf16[128,2048]{1,0:T(8,128)(2,1)S(1)} %multiply_convert_fusion.3), channel_id=1, source_target_pairs={{0,96},{1,33},{2,98},{3,35},{4,100},{5,37},{6,102},{7,39},{8,104},... | collective-permute-start | bytes 1572872 | tf_op jit(solution)/shard_map/ppermute | solution.py:60
  141.0 12.2 %collective-permute-start.28 = (bf16[128,2048]{1,0:T(8,128)(2,1)}, bf16[128,2048]{1,0:T(8,128)(2,1)}, u32[]{:S(2)}, u32[]{:S(2)}) collective-permute-start(bf16[128,2048]{1,0:T(8,128)(2,1)} %collective-permute-done.27), channel_id=1, source_target_pairs={{0,32},{1,97},{2,34},{3,99},{4,36},{5,101},{6,38},{7,103},{8,40},{... | collective-permute-start | bytes 1572872 | tf_op jit(solution)/shard_map/ppermute | solution.py:60
  194.5 26.4 %copy-start.17 = (f32[128,2048]{1,0:T(8,128)S(1)}, f32[128,2048]{1,0:T(8,128)}, u32[]{:S(2)}) copy-start(f32[128,2048]{1,0:T(8,128)} %copy-done.16) | copy-start | bytes 3145732
  194.6 15.6 %collective-permute-start.30 = (bf16[128,2048]{1,0:T(8,128)(2,1)S(1)}, bf16[128,2048]{1,0:T(8,128)(2,1)S(1)}, u32[]{:S(2)}, u32[]{:S(2)}) collective-permute-start(bf16[128,2048]{1,0:T(8,128)(2,1)S(1)} %get-tuple-element.121), channel_id=1, source_target_pairs={{0,32},{1,97},{2,34},{3,99},{4,36},{5,101},{6,38},{7,103},{8,40},{... | collective-permute-start | bytes 1572872 | tf_op jit(solution)/shard_map/ppermute | solution.py:60
  194.9 15.7 %collective-permute-start.31 = (bf16[128,2048]{1,0:T(8,128)(2,1)S(1)}, bf16[128,2048]{1,0:T(8,128)(2,1)S(1)}, u32[]{:S(2)}, u32[]{:S(2)}) collective-permute-start(bf16[128,2048]{1,0:T(8,128)(2,1)S(1)} %get-tuple-element.120), channel_id=1, source_target_pairs={{0,96},{1,33},{2,98},{3,35},{4,100},{5,37},{6,102},{7,39},{8,104},... | collective-permute-start | bytes 1572872 | tf_op jit(solution)/shard_map/ppermute | solution.py:60
  210.5 10.5 %collective-permute-start.32 = (bf16[128,2048]{1,0:T(8,128)(2,1)S(1)}, bf16[128,2048]{1,0:T(8,128)(2,1)S(1)}, u32[]{:S(2)}, u32[]{:S(2)}) collective-permute-start(bf16[128,2048]{1,0:T(8,128)(2,1)S(1)} %add_convert_fusion.6), channel_id=1, source_target_pairs={{0,32},{1,97},{2,34},{3,99},{4,36},{5,101},{6,38},{7,103},{8,40},{... | collective-permute-start | bytes 1572872 | tf_op jit(solution)/shard_map/ppermute | solution.py:60
  224.2 10.4 %collective-permute-start.34 = (bf16[128,2048]{1,0:T(8,128)(2,1)S(1)}, bf16[128,2048]{1,0:T(8,128)(2,1)S(1)}, u32[]{:S(2)}, u32[]{:S(2)}) collective-permute-start(bf16[128,2048]{1,0:T(8,128)(2,1)S(1)} %get-tuple-element.105), channel_id=1, source_target_pairs={{0,32},{1,97},{2,34},{3,99},{4,36},{5,101},{6,38},{7,103},{8,40},{... | collective-permute-start | bytes 1572872 | tf_op jit(solution)/shard_map/ppermute | solution.py:60
  224.2 18.0 %collective-permute-start.33 = (bf16[128,2048]{1,0:T(8,128)(2,1)S(1)}, bf16[128,2048]{1,0:T(8,128)(2,1)S(1)}, u32[]{:S(2)}, u32[]{:S(2)}) collective-permute-start(bf16[128,2048]{1,0:T(8,128)(2,1)S(1)} %get-tuple-element.105), channel_id=1, source_target_pairs={{0,96},{1,33},{2,98},{3,35},{4,100},{5,37},{6,102},{7,39},{8,104},... | collective-permute-start | bytes 1572872 | tf_op jit(solution)/shard_map/ppermute | solution.py:60
  234.6 10.4 %collective-permute-start.35 = (bf16[128,2048]{1,0:T(8,128)(2,1)S(1)}, bf16[128,2048]{1,0:T(8,128)(2,1)S(1)}, u32[]{:S(2)}, u32[]{:S(2)}) collective-permute-start(bf16[128,2048]{1,0:T(8,128)(2,1)S(1)} %collective-permute-done.34), channel_id=1, source_target_pairs={{0,32},{1,97},{2,34},{3,99},{4,36},{5,101},{6,38},{7,103},{8,40},{... | collective-permute-start | bytes 1572872 | tf_op jit(solution)/shard_map/ppermute | solution.py:60
  254.4 1.2 collective-permute-start.36
  255.5 5.4 %collective-permute-start.39 = (f32[2,8,640]{2,1,0:T(8,128)S(1)}, f32[2,8,640]{2,1,0:T(8,128)S(1)}, u32[]{:S(2)}, u32[]{:S(2)}) collective-permute-start(f32[2,8,640]{2,1,0:T(8,128)S(1)} %pad_maximum_fusion.11.refs_0_), channel_id=1, source_target_pairs={{0,2},{1,3},{2,4},{3,5},{4,6},{5,7},{6,0},{7,1},{8,10},{9,11},{10,... | collective-permute-start | bytes 122888 | tf_op jit(solution)/shard_map/ppermute | solution.py:42
  256.5 6.6 %collective-permute-start.38 = (f32[2,8,640]{2,1,0:T(8,128)S(1)}, f32[2,8,640]{2,1,0:T(8,128)S(1)}, u32[]{:S(2)}, u32[]{:S(2)}) collective-permute-start(f32[2,8,640]{2,1,0:T(8,128)S(1)} %pad_maximum_fusion.11.refs_0_), channel_id=1, source_target_pairs={{0,4},{1,5},{2,6},{3,7},{4,0},{5,1},{6,2},{7,3},{8,12},{9,13},{10,... | collective-permute-start | bytes 122888 | tf_op jit(solution)/shard_map/ppermute | solution.py:42
  258.4 6.1 %collective-permute-start.37 = (f32[2,8,640]{2,1,0:T(8,128)S(1)}, f32[2,8,640]{2,1,0:T(8,128)S(1)}, u32[]{:S(2)}, u32[]{:S(2)}) collective-permute-start(f32[2,8,640]{2,1,0:T(8,128)S(1)} %pad_maximum_fusion.11.refs_0_), channel_id=1, source_target_pairs={{0,6},{1,7},{2,0},{3,1},{4,2},{5,3},{6,4},{7,5},{8,14},{9,15},{10,... | collective-permute-start | bytes 122888 | tf_op jit(solution)/shard_map/ppermute | solution.py:42
  265.0 4.4 %collective-permute-start.42 = (f32[8,640]{1,0:T(8,128)S(1)}, f32[8,640]{1,0:T(8,128)S(1)}, u32[]{:S(2)}, u32[]{:S(2)}) collective-permute-start(f32[8,640]{1,0:T(8,128)S(1)} %get-tuple-element.75.piece0), channel_id=1, source_target_pairs={{0,8},{1,9},{2,10},{3,11},{4,12},{5,13},{6,14},{7,15},{8,16},{9,17... | collective-permute-start | bytes 61448 | tf_op jit(solution)/shard_map/ppermute | solution.py:42
  266.2 5.9 %collective-permute-start.41 = (f32[8,640]{1,0:T(8,128)S(1)}, f32[8,640]{1,0:T(8,128)S(1)}, u32[]{:S(2)}, u32[]{:S(2)}) collective-permute-start(f32[8,640]{1,0:T(8,128)S(1)} %get-tuple-element.75.piece0), channel_id=1, source_target_pairs={{0,16},{1,17},{2,18},{3,19},{4,20},{5,21},{6,22},{7,23},{8,24},{9,... | collective-permute-start | bytes 61448 | tf_op jit(solution)/shard_map/ppermute | solution.py:42
  267.2 5.0 %collective-permute-start.40 = (f32[8,640]{1,0:T(8,128)S(1)}, f32[8,640]{1,0:T(8,128)S(1)}, u32[]{:S(2)}, u32[]{:S(2)}) collective-permute-start(f32[8,640]{1,0:T(8,128)S(1)} %get-tuple-element.75.piece0), channel_id=1, source_target_pairs={{0,24},{1,25},{2,26},{3,27},{4,28},{5,29},{6,30},{7,31},{8,0},{9,1... | collective-permute-start | bytes 61448 | tf_op jit(solution)/shard_map/ppermute | solution.py:42
  284.9 3.1 collective-permute-start.43
  291.4 7.5 %collective-permute-start.44 = (bf16[8,208,640]{2,1,0:T(8,128)(2,1)S(1)}, bf16[8,208,640]{2,1,0:T(8,128)(2,1)S(1)}, u32[]{:S(2)}, u32[]{:S(2)}) collective-permute-start(bf16[8,208,640]{2,1,0:T(8,128)(2,1)S(1)} %get-tuple-element.89), channel_id=1, source_target_pairs={{0,1},{1,0},{2,3},{3,2},{4,5},{5,4},{6,7},{7,6},{8,9},{9,8},{10,11... | collective-permute-start | bytes 6389768 | tf_op jit(solution)/shard_map/ppermute | solution.py:42
  295.6 4.3 %collective-permute-start.45 = (bf16[8,208,640]{2,1,0:T(8,128)(2,1)S(1)}, bf16[8,208,640]{2,1,0:T(8,128)(2,1)S(1)}, u32[]{:S(2)}, u32[]{:S(2)}) collective-permute-start(bf16[8,208,640]{2,1,0:T(8,128)(2,1)S(1)} %get-tuple-element.86), channel_id=1, source_target_pairs={{0,1},{1,0},{2,3},{3,2},{4,5},{5,4},{6,7},{7,6},{8,9},{9,8},{10,11... | collective-permute-start | bytes 6389768 | tf_op jit(solution)/shard_map/ppermute | solution.py:42
  303.9 13.1 %collective-permute-start.47 = (bf16[128,2048]{1,0:T(8,128)(2,1)}, bf16[128,2048]{1,0:T(8,128)(2,1)S(1)}, u32[]{:S(2)}, u32[]{:S(2)}) collective-permute-start(bf16[128,2048]{1,0:T(8,128)(2,1)} %get-tuple-element.119), channel_id=1, source_target_pairs={{0,32},{1,97},{2,34},{3,99},{4,36},{5,101},{6,38},{7,103},{8,40},{... | collective-permute-start | bytes 1572872 | tf_op jit(solution)/shard_map/ppermute | solution.py:60
  303.9 74.5 %all-to-all-start = ((bf16[16,208,640]{2,1,0:T(8,128)(2,1)}), bf16[16,208,640]{2,1,0:T(8,128)(2,1)}, u32[]{:S(2)}, u32[]{:S(2)}) async-start(bf16[16,208,640]{2,1,0:T(8,128)(2,1)} %pad_maximum_fusion), calls=%async_computation | async-start | bytes 8519680 | tf_op jit(solution)/shard_map/all_to_all | solution.py:137
  313.7 15.2 %collective-permute-start.46 = (bf16[128,2048]{1,0:T(8,128)(2,1)S(1)}, bf16[128,2048]{1,0:T(8,128)(2,1)S(1)}, u32[]{:S(2)}, u32[]{:S(2)}) collective-permute-start(bf16[128,2048]{1,0:T(8,128)(2,1)S(1)} %get-tuple-element.118), channel_id=1, source_target_pairs={{0,96},{1,33},{2,98},{3,35},{4,100},{5,37},{6,102},{7,39},{8,104},... | collective-permute-start | bytes 1572872 | tf_op jit(solution)/shard_map/ppermute | solution.py:60
  317.2 12.0 %collective-permute-start.48 = (bf16[128,2048]{1,0:T(8,128)(2,1)S(1)}, bf16[128,2048]{1,0:T(8,128)(2,1)S(1)}, u32[]{:S(2)}, u32[]{:S(2)}) collective-permute-start(bf16[128,2048]{1,0:T(8,128)(2,1)S(1)} %add_convert_fusion.5), channel_id=1, source_target_pairs={{0,32},{1,97},{2,34},{3,99},{4,36},{5,101},{6,38},{7,103},{8,40},{... | collective-permute-start | bytes 1572872 | tf_op jit(solution)/shard_map/ppermute | solution.py:60
  329.8 14.4 %collective-permute-start.50 = (bf16[128,2048]{1,0:T(8,128)(2,1)S(1)}, bf16[128,2048]{1,0:T(8,128)(2,1)S(1)}, u32[]{:S(2)}, u32[]{:S(2)}) collective-permute-start(bf16[128,2048]{1,0:T(8,128)(2,1)S(1)} %get-tuple-element.117), channel_id=1, source_target_pairs={{0,32},{1,97},{2,34},{3,99},{4,36},{5,101},{6,38},{7,103},{8,40},{... | collective-permute-start | bytes 1572872 | tf_op jit(solution)/shard_map/ppermute | solution.py:60
  330.1 15.8 %collective-permute-start.49 = (bf16[128,2048]{1,0:T(8,128)(2,1)S(1)}, bf16[128,2048]{1,0:T(8,128)(2,1)S(1)}, u32[]{:S(2)}, u32[]{:S(2)}) collective-permute-start(bf16[128,2048]{1,0:T(8,128)(2,1)S(1)} %get-tuple-element.116), channel_id=1, source_target_pairs={{0,96},{1,33},{2,98},{3,35},{4,100},{5,37},{6,102},{7,39},{8,104},... | collective-permute-start | bytes 1572872 | tf_op jit(solution)/shard_map/ppermute | solution.py:60
  344.5 10.5 %collective-permute-start.51 = (bf16[128,2048]{1,0:T(8,128)(2,1)S(1)}, bf16[128,2048]{1,0:T(8,128)(2,1)S(1)}, u32[]{:S(2)}, u32[]{:S(2)}) collective-permute-start(bf16[128,2048]{1,0:T(8,128)(2,1)S(1)} %add_convert_fusion.4), channel_id=1, source_target_pairs={{0,32},{1,97},{2,34},{3,99},{4,36},{5,101},{6,38},{7,103},{8,40},{... | collective-permute-start | bytes 1572872 | tf_op jit(solution)/shard_map/ppermute | solution.py:60
  356.1 25.2 %copy-start.39 = (bf16[64,640]{1,0:T(8,128)(2,1)S(1)}, bf16[64,640]{1,0:T(8,128)(2,1)}, u32[]{:S(2)}) copy-start(bf16[64,640]{1,0:T(8,128)(2,1)} %param.20) | copy-start | bytes 245764
  356.1 25.2 %copy-start.40 = (bf16[64,640]{1,0:T(8,128)(2,1)S(1)}, bf16[64,640]{1,0:T(8,128)(2,1)}, u32[]{:S(2)}) copy-start(bf16[64,640]{1,0:T(8,128)(2,1)} %param.21) | copy-start | bytes 245764
  356.1 26.1 %copy-start.41 = (bf16[64]{0:T(256)(128)(2,1)S(1)}, bf16[64]{0:T(256)(128)(2,1)}, u32[]{:S(2)}) copy-start(bf16[64]{0:T(256)(128)(2,1)} %param.19) | copy-start | bytes 388
  356.1 28.9 %copy-start.42 = (bf16[20]{0:T(256)(128)(2,1)S(1)}, bf16[20]{0:T(256)(128)(2,1)}, u32[]{:S(2)}) copy-start(bf16[20]{0:T(256)(128)(2,1)} %param.28) | copy-start | bytes 124
  382.4 5.2 %collective-permute-start.54 = (f32[1,128]{1,0:T(1,128)S(1)}, f32[1,128]{1,0:T(1,128)S(1)}, u32[]{:S(2)}, u32[]{:S(2)}) collective-permute-start(f32[1,128]{1,0:T(1,128)S(1)} %maximum_bitcast_fusion), channel_id=1, source_target_pairs={{0,64},{32,96},{64,0},{96,32},{1,65},{33,97},{65,1},{97,33},{2,66}... | collective-permute-start | bytes 1544 | tf_op jit(solution)/shard_map/ppermute | solution.py:25
  382.4 5.1 %collective-permute-start.53 = (f32[1,128]{1,0:T(1,128)S(1)}, f32[1,128]{1,0:T(1,128)S(1)}, u32[]{:S(2)}, u32[]{:S(2)}) collective-permute-start(f32[1,128]{1,0:T(1,128)S(1)} %maximum_bitcast_fusion), channel_id=1, source_target_pairs={{0,96},{32,0},{64,32},{96,64},{1,97},{33,1},{65,33},{97,65},{2,98}... | collective-permute-start | bytes 1544 | tf_op jit(solution)/shard_map/ppermute | solution.py:25
  383.9 4.8 %collective-permute-start.52 = (f32[1,128]{1,0:T(1,128)S(1)}, f32[1,128]{1,0:T(1,128)S(1)}, u32[]{:S(2)}, u32[]{:S(2)}) collective-permute-start(f32[1,128]{1,0:T(1,128)S(1)} %maximum_bitcast_fusion), channel_id=1, source_target_pairs={{0,32},{32,64},{64,96},{96,0},{1,33},{33,65},{65,97},{97,1},{2,34}... | collective-permute-start | bytes 1544 | tf_op jit(solution)/shard_map/ppermute | solution.py:25
  (42 other events, 326.8 us)
Sparse Core Ops, SparseCore 0:
  10.9 55.2 all-gather.2
  68.4 75.9 all-gather.4
  183.9 123.2 reduce-scatter.1
